TPU v7x, 32 devices: a whole 2x2x4 slice. The times are simulated.
32 devices in a mesh: dp: 16 (over z, y, x), shard: 2 (over core).
Axes of the slice: x: 2, y: 2, z: 4, core: 2. Of those that a mesh axis runs over, the one named last changes fastest.
Arguments:
- canvases: bfloat16 [2, 128, 6, 6, 2048], P(None, ('dp', 'shard')), may hold values from -6 to 6
- crop_map: int32 [2, 128, 36], P(None, ('dp', 'shard')), may hold values from 0 to 3, as said below
- partner: int32 [2, 128, 4], P(None, ('dp', 'shard')), may hold values from 0 to 3, as said below
- queue: bfloat16 [512, 128], P(('dp', 'shard')), may hold values from -0.5 to 0.5
- w_reduce: bfloat16 [2048, 512], P(('dp', 'shard')), may hold values from -0.125 to 0.125
- w_spatial: bfloat16 [4608, 512], P(('dp', 'shard')), may hold values from -0.09375 to 0.09375
- w_expand: bfloat16 [512, 2048], P(('dp', 'shard')), may hold values from -0.25 to 0.25
- w_hidden: bfloat16 [2048, 2048], P(('dp', 'shard')), may hold values from -0.125 to 0.125
- w_project: bfloat16 [2048, 128], P(('dp', 'shard')), may hold values from -0.125 to 0.125
- norm_mid: float32 [4, 512], replicated, may hold values from -0.8 to 1.5, as said below
- norm_wide: float32 [4, 2048], replicated, may hold values from -0.8 to 1.5, as said below
- bias_out: float32 [128], replicated, may hold values from -1.5 to 1.5
- prototypes: bfloat16 [3000, 128], replicated, may hold values from -0.75 to 0.75
Outputs:
- loss: float32 [], replicated
- grad_canvases: float32 [2, 128, 6, 6, 2048], P(None, ('dp', 'shard'))
- grad_reduce: float32 [2048, 512], P(('dp', 'shard'))
- grad_spatial: float32 [4608, 512], P(('dp', 'shard'))
- grad_expand: float32 [512, 2048], P(('dp', 'shard'))
- grad_hidden: float32 [2048, 2048], P(('dp', 'shard'))
- grad_project: float32 [2048, 128], P(('dp', 'shard'))
- grad_norm_mid: float32 [4, 512], replicated
- grad_norm_wide: float32 [4, 2048], replicated
- grad_bias_out: float32 [128], replicated
- grad_prototypes: float32 [3000, 128], replicated
Inputs may be any that keep to these rules, and one draw needn't show every extreme that they name: `crop_map`: every one of a canvas's 4 crops covers at least one of its pixels. A crop's partner is another crop of the same canvas, never itself. `norm_mid`: rows 0 and 2 are gains, rows 1 and 3 shifts. `norm_wide`: rows 0 and 2 are gains, rows 1 and 3 shifts.
All inputs are finite; a program needn't handle non-finite values.
Results may differ from a plain program's by a relative error of at most 0.024.
Values may be sent and summed in bfloat16 or wider, within the bound.
No kernel may reach another device: no remote copies, remote signals or barrier semaphores. Data moves between devices by JAX's collectives and lax.ppermute only.
A program may use at most 128 MiB of HBM per device.

v0:
```python
import jax
import jax.numpy as jnp
from jax import lax
from jax.sharding import PartitionSpec as P

D = 2048
MID = 512
PROTOS = 3000
SIDE = 6
CROPS = 4
SINK_ITERS = 3
MICRO = 2


EPS_NORM = 1e-05
EPS_UNIT = 1e-06
SOFTMAX_HEAT = 0.1
SINK_EPS = 0.05
HIGH = lax.Precision.HIGHEST


def product(left, right):
    return jnp.dot(left, right, preferred_element_type=jnp.float32)


def product_t(left, right):
    return lax.dot_general(
        left, right, (((0,), (0,)), ((), ())), preferred_element_type=jnp.float32
    )


def product_bt(left, right):
    return lax.dot_general(
        left, right, (((1,), (1,)), ((), ())), preferred_element_type=jnp.float32
    )


def silu_slope(values):
    sigmoid_value = jax.nn.sigmoid(values)
    return sigmoid_value * (1.0 + values * (1.0 - sigmoid_value))


def norm_forward(hidden, gain_row, shift_row, row_total):
    totals = lax.psum((jnp.sum(hidden, 0), jnp.sum(hidden * hidden, 0)), ("dp", "shard"))
    average = totals[0] / row_total
    inverse = lax.rsqrt(totals[1] / row_total - average * average + EPS_NORM)
    normed = (hidden - average) * inverse
    return (gain_row * normed + shift_row, normed, inverse)


def norm_backward(grad_out, normed, inverse, gain_row, row_total):
    totals = lax.psum((jnp.sum(grad_out, 0), jnp.sum(grad_out * normed, 0)), ("dp", "shard"))
    grad_in = (
        gain_row * inverse * (grad_out - totals[0] / row_total - normed * (totals[1] / row_total))
    )
    return (grad_in, totals[1], totals[0])


def make_patches(values):
    canvas_count, side_len = (values.shape[0], values.shape[1])
    padded = jnp.pad(values, ((0, 0), (1, 1), (1, 1), (0, 0)))
    pieces = [
        padded[:, row_shift : row_shift + side_len, col_shift : col_shift + side_len, :]
        for row_shift in range(3)
        for col_shift in range(3)
    ]
    return jnp.concatenate(pieces, 3).reshape(canvas_count * side_len * side_len, -1)


def fold_patches(grads, canvas_count, side_len, channels):
    grads = grads.reshape(canvas_count, side_len, side_len, 9, channels)
    summed = jnp.zeros((canvas_count, side_len + 2, side_len + 2, channels), jnp.float32)
    for row_shift in range(3):
        for col_shift in range(3):
            summed = summed + jnp.pad(
                grads[:, :, :, row_shift * 3 + col_shift, :],
                ((0, 0), (row_shift, 2 - row_shift), (col_shift, 2 - col_shift), (0, 0)),
            )
    return summed[:, 1 : side_len + 1, 1 : side_len + 1, :].reshape(
        canvas_count * side_len * side_len, channels
    )


def per_device(
    canvases,
    crop_map,
    partner,
    queue,
    w_reduce,
    w_spatial,
    w_expand,
    w_hidden,
    w_project,
    norm_mid,
    norm_wide,
    bias_out,
    prototypes,
):
    devices_all = lax.axis_size("dp") * lax.axis_size("shard")
    canvas_count = canvases.shape[1]
    pixels = SIDE * SIDE
    local_rows = canvas_count * pixels
    pixel_total = float(local_rows * devices_all)
    crop_total = float(canvas_count * CROPS * devices_all)
    loss_factor_weight = 1.0 / (MICRO * crop_total)
    crop_ids = jnp.arange(CROPS, dtype=jnp.int32)
    shards = (w_reduce, w_spatial, w_expand, w_hidden, w_project)
    queue_codes = jnp.exp(product_bt(queue, prototypes) / SINK_EPS)
    full_sums = tuple(
        (
            jnp.zeros((weight_portion.shape[0] * devices_all, weight_portion.shape[1]), jnp.float32)
            for weight_portion in shards
        )
    )
    mid_grads = jnp.zeros(norm_mid.shape, jnp.float32)
    wide_grads = jnp.zeros(norm_wide.shape, jnp.float32)
    proto_grad = jnp.zeros(prototypes.shape, jnp.float32)
    bias_grad = jnp.zeros(bias_out.shape, jnp.float32)
    loss_local = jnp.zeros((), jnp.float32)
    input_grads = []
    for micro_index in range(MICRO):
        gathered = (
            lax.all_gather(shards[0], ("dp", "shard"), axis=0, tiled=True),
            lax.all_gather(shards[1], ("dp", "shard"), axis=0, tiled=True),
            lax.all_gather(shards[2], ("dp", "shard"), axis=0, tiled=True),
            lax.all_gather(shards[3], ("dp", "shard"), axis=0, tiled=True),
            lax.all_gather(shards[4], ("dp", "shard"), axis=0, tiled=True),
        )
        full_reduce, full_spatial, full_expand, full_hidden, full_project = gathered
        input_rows = canvases[micro_index].reshape(local_rows, D)
        pre_one = product(input_rows, full_reduce)
        norm_one, unit_one, inv_one = norm_forward(pre_one, norm_mid[0], norm_mid[1], pixel_total)
        first_activation = jax.nn.silu(norm_one).astype(jnp.bfloat16)
        image_patches = make_patches(first_activation.reshape(canvas_count, SIDE, SIDE, MID))
        pre_two = product(image_patches, full_spatial)
        norm_two, unit_two, inv_two = norm_forward(pre_two, norm_mid[2], norm_mid[3], pixel_total)
        act_two = jax.nn.silu(norm_two).astype(jnp.bfloat16)
        pre_three = product(act_two, full_expand)
        norm_three, unit_three, inv_three = norm_forward(
            pre_three, norm_wide[0], norm_wide[1], pixel_total
        )
        joined = norm_three + input_rows.astype(jnp.float32)
        block_out = jax.nn.silu(joined)
        onehot = (crop_map[micro_index][:, None, :] == crop_ids[None, :, None]).astype(jnp.float32)
        crop_sizes = jnp.sum(onehot, 2)
        pooled = (
            jnp.einsum(
                "cps,csd->cpd", onehot, block_out.reshape(canvas_count, pixels, D), precision=HIGH
            )
            / crop_sizes[:, :, None]
        )
        pooled_low = pooled.reshape(canvas_count * CROPS, D).astype(jnp.bfloat16)
        pre_head = product(pooled_low, full_hidden)
        norm_head, unit_head, inv_head = norm_forward(
            pre_head, norm_wide[2], norm_wide[3], crop_total
        )
        act_head = jax.nn.silu(norm_head).astype(jnp.bfloat16)
        embed = product(act_head, full_project) + bias_out
        inv_length = lax.rsqrt(jnp.sum(embed * embed, 1, keepdims=True) + EPS_UNIT)
        unit_embed = embed * inv_length
        unit_low = unit_embed.astype(jnp.bfloat16)
        prototype_scores = product_bt(unit_low, prototypes)
        batch_codes = jnp.exp(prototype_scores / SINK_EPS)
        stored_codes = queue_codes
        for turn in range(SINK_ITERS):
            row_totals = lax.psum(
                jnp.sum(batch_codes, 0) + jnp.sum(stored_codes, 0), ("dp", "shard")
            )
            batch_codes = batch_codes / row_totals
            stored_codes = stored_codes / row_totals
            batch_codes = batch_codes / jnp.sum(batch_codes, 1, keepdims=True)
            stored_codes = stored_codes / jnp.sum(stored_codes, 1, keepdims=True)
        pick = (partner[micro_index][:, :, None] == crop_ids[None, None, :]).astype(jnp.float32)
        target = jnp.einsum(
            "cab,cbk->cak", pick, batch_codes.reshape(canvas_count, CROPS, PROTOS), precision=HIGH
        ).reshape(canvas_count * CROPS, PROTOS)
        log_likelihoods = jax.nn.log_softmax(prototype_scores / SOFTMAX_HEAT, axis=1)
        loss_local = loss_local - jnp.sum(target * log_likelihoods)
        score_grad = (jnp.exp(log_likelihoods) * jnp.sum(target, 1, keepdims=True) - target) * (
            loss_factor_weight / SOFTMAX_HEAT
        )
        score_low = score_grad.astype(jnp.bfloat16)
        proto_grad = proto_grad + product_t(score_low, unit_low)
        unit_grad = product(score_low, prototypes)
        embed_grad = inv_length * (
            unit_grad - unit_embed * jnp.sum(unit_grad * unit_embed, 1, keepdims=True)
        )
        bias_grad = bias_grad + jnp.sum(embed_grad, 0)
        embed_low = embed_grad.astype(jnp.bfloat16)
        back_weights = (
            lax.all_gather(shards[0], ("dp", "shard"), axis=0, tiled=True),
            lax.all_gather(shards[1], ("dp", "shard"), axis=0, tiled=True),
            lax.all_gather(shards[2], ("dp", "shard"), axis=0, tiled=True),
            lax.all_gather(shards[3], ("dp", "shard"), axis=0, tiled=True),
            lax.all_gather(shards[4], ("dp", "shard"), axis=0, tiled=True),
        )
        back_reduce, back_spatial, back_expand, back_hidden, back_project = back_weights
        grad_project = product_t(act_head, embed_low)
        head_act_grad = product_bt(embed_low, back_project) * silu_slope(norm_head)
        head_grad, gain_head, shift_head = norm_backward(
            head_act_grad, unit_head, inv_head, norm_wide[2], crop_total
        )
        head_low = head_grad.astype(jnp.bfloat16)
        grad_hidden = product_t(pooled_low, head_low)
        pooled_grad = (
            product_bt(head_low, back_hidden).reshape(canvas_count, CROPS, D)
            / crop_sizes[:, :, None]
        )
        out_grad = jnp.einsum("cps,cpd->csd", onehot, pooled_grad, precision=HIGH).reshape(
            local_rows, D
        )
        joined_grad = out_grad * silu_slope(joined)
        three_grad, gain_three, shift_three = norm_backward(
            joined_grad, unit_three, inv_three, norm_wide[0], pixel_total
        )
        three_low = three_grad.astype(jnp.bfloat16)
        grad_expand = product_t(act_two, three_low)
        two_act_grad = product_bt(three_low, back_expand) * silu_slope(norm_two)
        two_grad, gain_two, shift_two = norm_backward(
            two_act_grad, unit_two, inv_two, norm_mid[2], pixel_total
        )
        two_low = two_grad.astype(jnp.bfloat16)
        grad_spatial = product_t(image_patches, two_low)
        patch_grad = product_bt(two_low, back_spatial)
        one_act_grad = fold_patches(patch_grad, canvas_count, SIDE, MID) * silu_slope(norm_one)
        one_grad, gain_one, shift_one = norm_backward(
            one_act_grad, unit_one, inv_one, norm_mid[0], pixel_total
        )
        one_low = one_grad.astype(jnp.bfloat16)
        grad_reduce = product_t(input_rows, one_low)
        input_grad = joined_grad + product_bt(one_low, back_reduce)
        input_grads.append(input_grad.reshape(canvas_count, SIDE, SIDE, D))
        mid_grads = mid_grads + jnp.stack([gain_one, shift_one, gain_two, shift_two])
        wide_grads = wide_grads + jnp.stack([gain_three, shift_three, gain_head, shift_head])
        micro_grads = (grad_reduce, grad_spatial, grad_expand, grad_hidden, grad_project)
        full_sums = tuple((former + latest for former, latest in zip(full_sums, micro_grads)))
    weight_grads = lax.psum_scatter(full_sums, ("dp", "shard"), scatter_dimension=0, tiled=True)
    head_sums = lax.psum((loss_local, proto_grad, bias_grad), ("dp", "shard"))
    return (
        head_sums[0] * loss_factor_weight,
        jnp.stack(input_grads),
        weight_grads[0],
        weight_grads[1],
        weight_grads[2],
        weight_grads[3],
        weight_grads[4],
        mid_grads,
        wide_grads,
        head_sums[2],
        head_sums[1],
    )


def solution(mesh):
    return jax.shard_map(
        per_device,
        mesh=mesh,
        in_specs=(
            P(None, ("dp", "shard"), None, None, None),
            P(None, ("dp", "shard"), None),
            P(None, ("dp", "shard"), None),
            P(("dp", "shard"), None),
            P(("dp", "shard"), None),
            P(("dp", "shard"), None),
            P(("dp", "shard"), None),
            P(("dp", "shard"), None),
            P(("dp", "shard"), None),
            P(),
            P(),
            P(),
            P(),
        ),
        out_specs=(
            P(),
            P(None, ("dp", "shard"), None, None, None),
            P(("dp", "shard"), None),
            P(("dp", "shard"), None),
            P(("dp", "shard"), None),
            P(("dp", "shard"), None),
            P(("dp", "shard"), None),
            P(),
            P(),
            P(),
            P(),
        ),
        check_vma=False,
    )
```

profile of v0, /device:TPU:1, one launch (start us, length us, event | category | flops | bytes accessed | tf_op | source)
XLA Modules:
  0.0 1600.7 jit_solution(2316197858974951655)
XLA Ops:
  16.3 47.6 %all_gather.14 = bf16[2048,128]{1,0:T(8,128)(2,1)} all-gather(bf16[64,128]{1,0:T(8,128)(2,1)S(1)} %copy-done.155), channel_id=1, replica_groups=mesh['dp'=16,'shard'=2] {'dp','shard'}, dimensions={0}, use_global_device_ids=true | all-gather | bytes 540672 | tf_op jit(solution)/shard_map/all_gather | solution.py:127
  64.0 6.2 all-gather.5.cloned.1.call-done
  74.3 38.0 %all-reduce.30 = (f32[512]{0:T(512)}, f32[512]{0:T(512)}, f32[512]{0:T(512)}, f32[512]{0:T(512)}) all-reduce(f32[512]{0:T(512)S(1)} %get-tuple-element.163, f32[512]{0:T(512)S(1)} %get-tuple-element.162, f32[512]{0:T(512)S(1)} %get-tuple-element.167, f32[512]{0:T(512)S(1)} %get-tuple-element.166), channel_id=1, replica_groups=mesh['dp'=16,'shard'=2] {'dp','shard'}, use_global_device_ids=true, to_apply=%region_38.40 | all-reduce | flops 2048 | bytes 16384 | tf_op jit(solution)/shard_map/psum | solution.py:44
  175.7 41.5 %all-reduce.29 = (f32[512]{0:T(512)S(1)}, f32[512]{0:T(512)S(1)}, f32[512]{0:T(512)S(1)}, f32[512]{0:T(512)S(1)}) all-reduce(f32[512]{0:T(512)S(1)} %get-tuple-element.161, f32[512]{0:T(512)S(1)} %get-tuple-element.160, f32[512]{0:T(512)S(1)} %get-tuple-element.165, ...), channel_id=1, replica_groups=mesh['dp'=16,'shard'=2] {'dp','shard'}, use_global_device_ids=true, to_apply=%region_42.44 | all-reduce | flops 2048 | bytes 16384 | tf_op jit(solution)/shard_map/psum | solution.py:44
  223.6 41.6 %all-reduce.28 = (f32[2048]{0:T(1024)S(1)}, f32[2048]{0:T(1024)}, f32[2048]{0:T(1024)}, f32[2048]{0:T(1024)}) all-reduce(f32[2048]{0:T(1024)S(1)} %get-tuple-element.149, f32[2048]{0:T(1024)S(1)} %get-tuple-element.148, f32[2048]{0:T(1024)} %get-tuple-element.151, ...), channel_id=1, replica_groups=mesh['dp'=16,'shard'=2] {'dp','shard'}, use_global_device_ids=true, to_apply=%region_46.48 | all-reduce | flops 8192 | bytes 65536 | tf_op jit(solution)/shard_map/psum | solution.py:44
  289.9 41.4 %all-reduce.27 = (f32[2048]{0:T(1024)}, f32[2048]{0:T(1024)}, f32[2048]{0:T(1024)}, f32[2048]{0:T(1024)}) all-reduce(f32[2048]{0:T(1024)S(1)} %get-tuple-element.189, f32[2048]{0:T(1024)S(1)} %get-tuple-element.188, f32[2048]{0:T(1024)} %get-tuple-element.191, ...), channel_id=1, replica_groups=mesh['dp'=16,'shard'=2] {'dp','shard'}, use_global_device_ids=true, to_apply=%region_51.53 | all-reduce | flops 8192 | bytes 65536 | tf_op jit(solution)/shard_map/psum | solution.py:44
  339.6 39.6 %all-reduce.26 = (f32[3000]{0:T(1024)S(1)}, f32[3000]{0:T(1024)S(1)}) all-reduce(f32[3000]{0:T(1024)} %get-tuple-element.304, f32[3000]{0:T(1024)} %get-tuple-element.303), channel_id=1, replica_groups=mesh['dp'=16,'shard'=2] {'dp','shard'}, use_global_device_ids=true, to_apply=%region_54.56 | all-reduce | flops 6000 | bytes 48000 | tf_op jit(solution)/shard_map/psum | solution.py:166
  386.3 42.2 %all-reduce.25 = (f32[3000]{0:T(1024)}, f32[3000]{0:T(1024)}) all-reduce(f32[3000]{0:T(1024)} %add.460, f32[3000]{0:T(1024)} %add.442), channel_id=1, replica_groups=mesh['dp'=16,'shard'=2] {'dp','shard'}, use_global_device_ids=true, to_apply=%region_59.61 | all-reduce | flops 6000 | bytes 48000 | tf_op jit(solution)/shard_map/psum | solution.py:166
  433.8 40.6 %all-reduce.24 = (f32[3000]{0:T(1024)}, f32[3000]{0:T(1024)}) all-reduce(f32[3000]{0:T(1024)} %add.443, f32[3000]{0:T(1024)} %add.461), channel_id=1, replica_groups=mesh['dp'=16,'shard'=2] {'dp','shard'}, use_global_device_ids=true, to_apply=%region_30.31 | all-reduce | flops 6000 | bytes 48000 | tf_op jit(solution)/shard_map/psum | solution.py:166
  504.2 41.5 %all-reduce.23 = (f32[2048]{0:T(1024)S(1)}, f32[2048]{0:T(1024)S(1)}, f32[2048]{0:T(1024)S(1)}, f32[2048]{0:T(1024)S(1)}) all-reduce(f32[2048]{0:T(1024)S(1)} %get-tuple-element.187, f32[2048]{0:T(1024)S(1)} %get-tuple-element.186, f32[2048]{0:T(1024)S(1)} %get-tuple-element.185, ...), channel_id=1, replica_groups=mesh['dp'=16,'shard'=2] {'dp','shard'}, use_global_device_ids=true, to_apply=%region_91.93 | all-reduce | flops 8192 | bytes 65536 | tf_op jit(solution)/shard_map/psum | solution.py:52
  546.4 5.7 fusion.101
  572.2 39.4 %all-reduce.22 = (f32[2048]{0:T(1024)S(1)}, f32[2048]{0:T(1024)S(1)}, f32[2048]{0:T(1024)S(1)}, f32[2048]{0:T(1024)S(1)}) all-reduce(f32[2048]{0:T(1024)S(1)} %get-tuple-element.294, f32[2048]{0:T(1024)S(1)} %get-tuple-element.295, f32[2048]{0:T(1024)S(1)} %get-tuple-element.145, ...), channel_id=1, replica_groups=mesh['dp'=16,'shard'=2] {'dp','shard'}, use_global_device_ids=true, to_apply=%region_95.97 | all-reduce | flops 8192 | bytes 65536 | tf_op jit(solution)/shard_map/psum | solution.py:52
  619.5 41.2 %all-reduce.21 = (f32[512]{0:T(512)}, f32[512]{0:T(512)}, f32[512]{0:T(512)S(1)}, f32[512]{0:T(512)S(1)}) all-reduce(f32[512]{0:T(512)S(1)} %get-tuple-element.159, f32[512]{0:T(512)S(1)} %get-tuple-element.158, f32[512]{0:T(512)S(1)} %get-tuple-element.155, ...), channel_id=1, replica_groups=mesh['dp'=16,'shard'=2] {'dp','shard'}, use_global_device_ids=true, to_apply=%region_99.101 | all-reduce | flops 2048 | bytes 16384 | tf_op jit(solution)/shard_map/psum | solution.py:52
  672.7 10.5 fusion.92
  698.6 10.5 fusion.93
  723.6 40.8 %all-reduce.20 = (f32[]{:T(128)}, f32[512]{0:T(512)S(1)}, f32[512]{0:T(512)S(1)}, f32[512]{0:T(512)S(1)}, f32[512]{0:T(512)S(1)}, /*index=5*/f32[128]{0:T(128)}) all-reduce(f32[]{:T(128)S(6)} %sub.259, f32[512]{0:T(512)S(1)} %get-tuple-element.321, ...), channel_id=1, replica_groups=mesh['dp'=16,'shard'=2] {'dp','shard'}, use_global_device_ids=true, to_apply=%region_67.69 | all-reduce | flops 2177 | bytes 17416 | tf_op jit(solution)/shard_map/psum | solution.py:238
  785.5 6.4 convolution_add_fusion.1
  795.2 8.1 convolution_add_fusion
  822.6 26.1 %all-reduce.33.cloned.1.call-done = f32[3000,128]{1,0:T(8,128)} async-done(((f32[3000,128]{1,0:T(8,128)}), f32[3000,128]{1,0:T(8,128)}) %all-reduce.33.cloned.1.call-update) | async-done | bytes 1536016 | tf_op jit(solution)/shard_map/psum | solution.py:238
  848.7 132.1 %reduce-scatter.14.cloned.1.call-done = f32[64,128]{1,0:T(8,128)} async-done(((f32[2048,128]{1,0:T(8,128)}), f32[64,128]{1,0:T(8,128)}) %reduce-scatter.14.cloned.1.call-update) | async-done | bytes 32784 | tf_op jit(solution)/shard_map/reduce_scatter | solution.py:237
  980.8 139.7 %reduce-scatter.16.cloned.1.call-done = f32[64,512]{1,0:T(8,128)} async-done(((f32[2048,512]{1,0:T(8,128)}), f32[64,512]{1,0:T(8,128)}) %reduce-scatter.16.cloned.1.call-update) | async-done | bytes 131088
  1120.5 139.7 %reduce-scatter.10.cloned.1.call-done = f32[16,2048]{1,0:T(8,128)} async-done(((f32[512,2048]{1,0:T(8,128)}), f32[16,2048]{1,0:T(8,128)}) %reduce-scatter.10.cloned.1.call-update) | async-done | bytes 131088 | tf_op jit(solution)/shard_map/reduce_scatter | solution.py:237
  1260.3 142.5 %reduce-scatter.8.cloned.1.call-done = f32[144,512]{1,0:T(8,128)} async-done(((f32[4608,512]{1,0:T(8,128)}), f32[144,512]{1,0:T(8,128)}) %reduce-scatter.8.cloned.1.call-update) | async-done | bytes 294928 | tf_op jit(solution)/shard_map/reduce_scatter | solution.py:237
  1402.7 186.8 %reduce-scatter.12.cloned.1.call-done = f32[64,2048]{1,0:T(8,128)} async-done(((f32[2048,2048]{1,0:T(8,128)}), f32[64,2048]{1,0:T(8,128)}) %reduce-scatter.12.cloned.1.call-update) | async-done | bytes 524304 | tf_op jit(solution)/shard_map/reduce_scatter | solution.py:237
  (592 shorter events, 271.1 us)
Async XLA Ops:
  7.2 62.9 %all-gather.5.cloned.1.call-start = ((), (), s32[]{:S(2)}) async-start(), calls=%async_computation.5 | async-start | bytes 2162688 | tf_op jit(solution)/shard_map/all_gather | solution.py:123
  7.9 160.5 %all-gather.7.cloned.1.call-start = ((), (), s32[]{:S(2)}) async-start(), calls=%async_computation.6 | async-start | bytes 4866048 | tf_op jit(solution)/shard_map/all_gather | solution.py:124
  8.7 209.2 %all-gather.9.cloned.1.call-start = ((), (), s32[]{:S(2)}) async-start(), calls=%async_computation.7 | async-start | bytes 2162688 | tf_op jit(solution)/shard_map/all_gather | solution.py:125
  9.4 272.2 %all-gather.11.cloned.1.call-start = ((), (), s32[]{:S(2)}) async-start(), calls=%async_computation.8 | async-start | bytes 8650752 | tf_op jit(solution)/shard_map/all_gather | solution.py:126
  10.0 838.7 %all-reduce.33.cloned.1.call-start = ((), (), s32[]{:S(2)}) async-start(), calls=%async_computation.13 | async-start | bytes 3072000 | tf_op jit(solution)/shard_map/psum | solution.py:238
  12.8 51.1 %copy-start.121 = (f32[4,2048]{1,0:T(4,128)S(1)}, f32[4,2048]{1,0:T(4,128)}, u32[]{:S(2)}) copy-start(f32[4,2048]{1,0:T(4,128)} %param.24) | copy-start | bytes 98308
  13.8 259.5 %copy-start.97 = (s32[4,36]{1,0:T(4,128)}, s32[4,36]{1,0:T(4,128)S(1)}, u32[]{:S(2)}) copy-start(s32[4,36]{1,0:T(4,128)S(1)} %get-tuple-element.331) | copy-start | bytes 1732
  13.9 264.4 %copy-start.99 = (s32[4,36]{1,0:T(4,128)}, s32[4,36]{1,0:T(4,128)S(1)}, u32[]{:S(2)}) copy-start(s32[4,36]{1,0:T(4,128)S(1)} %get-tuple-element.330) | copy-start | bytes 1732
  13.9 259.4 %copy-start.136 = (f32[4,4]{1,0:T(4,128)}, f32[4,4]{1,0:T(4,128)S(1)}, u32[]{:S(2)}) copy-start(f32[4,4]{1,0:T(4,128)S(1)} %convert_reduce_fusion) | copy-start | bytes 196
  14.0 264.2 %copy-start.138 = (f32[4,4]{1,0:T(4,128)}, f32[4,4]{1,0:T(4,128)S(1)}, u32[]{:S(2)}) copy-start(f32[4,4]{1,0:T(4,128)S(1)} %convert_reduce_fusion.1) | copy-start | bytes 196
  14.7 99.0 %copy-start.104 = (f32[1,512]{1,0:T(1,128)}, f32[1,512]{1,0:T(1,128)S(1)}, u32[]{:S(2)}) copy-start(f32[1,512]{1,0:T(1,128)S(1)} %get-tuple-element.314) | copy-start | bytes 6148
  14.7 99.0 %copy-start.140 = (f32[1,512]{1,0:T(1,128)}, f32[1,512]{1,0:T(1,128)S(1)}, u32[]{:S(2)}) copy-start(f32[1,512]{1,0:T(1,128)S(1)} %get-tuple-element.316) | copy-start | bytes 6148
  14.7 206.7 %copy-start.124 = (f32[1,512]{1,0:T(1,128)}, f32[1,512]{1,0:T(1,128)S(1)}, u32[]{:S(2)}) copy-start(f32[1,512]{1,0:T(1,128)S(1)} %get-tuple-element.313) | copy-start | bytes 6148
  14.7 206.6 %copy-start.143 = (f32[1,512]{1,0:T(1,128)}, f32[1,512]{1,0:T(1,128)S(1)}, u32[]{:S(2)}) copy-start(f32[1,512]{1,0:T(1,128)S(1)} %get-tuple-element.315) | copy-start | bytes 6148
  63.9 202.7 %copy-start.68 = (f32[1,2048]{1,0:T(1,128)}, f32[1,2048]{1,0:T(1,128)S(1)}, u32[]{:S(2)}) copy-start(f32[1,2048]{1,0:T(1,128)S(1)} %get-tuple-element.287) | copy-start | bytes 24580
  63.9 202.7 %copy-start.85 = (f32[1,2048]{1,0:T(1,128)}, f32[1,2048]{1,0:T(1,128)S(1)}, u32[]{:S(2)}) copy-start(f32[1,2048]{1,0:T(1,128)S(1)} %get-tuple-element.289) | copy-start | bytes 24580
  63.9 270.2 %copy-start.58 = (f32[1,2048]{1,0:T(1,128)}, f32[1,2048]{1,0:T(1,128)S(1)}, u32[]{:S(2)}) copy-start(f32[1,2048]{1,0:T(1,128)S(1)} %get-tuple-element.286) | copy-start | bytes 24580
  64.0 270.2 %copy-start.70 = (f32[1,2048]{1,0:T(1,128)}, f32[1,2048]{1,0:T(1,128)S(1)}, u32[]{:S(2)}) copy-start(f32[1,2048]{1,0:T(1,128)S(1)} %get-tuple-element.288) | copy-start | bytes 24580
  567.0 45.2 %copy-start.103 = (f32[2048]{0:T(1024)S(1)}, f32[2048]{0:T(1024)}, u32[]{:S(2)}) copy-start(f32[2048]{0:T(1024)} %get-tuple-element.290) | copy-start | bytes 24580
  716.5 264.3 %reduce-scatter.14.cloned.1.call-start = ((), (), s32[]{:S(2)}) async-start(), calls=%async_computation.12 | async-start | bytes 1081344 | tf_op jit(solution)/shard_map/reduce_scatter | solution.py:237
  723.5 397.0 %reduce-scatter.16.cloned.1.call-start = ((), (), s32[]{:S(2)}) async-start(), calls=%async_computation.14 | async-start | bytes 4325376
  777.0 483.3 %reduce-scatter.10.cloned.1.call-start = ((), (), s32[]{:S(2)}) async-start(), calls=%async_computation.10 | async-start | bytes 4325376 | tf_op jit(solution)/shard_map/reduce_scatter | solution.py:237
  781.9 620.9 %reduce-scatter.8.cloned.1.call-start = ((), (), s32[]{:S(2)}) async-start(), calls=%async_computation.9 | async-start | bytes 9732096 | tf_op jit(solution)/shard_map/reduce_scatter | solution.py:237
  792.0 797.5 %reduce-scatter.12.cloned.1.call-start = ((), (), s32[]{:S(2)}) async-start(), calls=%async_computation.11 | async-start | bytes 17301504 | tf_op jit(solution)/shard_map/reduce_scatter | solution.py:237
  (173 other events, 923.8 us)
Sparse Core Ops, SparseCore 0:
  10.9 59.1 all-gather.4
  73.0 62.4 all-gather.6
  138.4 55.4 all-gather.8
  196.6 77.1 all-gather.10
  716.6 132.0 all-reduce.32
  851.3 129.3 reduce-scatter.13
  983.7 136.7 reduce-scatter.15
  1123.5 136.7 reduce-scatter.9
  1267.7 134.9 reduce-scatter.7
  1405.5 184.0 reduce-scatter.11
where the time goes:
time: 1610 us; the launch traced here: 1600 us
  waiting for transfers between devices  776 us (48%)
  blocking collectives  496 us (31%)
  local copies, waits for them, and re-layouts  141 us (9%)
  matrix products  116 us (7%)
  other arithmetic  52 us (3%)
  between operations  19.6 us (1%)
    reduce_scatter x4, waiting for transfers between devices, per_device(): lax.psum_scatter(full_sums, ('dp', 'shard'), scatter_dimension=0, tiled=T...  601 us
    psum x4, blocking collectives, norm_forward(): lax.psum((jnp.sum(hidden, 0), jnp.sum(hidden * hidden, 0)), ('dp', 'shard'))  163 us
    unnamed x11, waiting for transfers between devices  142 us
    psum x3, blocking collectives, per_device(): lax.psum(jnp.sum(batch_codes, 0) + jnp.sum(stored_codes, 0), ('dp', 'shar...  122 us
    psum x3, blocking collectives, norm_backward(): lax.psum((jnp.sum(grad_out, 0), jnp.sum(grad_out * normed, 0)), ('dp', 's...  122 us
    all_gather x1, blocking collectives, per_device(): lax.all_gather(shards[4], ('dp', 'shard'), axis=0, tiled=True)  47.6 us
    psum x1, blocking collectives, per_device(): head_sums = lax.psum((loss_local, proto_grad, bias_grad), ('dp', 'shard'))  40.8 us
    dot_general x13, matrix products, product_bt(): lax.dot_general(left, right, (((1,), (1,)), ((), ())), preferred_element_...  37.4 us
  transfers between devices with their start and end apart: 10, of which 7 were waited for; matrix products, arithmetic and copies ran while one was open for 10% of the time, Pallas kernels for 0%

commit v1 on v0

v1 whole, which is shorter than its diff:
```python
import jax
import jax.numpy as jnp
from jax import lax
from jax.experimental import pallas as pl
from jax.experimental.pallas import tpu as pltpu
from jax.sharding import PartitionSpec as P

D = 2048
MID = 512
PROTOS = 3000
SIDE = 6
CROPS = 4
SINK_ITERS = 3
MICRO = 2


EPS_NORM = 1e-05
EPS_UNIT = 1e-06
SOFTMAX_HEAT = 0.1
SINK_EPS = 0.05
HIGH = lax.Precision.HIGHEST
BOTH = ("dp", "shard")
GATHERED_CODES_BYTES = 32 * 2**20


def product(left, right):
    return jnp.dot(left, right, preferred_element_type=jnp.float32)


def product_t(left, right):
    return lax.dot_general(
        left, right, (((0,), (0,)), ((), ())), preferred_element_type=jnp.float32
    )


def product_bt(left, right):
    return lax.dot_general(
        left, right, (((1,), (1,)), ((), ())), preferred_element_type=jnp.float32
    )


def silu_slope(values):
    sigmoid_value = jax.nn.sigmoid(values)
    return sigmoid_value * (1.0 + values * (1.0 - sigmoid_value))


def swap_cores(values):
    return lax.ppermute(values, "shard", [(0, 1), (1, 0)])


def flip_dp(values, bits, size):
    return lax.ppermute(values, "dp", [(i, i ^ bits) for i in range(size)])


def flip_both(values, dp_bits, size):
    pairs = [(2 * i + c, 2 * (i ^ dp_bits[c]) + c) for i in range(size) for c in range(2)]
    return lax.ppermute(values, BOTH, pairs)


def sum_over_dp(values, size):
    bit = 1
    while bit < size:
        if bit * 2 < size:
            one, two, three = (flip_dp(values, bit * k, size) for k in (1, 2, 3))
            values = (values + one) + (two + three)
            bit *= 4
        else:
            values = values + flip_dp(values, bit, size)
            bit *= 2
    return values


def exchange_orders(size):
    bits = [1 << k for k in range(size.bit_length() - 1)][::-1]
    first = bits[:-2] + [bits[-1], bits[-2]] if len(bits) > 1 else bits
    return list(zip(first, bits))


def relative_slots(size):
    orders = exchange_orders(size)
    me_dp, me_core = lax.axis_index("dp"), lax.axis_index("shard")
    device = jnp.arange(2 * size, dtype=jnp.int32)
    apart_dp, apart_core = (device // 2) ^ me_dp, (device % 2) ^ me_core
    holder = device % 2
    slot = apart_core * size
    for place, (bit_zero, bit_one) in enumerate(orders):
        on = jnp.where(holder == 0, apart_dp & bit_zero, apart_dp & bit_one) != 0
        slot = slot + jnp.where(on, 1 << place, 0)
    return slot.astype(jnp.int32)


def gather_relative(shard, size):
    held = shard[None]
    for dp_bits in exchange_orders(size):
        held = jnp.concatenate([held, flip_both(held, dp_bits, size)], 0)
    return jnp.concatenate([held, swap_cores(held)], 0)


def scatter_relative(blocks, size):
    half = blocks.shape[0] // 2
    held = blocks[:half].astype(jnp.float32) + swap_cores(blocks[half:]).astype(jnp.float32)
    for dp_bits in exchange_orders(size)[::-1]:
        half = held.shape[0] // 2
        sent = held[half:].astype(jnp.bfloat16)
        held = held[:half] + flip_both(sent, dp_bits, size).astype(jnp.float32)
    return held[0]


def reorder_kernel(to_slots, table, source, target):
    def move(i, carry):
        slot = table[i]
        if to_slots:
            target[slot] = source[i].astype(target.dtype)
        else:
            target[i] = source[slot]
        return carry

    lax.fori_loop(0, source.shape[0], move, 0)


def reorder(blocks, slots, to_slots):
    return pl.pallas_call(
        lambda *refs: reorder_kernel(to_slots, *refs),
        out_shape=jax.ShapeDtypeStruct(blocks.shape, jnp.bfloat16),
        in_specs=[
            pl.BlockSpec(memory_space=pltpu.SMEM),
            pl.BlockSpec(memory_space=pltpu.VMEM),
        ],
        out_specs=pl.BlockSpec(memory_space=pltpu.VMEM),
        compiler_params=pltpu.CompilerParams(vmem_limit_bytes=32 * 2**20),
        cost_estimate=pl.CostEstimate(
            flops=0, bytes_accessed=4 * blocks.size, transcendentals=0
        ),
    )(slots, blocks)


def gather_rows(shard, slots, size):
    blocks = reorder(gather_relative(shard, size), slots, False)
    return blocks.reshape(-1, shard.shape[1])


def scatter_rows(grads, slots, size):
    blocks = grads.reshape(2 * size, -1, grads.shape[1])
    return scatter_relative(reorder(blocks, slots, True), size)


def norm_forward(hidden, gain_row, shift_row, row_total, size):
    totals = sum_over_dp(jnp.stack([jnp.sum(hidden, 0), jnp.sum(hidden * hidden, 0)]), size)
    average = totals[0] / row_total
    inverse = lax.rsqrt(totals[1] / row_total - average * average + EPS_NORM)
    normed = (hidden - average) * inverse
    return (gain_row * normed + shift_row, normed, inverse)


def norm_backward(grad_out, normed, inverse, gain_row, row_total, size, extra=None):
    totals = jnp.stack([jnp.sum(grad_out, 0), jnp.sum(grad_out * normed, 0)])
    if extra is None:
        totals = sum_over_dp(totals, size)
    else:
        width = extra.shape[0]
        extra_rows = jnp.pad(extra, (0, totals.shape[1] - width))[None]
        totals = sum_over_dp(jnp.concatenate([totals, extra_rows], 0), size)
        extra = totals[2, :width]
    grad_in = (
        gain_row * inverse * (grad_out - totals[0] / row_total - normed * (totals[1] / row_total))
    )
    return (grad_in, totals[1], totals[0], extra)


def make_patches(values):
    canvas_count, side_len = (values.shape[0], values.shape[1])
    padded = jnp.pad(values, ((0, 0), (1, 1), (1, 1), (0, 0)))
    pieces = [
        padded[:, row_shift : row_shift + side_len, col_shift : col_shift + side_len, :]
        for row_shift in range(3)
        for col_shift in range(3)
    ]
    return jnp.concatenate(pieces, 3).reshape(canvas_count * side_len * side_len, -1)


def fold_patches(grads, canvas_count, side_len, channels):
    grads = grads.reshape(canvas_count, side_len, side_len, 9, channels)
    summed = jnp.zeros((canvas_count, side_len + 2, side_len + 2, channels), jnp.float32)
    for row_shift in range(3):
        for col_shift in range(3):
            summed = summed + jnp.pad(
                grads[:, :, :, row_shift * 3 + col_shift, :],
                ((0, 0), (row_shift, 2 - row_shift), (col_shift, 2 - col_shift), (0, 0)),
            )
    return summed[:, 1 : side_len + 1, 1 : side_len + 1, :].reshape(
        canvas_count * side_len * side_len, channels
    )


def sinkhorn(batch_codes, stored_codes, total):
    for turn in range(SINK_ITERS):
        column_totals = total(jnp.sum(batch_codes, 0) + jnp.sum(stored_codes, 0))
        batch_codes = batch_codes / column_totals
        stored_codes = stored_codes / column_totals
        batch_codes = batch_codes / jnp.sum(batch_codes, 1, keepdims=True)
        stored_codes = stored_codes / jnp.sum(stored_codes, 1, keepdims=True)
    return batch_codes


def swapped_loss(scores, codes, pick, loss_factor_weight):
    rows = scores.shape[0]
    target = jnp.einsum(
        "cab,cbk->cak", pick, codes.reshape(rows // CROPS, CROPS, PROTOS), precision=HIGH
    ).reshape(rows, PROTOS)
    log_likelihoods = jax.nn.log_softmax(scores / SOFTMAX_HEAT, axis=1)
    score_grad = (jnp.exp(log_likelihoods) * jnp.sum(target, 1, keepdims=True) - target) * (
        loss_factor_weight / SOFTMAX_HEAT
    )
    return -jnp.sum(target * log_likelihoods), score_grad.astype(jnp.bfloat16)


def per_device(
    canvases,
    crop_map,
    partner,
    queue,
    w_reduce,
    w_spatial,
    w_expand,
    w_hidden,
    w_project,
    norm_mid,
    norm_wide,
    bias_out,
    prototypes,
):
    size = lax.axis_size("dp")
    me_dp, me_core = lax.axis_index("dp"), lax.axis_index("shard")
    own_canvases = canvases.shape[1]
    canvas_count = 2 * own_canvases
    pixels = SIDE * SIDE
    local_rows = canvas_count * pixels
    local_crops = canvas_count * CROPS
    pixel_total = float(local_rows * size)
    crop_count = local_crops * size
    crop_total = float(crop_count)
    loss_factor_weight = 1.0 / (MICRO * crop_total)
    crop_ids = jnp.arange(CROPS, dtype=jnp.int32)
    slots = relative_slots(size)

    def both_cores(values):
        mine = lax.dynamic_index_in_dim(values, me_core, 0, keepdims=False)
        other = lax.dynamic_index_in_dim(values, 1 - me_core, 0, keepdims=False)
        return jnp.concatenate([mine, swap_cores(other)], 0)

    full_reduce = gather_rows(w_reduce, slots, size)
    full_spatial = gather_rows(w_spatial, slots, size)
    full_expand = gather_rows(w_expand, slots, size)
    full_head = lax.all_gather(
        jnp.concatenate([w_hidden, w_project], 1), BOTH, axis=0, tiled=True
    )
    full_hidden, full_project = full_head[:, :D], full_head[:, D:]

    input_rows = both_cores(canvases).reshape(local_rows, D)
    labels = both_cores(jnp.concatenate([crop_map, partner], 2))
    crop_map, partner = labels[:, :pixels], labels[:, pixels:]
    onehot = (crop_map[:, None, :] == crop_ids[None, :, None]).astype(jnp.float32)
    crop_sizes = jnp.sum(onehot, 2)

    gathered_codes = crop_count * PROTOS * 4 <= GATHERED_CODES_BYTES
    if gathered_codes:
        all_queue = lax.all_gather(queue, BOTH, axis=0, tiled=True)
        all_partner = lax.all_gather(partner, "dp", axis=0, tiled=True)
    else:
        all_queue = jnp.concatenate([queue, swap_cores(queue)], 0)
        all_partner = partner
    queue_codes = jnp.exp(product_bt(all_queue, prototypes) / SINK_EPS)
    pick = (all_partner[:, :, None] == crop_ids[None, None, :]).astype(jnp.float32)

    pre_one = product(input_rows, full_reduce)
    norm_one, unit_one, inv_one = norm_forward(
        pre_one, norm_mid[0], norm_mid[1], pixel_total, size
    )
    first_activation = jax.nn.silu(norm_one).astype(jnp.bfloat16)
    image_patches = make_patches(first_activation.reshape(canvas_count, SIDE, SIDE, MID))
    pre_two = product(image_patches, full_spatial)
    norm_two, unit_two, inv_two = norm_forward(
        pre_two, norm_mid[2], norm_mid[3], pixel_total, size
    )
    act_two = jax.nn.silu(norm_two).astype(jnp.bfloat16)
    pre_three = product(act_two, full_expand)
    norm_three, unit_three, inv_three = norm_forward(
        pre_three, norm_wide[0], norm_wide[1], pixel_total, size
    )
    joined = norm_three + input_rows.astype(jnp.float32)
    block_out = jax.nn.silu(joined)
    pooled = (
        jnp.einsum(
            "cps,csd->cpd", onehot, block_out.reshape(canvas_count, pixels, D), precision=HIGH
        )
        / crop_sizes[:, :, None]
    )
    pooled_low = pooled.reshape(local_crops, D).astype(jnp.bfloat16)
    pre_head = product(pooled_low, full_hidden)
    norm_head, unit_head, inv_head = norm_forward(
        pre_head, norm_wide[2], norm_wide[3], crop_total, size
    )
    act_head = jax.nn.silu(norm_head).astype(jnp.bfloat16)
    embed = product(act_head, full_project) + bias_out
    inv_length = lax.rsqrt(jnp.sum(embed * embed, 1, keepdims=True) + EPS_UNIT)
    unit_embed = embed * inv_length
    unit_low = unit_embed.astype(jnp.bfloat16)

    if gathered_codes:
        spread = jnp.broadcast_to(unit_low[None], (size,) + unit_low.shape)
        all_units = lax.all_to_all(spread, "dp", 0, 0).reshape(crop_count, -1)
        scores = product_bt(all_units, prototypes)
        codes = sinkhorn(jnp.exp(scores / SINK_EPS), queue_codes, lambda sums: sums)
        loss_part, score_low = swapped_loss(scores, codes, pick, loss_factor_weight)
        proto_part = product_t(score_low, all_units)
        score_low = lax.dynamic_slice_in_dim(score_low, me_dp * local_crops, local_crops, 0)
    else:
        scores = product_bt(unit_low, prototypes)
        codes = sinkhorn(
            jnp.exp(scores / SINK_EPS), queue_codes, lambda sums: sum_over_dp(sums, size)
        )
        loss_part, score_low = swapped_loss(scores, codes, pick, loss_factor_weight)
        proto_part, loss_part = lax.psum((product_t(score_low, unit_low), loss_part), "dp")
    proto_grad = proto_part + swap_cores(proto_part)
    unit_grad = product(score_low, prototypes)
    embed_grad = inv_length * (
        unit_grad - unit_embed * jnp.sum(unit_grad * unit_embed, 1, keepdims=True)
    )
    embed_low = embed_grad.astype(jnp.bfloat16)

    head_act_grad = product_bt(embed_low, full_project) * silu_slope(norm_head)
    head_grad, gain_head, shift_head, bias_part = norm_backward(
        head_act_grad,
        unit_head,
        inv_head,
        norm_wide[2],
        crop_total,
        size,
        jnp.sum(embed_grad, 0),
    )
    head_low = head_grad.astype(jnp.bfloat16)
    left = lax.all_gather(
        jnp.concatenate([pooled_low, act_head], 1), "dp", axis=0, tiled=True
    )
    right = lax.all_gather(jnp.concatenate([head_low, embed_low], 1), "dp", axis=0, tiled=True)
    chip_rows = 2 * w_hidden.shape[0]
    first_row = me_dp * chip_rows
    hidden_part = product_t(
        lax.dynamic_slice_in_dim(left[:, :D], first_row, chip_rows, 1), right[:, :D]
    )
    project_part = product_t(
        lax.dynamic_slice_in_dim(left[:, D:], first_row, chip_rows, 1), right[:, D:]
    )

    def own_rows(part):
        half = chip_rows // 2
        mine = lax.dynamic_slice_in_dim(part, me_core * half, half, 0)
        other = lax.dynamic_slice_in_dim(part, (1 - me_core) * half, half, 0)
        return mine + swap_cores(other)

    grad_hidden, grad_project = own_rows(hidden_part), own_rows(project_part)

    pooled_grad = (
        product_bt(head_low, full_hidden).reshape(canvas_count, CROPS, D)
        / crop_sizes[:, :, None]
    )
    out_grad = jnp.einsum("cps,cpd->csd", onehot, pooled_grad, precision=HIGH).reshape(
        local_rows, D
    )
    joined_grad = out_grad * silu_slope(joined)
    three_grad, gain_three, shift_three, _ = norm_backward(
        joined_grad, unit_three, inv_three, norm_wide[0], pixel_total, size
    )
    three_low = three_grad.astype(jnp.bfloat16)
    grad_expand = scatter_rows(product_t(act_two, three_low), slots, size)
    two_act_grad = product_bt(three_low, full_expand) * silu_slope(norm_two)
    two_grad, gain_two, shift_two, _ = norm_backward(
        two_act_grad, unit_two, inv_two, norm_mid[2], pixel_total, size
    )
    two_low = two_grad.astype(jnp.bfloat16)
    grad_spatial = scatter_rows(product_t(image_patches, two_low), slots, size)
    patch_grad = product_bt(two_low, full_spatial)
    one_act_grad = fold_patches(patch_grad, canvas_count, SIDE, MID) * silu_slope(norm_one)
    one_grad, gain_one, shift_one, _ = norm_backward(
        one_act_grad, unit_one, inv_one, norm_mid[0], pixel_total, size
    )
    one_low = one_grad.astype(jnp.bfloat16)
    grad_reduce = scatter_rows(product_t(input_rows, one_low), slots, size)
    input_grad = (joined_grad + product_bt(one_low, full_reduce)).reshape(
        2, own_canvases, SIDE, SIDE, D
    )
    other_micro = swap_cores(input_grad[1])
    on_first = me_core == 0
    grad_canvases = jnp.stack(
        [
            jnp.where(on_first, input_grad[0], other_micro),
            jnp.where(on_first, other_micro, input_grad[0]),
        ]
    )
    narrow = jnp.concatenate(
        [
            jnp.stack([gain_one, shift_one, gain_two, shift_two]).reshape(-1),
            jnp.stack([gain_three, shift_three, gain_head, shift_head]).reshape(-1),
            bias_part,
            jnp.broadcast_to(loss_part, (128,)),
        ]
    )
    narrow = narrow + swap_cores(narrow)
    mid_end, wide_end = norm_mid.size, norm_mid.size + norm_wide.size
    bias_end = wide_end + bias_out.shape[0]
    return (
        narrow[bias_end] * loss_factor_weight,
        grad_canvases,
        grad_reduce,
        grad_spatial,
        grad_expand,
        grad_hidden,
        grad_project,
        narrow[:mid_end].reshape(norm_mid.shape),
        narrow[mid_end:wide_end].reshape(norm_wide.shape),
        narrow[wide_end:bias_end],
        proto_grad,
    )


def solution(mesh):
    return jax.shard_map(
        per_device,
        mesh=mesh,
        in_specs=(
            P(None, ("dp", "shard"), None, None, None),
            P(None, ("dp", "shard"), None),
            P(None, ("dp", "shard"), None),
            P(("dp", "shard"), None),
            P(("dp", "shard"), None),
            P(("dp", "shard"), None),
            P(("dp", "shard"), None),
            P(("dp", "shard"), None),
            P(("dp", "shard"), None),
            P(),
            P(),
            P(),
            P(),
        ),
        out_specs=(
            P(),
            P(None, ("dp", "shard"), None, None, None),
            P(("dp", "shard"), None),
            P(("dp", "shard"), None),
            P(("dp", "shard"), None),
            P(("dp", "shard"), None),
            P(("dp", "shard"), None),
            P(),
            P(),
            P(),
            P(),
        ),
        check_vma=False,
    )
```

time: 1610 us -> 591 us (0.37)
  waiting for transfers between devices: 776 us -> 91.2 us
  blocking collectives: 496 us -> 77.7 us
  starting transfers between devices: 0.65 us -> 108 us
  matrix products: 116 us -> 64.6 us
  other arithmetic: 52 us -> 74.8 us
    reduce_scatter x4 -> x0, waiting for transfers between devices: 601 us -> none  [per_device(): lax.psum_scatter(full_sums, ('dp', 'shard'), scatter_dimension=0, tiled=T...]
    psum x11 -> x0, blocking collectives: 448 us -> none  [the longest x4 163 us: norm_forward(): lax.psum((jnp.sum(hidden, 0), jnp.sum(hidden * hidden, 0)), ('dp', 'shard'))]
    unnamed x11 -> x3, waiting for transfers between devices: 142 us -> 0.05 us
    ppermute x0 -> x85, starting transfers between devices: none -> 104 us  [the longest x48 50.4 us: flip_dp(): return lax.ppermute(values, 'dp', [(i, i ^ bits) for i in range(size)])]
    ppermute x0 -> x85, waiting for transfers between devices: none -> 86.3 us  [the longest x24 71.6 us: flip_both(): return lax.ppermute(values, BOTH, pairs)]
    all_gather x1 -> x2, blocking collectives: 47.6 us -> 77.7 us  [the longest x1 47.6 us: per_device(): all_queue = lax.all_gather(queue, BOTH, axis=0, tiled=True)]
    psum x1 -> x0, waiting for transfers between devices: 26.1 us -> none  [per_device(): head_sums = lax.psum((loss_local, proto_grad, bias_grad), ('dp', 'shard'))]
    dot_general x12 -> x6, matrix products: 34.9 us -> 14.9 us  [product_t(): lax.dot_general(left, right, (((0,), (0,)), ((), ())), preferred_element_...]
  transfers between devices with their start and end apart: 10 -> 89, of which waited for: 7 -> 26; matrix products, arithmetic and copies ran while one was open for 10% -> 44% of each run, Pallas kernels for 0% -> 1%
where the time goes in v1:
time: 591 us; the launch traced here: 585 us
  local copies, waits for them, and re-layouts  142 us (24%)
  starting transfers between devices  108 us (18%)
  waiting for transfers between devices  91.2 us (15%)
  blocking collectives  77.7 us (13%)
  other arithmetic  74.8 us (13%)
  matrix products  64.6 us (11%)
  between operations  18.5 us (3%)
  Pallas kernels  8.55 us (1%)
    ppermute x24, waiting for transfers between devices, flip_both(): return lax.ppermute(values, BOTH, pairs)  71.6 us
    ppermute x48, starting transfers between devices, flip_dp(): return lax.ppermute(values, 'dp', [(i, i ^ bits) for i in range(size)])  50.4 us
    all_gather x1, blocking collectives, per_device(): all_queue = lax.all_gather(queue, BOTH, axis=0, tiled=True)  47.6 us
    all_gather x1, blocking collectives, per_device(): all_partner = lax.all_gather(partner, 'dp', axis=0, tiled=True)  30.1 us
    ppermute x13, starting transfers between devices, swap_cores(): return lax.ppermute(values, 'shard', [(0, 1), (1, 0)])  29.5 us
    unnamed x199, local copies, waits for them, and re-layouts  26.5 us
    ppermute x24, starting transfers between devices, flip_both(): return lax.ppermute(values, BOTH, pairs)  24.1 us
    dot_general x7, matrix products, product_bt(): lax.dot_general(left, right, (((1,), (1,)), ((), ())), preferred_element_...  21.1 us
  transfers between devices with their start and end apart: 89, of which 26 were waited for; matrix products, arithmetic and copies ran while one was open for 44% of the time, Pallas kernels for 1%

profile of v1, /device:TPU:1, one launch (start us, length us, event | category | flops | bytes accessed | tf_op | source)
XLA Modules:
  0.0 585.1 jit_solution(9897723077244799103)
XLA Ops:
  21.9 9.2 %collective-permute-done.23 = bf16[1,16,2048]{2,1,0:T(8,128)(2,1)S(1)} collective-permute-done((bf16[1,16,2048]{2,1,0:T(8,128)(2,1)S(1)}, bf16[1,16,2048]{2,1,0:T(8,128)(2,1)S(1)}, u32[]{:S(2)}, u32[]{:S(2)}) %collective-permute-start.23) | collective-permute-done | bytes 65568 | tf_op jit(solution)/shard_map/ppermute | solution.py:57
  45.6 14.0 %collective-permute-done.4 = bf16[8,64,512]{2,1,0:T(8,128)(2,1)S(1)} collective-permute-done((bf16[8,64,512]{2,1,0:T(8,128)(2,1)S(1)}, bf16[8,64,512]{2,1,0:T(8,128)(2,1)S(1)}, u32[]{:S(2)}, u32[]{:S(2)}) %collective-permute-start.4) | collective-permute-done | bytes 524320 | tf_op jit(solution)/shard_map/ppermute | solution.py:57
  83.8 16.5 %collective-permute-done.15 = bf16[8,144,512]{2,1,0:T(8,128)(2,1)} collective-permute-done((bf16[8,144,512]{2,1,0:T(8,128)(2,1)}, bf16[8,144,512]{2,1,0:T(8,128)(2,1)}, u32[]{:S(2)}, u32[]{:S(2)}) %collective-permute-start.15) | collective-permute-done | bytes 1179680 | tf_op jit(solution)/shard_map/ppermute | solution.py:57
  183.3 5.8 fusion.78
  191.8 47.6 %all_gather.17 = bf16[512,128]{1,0:T(8,128)(2,1)S(1)} all-gather(bf16[16,128]{1,0:T(8,128)(2,1)S(1)} %copy-done.79), channel_id=1, replica_groups=mesh['dp'=16,'shard'=2] {'dp','shard'}, dimensions={0}, use_global_device_ids=true | all-gather | bytes 135168 | tf_op jit(solution)/shard_map/all_gather | solution.py:267
  247.5 30.1 %all-gather = s32[16,8,4]{1,2,0:T(4,128)} all-gather(s32[1,8,4]{1,2,0:T(4,128)S(1)} %bitcast.275), channel_id=1, replica_groups=mesh['dp'=16,'shard'=2] {'dp'}, dimensions={0}, use_global_device_ids=true | all-gather | bytes 2176 | tf_op jit(solution)/shard_map/all_gather | solution.py:268
  291.7 4.8 all-to-all-done
  300.7 5.0 exponential_reduce_fusion
  311.4 5.1 fusion.18
  323.2 6.5 %copy.66 = f32[512,3000]{1,0:T(8,128)} copy(f32[512,3000]{0,1:T(8,128)} %fusion.12) | data formatting | bytes 12288000 | tf_op jit(solution)/shard_map/div | solution.py:200
  329.7 7.7 %reshape.148 = f32[128,4,3000]{2,1,0:T(4,128)} reshape(f32[512,3000]{1,0:T(8,128)} %copy.66) | data formatting | bytes 12288000 | tf_op jit(solution)/shard_map/reshape | solution.py:208
  337.4 11.3 %fusion.82 = (f32[128,4]{1,0:T(8,128)}, f32[128,4,3000]{2,1,0:T(4,128)}) fusion(f32[128,4,3000]{2,1,0:T(4,128)} %reshape.148, s32[128,4]{1,0:T(8,128)S(1)} %bitcast.193), kind=kOutput, calls=%fused_computation.321 | convolution fusion | flops 75265536 | bytes 12292096 | tf_op jit(solution)/shard_map/cab,cbk->cak/dot_general | solution.py:207
  348.7 8.0 %reshape.149 = f32[512,3000]{1,0:T(8,128)} reshape(f32[128,4,3000]{2,1,0:T(4,128)} %get-tuple-element.167) | data formatting | bytes 12288000 | tf_op jit(solution)/shard_map/reshape | solution.py:209
  356.7 6.6 %copy.67 = f32[512,3000]{0,1:T(8,128)} copy(f32[512,3000]{1,0:T(8,128)} %reshape.149) | data formatting | bytes 12288000 | tf_op jit(solution)/shard_map/reshape | solution.py:209
  364.7 6.3 %multiply_convert_fusion = (bf16[512,3000]{0,1:T(8,128)(2,1)S(1)}, f32[]{:T(128)}) fusion(f32[512,3000]{0,1:T(8,128)} %copy.67, f32[512,3000]{0,1:T(8,128)} %copy-done.12, f32[512]{0:T(512)} %mul.394, f32[512]{0:T(512)S(1)} %log.9, f32[512]{0:T(512)} %copy-done.69), kind=kLoop, calls=%fused_computation.19 | loop fusion | flops 13823999 | bytes 15366148 | tf_op jit(solution)/shard_map/convert_element_type | solution.py:214
  390.6 6.1 %fusion.8 = f32[32,2048]{1,0:T(8,128)S(1)} fusion(bf16[32,2048]{1,0:T(8,128)(2,1)S(1)} %multiply_convert_fusion.6, bf16[2048,2176]{1,0:T(8,128)(2,1)} %all-gather.5.cloned.1.call-done), kind=kOutput, calls=%fused_computation.12 | convolution fusion | flops 268435456 | bytes 8781824 | tf_op jit(solution)/shard_map/dot_general | solution.py:37
  402.5 5.6 fusion.71
  413.9 12.8 %collective-permute-start.84 = (f32[3000,128]{1,0:T(8,128)}, f32[3000,128]{1,0:T(8,128)}, u32[]{:S(2)}, u32[]{:S(2)}) collective-permute-start(f32[3000,128]{1,0:T(8,128)} %fusion.83), channel_id=1, source_target_pairs={{0,1},{1,0},{2,3},{3,2},{4,5},{5,4},{6,7},{7,6},{8,9},{9,8},{10,11... | collective-permute-start | bytes 4608008 | tf_op jit(solution)/shard_map/ppermute | solution.py:48
  526.9 6.5 %collective-permute-done.79 = bf16[4,16,2048]{2,1,0:T(8,128)(2,1)S(1)} collective-permute-done((bf16[4,16,2048]{2,1,0:T(8,128)(2,1)S(1)}, bf16[4,16,2048]{2,1,0:T(8,128)(2,1)S(1)}, u32[]{:S(2)}, u32[]{:S(2)}) %collective-permute-start.79) | collective-permute-done | bytes 262176 | tf_op jit(solution)/shard_map/ppermute | solution.py:57
  533.5 5.4 collective-permute-done.69
  539.2 5.6 collective-permute-done.73
  548.9 5.5 collective-permute-done.74
  556.0 5.0 collective-permute-done.75
  562.5 4.8 fusion.79
  (556 shorter events, 324.7 us)
Async XLA Ops:
  7.2 176.1 %all-gather.5.cloned.1.call-start = ((), (), s32[]{:S(2)}) async-start(), calls=%async_computation.1 | async-start | bytes 9191424 | tf_op jit(solution)/shard_map/all_gather | solution.py:254
  15.1 51.3 %collective-permute-start = (bf16[4,6,6,2048]{3,0,2,1:T(4,128)(2,1)}, bf16[4,6,6,2048]{3,0,2,1:T(4,128)(2,1)}, u32[]{:S(2)}, u32[]{:S(2)}) collective-permute-start(bf16[4,6,6,2048]{3,0,2,1:T(4,128)(2,1)} %get-tuple-element.88), channel_id=1, source_target_pairs={{0,1},{1,0},{2,3},{3,2},{4,5},{5,4},{6,7},{7,6},{8,9},{9,8},{10,11... | collective-permute-start | bytes 1769480 | tf_op jit(solution)/shard_map/ppermute | solution.py:48
  36.4 25.7 %collective-permute-start.25 = (bf16[4,16,2048]{2,1,0:T(8,128)(2,1)S(1)}, bf16[4,16,2048]{2,1,0:T(8,128)(2,1)S(1)}, u32[]{:S(2)}, u32[]{:S(2)}) collective-permute-start(bf16[4,16,2048]{2,1,0:T(8,128)(2,1)S(1)} %pad_maximum_fusion.9), channel_id=1, source_target_pairs={{0,2},{1,5},{2,0},{3,7},{4,6},{5,1},{6,4},{7,3},{8,10},{9,13},{10,... | collective-permute-start | bytes 786440 | tf_op jit(solution)/shard_map/ppermute | solution.py:57
  39.7 19.9 %collective-permute-start.4 = (bf16[8,64,512]{2,1,0:T(8,128)(2,1)S(1)}, bf16[8,64,512]{2,1,0:T(8,128)(2,1)S(1)}, u32[]{:S(2)}, u32[]{:S(2)}) collective-permute-start(bf16[8,64,512]{2,1,0:T(8,128)(2,1)S(1)} %pad_maximum_fusion.4), channel_id=1, source_target_pairs={{0,4},{1,3},{2,6},{3,1},{4,0},{5,7},{6,2},{7,5},{8,12},{9,11},{10,... | collective-permute-start | bytes 1572872 | tf_op jit(solution)/shard_map/ppermute | solution.py:57
  43.6 20.5 %collective-permute-start.14 = (bf16[4,144,512]{2,1,0:T(8,128)(2,1)S(1)}, bf16[4,144,512]{2,1,0:T(8,128)(2,1)S(1)}, u32[]{:S(2)}, u32[]{:S(2)}) collective-permute-start(bf16[4,144,512]{2,1,0:T(8,128)(2,1)S(1)} %pad_maximum_fusion.3), channel_id=1, source_target_pairs={{0,2},{1,5},{2,0},{3,7},{4,6},{5,1},{6,4},{7,3},{8,10},{9,13},{10,... | collective-permute-start | bytes 1769480 | tf_op jit(solution)/shard_map/ppermute | solution.py:57
  62.9 43.9 %collective-permute-start.26 = (bf16[8,16,2048]{2,1,0:T(8,128)(2,1)}, bf16[8,16,2048]{2,1,0:T(8,128)(2,1)}, u32[]{:S(2)}, u32[]{:S(2)}) collective-permute-start(bf16[8,16,2048]{2,1,0:T(8,128)(2,1)} %pad_maximum_fusion.5), channel_id=1, source_target_pairs={{0,4},{1,3},{2,6},{3,1},{4,0},{5,7},{6,2},{7,5},{8,12},{9,11},{10,... | collective-permute-start | bytes 1572872 | tf_op jit(solution)/shard_map/ppermute | solution.py:57
  65.3 35.0 %collective-permute-start.15 = (bf16[8,144,512]{2,1,0:T(8,128)(2,1)}, bf16[8,144,512]{2,1,0:T(8,128)(2,1)}, u32[]{:S(2)}, u32[]{:S(2)}) collective-permute-start(bf16[8,144,512]{2,1,0:T(8,128)(2,1)} %pad_maximum_fusion.2), channel_id=1, source_target_pairs={{0,4},{1,3},{2,6},{3,1},{4,0},{5,7},{6,2},{7,5},{8,12},{9,11},{10,... | collective-permute-start | bytes 3538952 | tf_op jit(solution)/shard_map/ppermute | solution.py:57
  80.7 23.3 %collective-permute-start.6 = (f32[2,512]{1,0:T(2,128)S(1)}, f32[2,512]{1,0:T(2,128)S(1)}, u32[]{:S(2)}, u32[]{:S(2)}) collective-permute-start(f32[2,512]{1,0:T(2,128)S(1)} %pad_maximum_fusion.19), channel_id=1, source_target_pairs={{0,2},{2,0},{4,6},{6,4},{8,10},{10,8},{12,14},{14,12},{16,18},{18,... | collective-permute-start | bytes 12296 | tf_op jit(solution)/shard_map/ppermute | solution.py:52
  82.2 21.8 %collective-permute-start.7 = (f32[2,512]{1,0:T(2,128)S(1)}, f32[2,512]{1,0:T(2,128)S(1)}, u32[]{:S(2)}, u32[]{:S(2)}) collective-permute-start(f32[2,512]{1,0:T(2,128)S(1)} %pad_maximum_fusion.19), channel_id=1, source_target_pairs={{0,4},{2,6},{4,0},{6,2},{8,12},{10,14},{12,8},{14,10},{16,20},{18,... | collective-permute-start | bytes 12296 | tf_op jit(solution)/shard_map/ppermute | solution.py:52
  83.8 20.3 %collective-permute-start.8 = (f32[2,512]{1,0:T(2,128)S(1)}, f32[2,512]{1,0:T(2,128)S(1)}, u32[]{:S(2)}, u32[]{:S(2)}) collective-permute-start(f32[2,512]{1,0:T(2,128)S(1)} %pad_maximum_fusion.19), channel_id=1, source_target_pairs={{0,6},{2,4},{4,2},{6,0},{8,14},{10,12},{12,10},{14,8},{16,22},{18,... | collective-permute-start | bytes 12296 | tf_op jit(solution)/shard_map/ppermute | solution.py:52
  103.3 33.7 %collective-permute-start.16 = (bf16[16,144,512]{2,1,0:T(8,128)(2,1)}, bf16[16,144,512]{2,1,0:T(8,128)(2,1)}, u32[]{:S(2)}, u32[]{:S(2)}) collective-permute-start(bf16[16,144,512]{2,1,0:T(8,128)(2,1)} %get-tuple-element.85), channel_id=1, source_target_pairs={{0,1},{1,0},{2,3},{3,2},{4,5},{5,4},{6,7},{7,6},{8,9},{9,8},{10,11... | collective-permute-start | bytes 7077896 | tf_op jit(solution)/shard_map/ppermute | solution.py:48
  108.9 47.2 %collective-permute-start.27 = (bf16[16,16,2048]{2,1,0:T(8,128)(2,1)}, bf16[16,16,2048]{2,1,0:T(8,128)(2,1)}, u32[]{:S(2)}, u32[]{:S(2)}) collective-permute-start(bf16[16,16,2048]{2,1,0:T(8,128)(2,1)} %get-tuple-element.93), channel_id=1, source_target_pairs={{0,1},{1,0},{2,3},{3,2},{4,5},{5,4},{6,7},{7,6},{8,9},{9,8},{10,11... | collective-permute-start | bytes 3145736 | tf_op jit(solution)/shard_map/ppermute | solution.py:48
  189.1 50.3 %collective-permute-start.35 = (f32[2,2048]{1,0:T(2,128)S(1)}, f32[2,2048]{1,0:T(2,128)S(1)}, u32[]{:S(2)}, u32[]{:S(2)}) collective-permute-start(f32[2,2048]{1,0:T(2,128)S(1)} %pad_maximum_fusion.17), channel_id=1, source_target_pairs={{0,2},{2,0},{4,6},{6,4},{8,10},{10,8},{12,14},{14,12},{16,18},{18,... | collective-permute-start | bytes 49160 | tf_op jit(solution)/shard_map/ppermute | solution.py:52
  189.7 49.7 %collective-permute-start.36 = (f32[2,2048]{1,0:T(2,128)S(1)}, f32[2,2048]{1,0:T(2,128)S(1)}, u32[]{:S(2)}, u32[]{:S(2)}) collective-permute-start(f32[2,2048]{1,0:T(2,128)S(1)} %pad_maximum_fusion.17), channel_id=1, source_target_pairs={{0,4},{2,6},{4,0},{6,2},{8,12},{10,14},{12,8},{14,10},{16,20},{18,... | collective-permute-start | bytes 49160 | tf_op jit(solution)/shard_map/ppermute | solution.py:52
  191.2 48.3 %collective-permute-start.37 = (f32[2,2048]{1,0:T(2,128)S(1)}, f32[2,2048]{1,0:T(2,128)S(1)}, u32[]{:S(2)}, u32[]{:S(2)}) collective-permute-start(f32[2,2048]{1,0:T(2,128)S(1)} %pad_maximum_fusion.17), channel_id=1, source_target_pairs={{0,6},{2,4},{4,2},{6,0},{8,14},{10,12},{12,10},{14,8},{16,22},{18,... | collective-permute-start | bytes 49160 | tf_op jit(solution)/shard_map/ppermute | solution.py:52
  239.5 39.0 %collective-permute-start.38 = (f32[2,2048]{1,0:T(2,128)S(1)}, f32[2,2048]{1,0:T(2,128)}, u32[]{:S(2)}, u32[]{:S(2)}) collective-permute-start(f32[2,2048]{1,0:T(2,128)S(1)} %add_add_fusion.5), channel_id=1, source_target_pairs={{0,8},{2,10},{4,12},{6,14},{8,0},{10,2},{12,4},{14,6},{16,24},{18,... | collective-permute-start | bytes 49160 | tf_op jit(solution)/shard_map/ppermute | solution.py:52
  239.6 38.9 %collective-permute-start.39 = (f32[2,2048]{1,0:T(2,128)S(1)}, f32[2,2048]{1,0:T(2,128)}, u32[]{:S(2)}, u32[]{:S(2)}) collective-permute-start(f32[2,2048]{1,0:T(2,128)S(1)} %add_add_fusion.5), channel_id=1, source_target_pairs={{0,16},{2,18},{4,20},{6,22},{8,24},{10,26},{12,28},{14,30},{16,0},... | collective-permute-start | bytes 49160 | tf_op jit(solution)/shard_map/ppermute | solution.py:52
  239.6 38.8 %collective-permute-start.40 = (f32[2,2048]{1,0:T(2,128)S(1)}, f32[2,2048]{1,0:T(2,128)}, u32[]{:S(2)}, u32[]{:S(2)}) collective-permute-start(f32[2,2048]{1,0:T(2,128)S(1)} %add_add_fusion.5), channel_id=1, source_target_pairs={{0,24},{2,26},{4,28},{6,30},{8,16},{10,18},{12,20},{14,22},{16,8},... | collective-permute-start | bytes 49160 | tf_op jit(solution)/shard_map/ppermute | solution.py:52
  289.9 272.7 %all-gather.7.cloned.1.call-start = ((), (), s32[]{:S(2)}) async-start(), calls=%async_computation.2 | async-start | bytes 4456448 | tf_op jit(solution)/shard_map/all_gather | solution.py:342
  291.6 275.7 %all-gather.9.cloned.1.call-start = ((), (), s32[]{:S(2)}) async-start(), calls=%async_computation.3 | async-start | bytes 2367488 | tf_op jit(solution)/shard_map/all_gather | solution.py:345
  413.9 104.0 %collective-permute-start.84 = (f32[3000,128]{1,0:T(8,128)}, f32[3000,128]{1,0:T(8,128)}, u32[]{:S(2)}, u32[]{:S(2)}) collective-permute-start(f32[3000,128]{1,0:T(8,128)} %fusion.83), channel_id=1, source_target_pairs={{0,1},{1,0},{2,3},{3,2},{4,5},{5,4},{6,7},{7,6},{8,9},{9,8},{10,11... | collective-permute-start | bytes 4608008 | tf_op jit(solution)/shard_map/ppermute | solution.py:48
  453.7 53.6 %collective-permute-start.77 = (bf16[16,16,2048]{2,1,0:T(8,128)(2,1)}, bf16[16,16,2048]{2,1,0:T(8,128)(2,1)}, u32[]{:S(2)}, u32[]{:S(2)}) collective-permute-start(bf16[16,16,2048]{2,1,0:T(8,128)(2,1)} %slice.429), channel_id=1, source_target_pairs={{0,1},{1,0},{2,3},{3,2},{4,5},{5,4},{6,7},{7,6},{8,9},{9,8},{10,11... | collective-permute-start | bytes 3145736 | tf_op jit(solution)/shard_map/ppermute | solution.py:48
  483.9 37.2 %collective-permute-start.72 = (bf16[16,144,512]{2,1,0:T(8,128)(2,1)}, bf16[16,144,512]{2,1,0:T(8,128)(2,1)}, u32[]{:S(2)}, u32[]{:S(2)}) collective-permute-start(bf16[16,144,512]{2,1,0:T(8,128)(2,1)} %slice.419), channel_id=1, source_target_pairs={{0,1},{1,0},{2,3},{3,2},{4,5},{5,4},{6,7},{7,6},{8,9},{9,8},{10,11... | collective-permute-start | bytes 7077896 | tf_op jit(solution)/shard_map/ppermute | solution.py:48
  523.8 21.0 %collective-permute-start.73 = (bf16[8,144,512]{2,1,0:T(8,128)(2,1)S(1)}, bf16[8,144,512]{2,1,0:T(8,128)(2,1)S(1)}, u32[]{:S(2)}, u32[]{:S(2)}) collective-permute-start(bf16[8,144,512]{2,1,0:T(8,128)(2,1)S(1)} %slice.553), channel_id=1, source_target_pairs={{0,4},{1,3},{2,6},{3,1},{4,0},{5,7},{6,2},{7,5},{8,12},{9,11},{10,... | collective-permute-start | bytes 3538952 | tf_op jit(solution)/shard_map/ppermute | solution.py:57
  (153 other events, 1322.0 us)
Sparse Core Ops, SparseCore 0:
  10.9 102.4 all-gather.4
  294.0 83.8 all-gather.6
  441.0 63.2 all-gather.8

commit v2 on v1

--- a/solution.py
+++ b/solution.py
@@ -21,6 +21,8 @@
 HIGH = lax.Precision.HIGHEST
 BOTH = ("dp", "shard")
 GATHERED_CODES_BYTES = 32 * 2**20
+MIB = 2**20
+LANES = 512
 
 
 def product(left, right):
@@ -144,6 +146,10 @@
     return scatter_relative(reorder(blocks, slots, True), size)
 
 
+def spread_dp(values, size):
+    return lax.all_to_all(jnp.broadcast_to(values[None], (size,) + values.shape), "dp", 0, 0)
+
+
 def norm_forward(hidden, gain_row, shift_row, row_total, size):
     totals = sum_over_dp(jnp.stack([jnp.sum(hidden, 0), jnp.sum(hidden * hidden, 0)]), size)
     average = totals[0] / row_total
@@ -190,6 +196,191 @@
     return summed[:, 1 : side_len + 1, 1 : side_len + 1, :].reshape(
         canvas_count * side_len * side_len, channels
     )
+
+
+def kernel_call(body, outs, args, smem=0, scratch=(), flops=0, transcendentals=0, limit=32):
+    size_of = lambda a: a.size * a.dtype.itemsize
+    result = pl.pallas_call(
+        body,
+        out_shape=[jax.ShapeDtypeStruct(shape, dtype) for shape, dtype in outs],
+        in_specs=[
+            pl.BlockSpec(memory_space=pltpu.SMEM if i < smem else pltpu.VMEM)
+            for i in range(len(args))
+        ],
+        out_specs=[pl.BlockSpec(memory_space=pltpu.VMEM) for _ in outs],
+        scratch_shapes=list(scratch),
+        compiler_params=pltpu.CompilerParams(vmem_limit_bytes=limit * MIB),
+        cost_estimate=pl.CostEstimate(
+            flops=int(flops),
+            bytes_accessed=int(sum(size_of(a) for a in args)),
+            transcendentals=int(transcendentals),
+        ),
+    )(*args)
+    return result
+
+
+def add_columns(total_ref, columns, values):
+    rows, width = values.shape
+    total_ref[:, columns] += jnp.sum(values.reshape(rows // 8, 8, width), 0)
+
+
+def codes_kernel(
+    crops,
+    first_row,
+    units_ref,
+    partner_ref,
+    proto_ref,
+    loss_ref,
+    proto_grad_ref,
+    unit_grad_ref,
+    codes_ref,
+    heat_ref,
+    score_ref,
+    total_ref,
+    scale_ref,
+    inverse_ref,
+    *,
+    factor,
+):
+    rows_all, width = codes_ref.shape
+    own = unit_grad_ref.shape[0]
+    chunks = [slice(k, k + LANES) for k in range(0, width, LANES)]
+    lane = lax.broadcasted_iota(jnp.int32, (1, width), 1)
+    real = lane < PROTOS
+
+    def scores(rows, columns):
+        return lax.dot_general(
+            units_ref[rows, :],
+            proto_ref[columns, :],
+            (((1,), (1,)), ((), ())),
+            preferred_element_type=jnp.float32,
+        )
+
+    def keep(values, columns):
+        if columns.stop <= PROTOS:
+            return values
+        lanes = columns.start + lax.broadcasted_iota(jnp.int32, values.shape, 1)
+        return jnp.where(lanes < PROTOS, values, 0.0)
+
+    def fold(values):
+        return sum(values[:, k : k + 128] for k in range(0, values.shape[1], 128))
+
+    total_ref[...] = jnp.zeros_like(total_ref)
+
+    def first(i, carry):
+        rows = pl.ds(pl.multiple_of(i * 128, 128), 128)
+        for columns in chunks:
+            powers = keep(jnp.exp(scores(rows, columns) * (1.0 / SINK_EPS)), columns)
+            codes_ref[rows, columns] = powers
+            add_columns(total_ref, columns, powers)
+        return carry
+
+    lax.fori_loop(0, rows_all // 128, first, 0)
+
+    def column_factors(turn):
+        total = jnp.sum(total_ref[...], 0, keepdims=True)
+        total = jnp.where(real, total, 1.0)
+        if turn == 0:
+            scale = jnp.where(total > 1e30, 2.0**-64, 1.0)
+            scale_ref[...] = jnp.broadcast_to(scale, scale_ref.shape)
+            total = total * scale
+        inverse_ref[...] = jnp.broadcast_to(1.0 / total, inverse_ref.shape)
+
+    def divided(turn, rows, columns):
+        values = codes_ref[rows, columns]
+        if turn == 0:
+            values = values * scale_ref[0:1, columns]
+        return values * inverse_ref[0:1, columns]
+
+    def row_inverse(turn, rows):
+        part = sum(fold(divided(turn, rows, columns)) for columns in chunks)
+        return 1.0 / jnp.sum(part, 1, keepdims=True)
+
+    for turn in range(SINK_ITERS - 1):
+        column_factors(turn)
+        total_ref[...] = jnp.zeros_like(total_ref)
+
+        def both(i, carry):
+            rows = pl.ds(pl.multiple_of(i * 64, 64), 64)
+            inverse = row_inverse(turn, rows)
+            for columns in chunks:
+                values = divided(turn, rows, columns) * inverse
+                codes_ref[rows, columns] = values
+                add_columns(total_ref, columns, values)
+            return carry
+
+        lax.fori_loop(0, rows_all // 64, both, 0)
+
+    column_factors(SINK_ITERS - 1)
+    proto_grad_ref[...] = jnp.zeros_like(proto_grad_ref)
+    loss_ref[...] = jnp.zeros_like(loss_ref)
+    block = 128
+
+    def last(i, carry):
+        rows = pl.ds(pl.multiple_of(i * block, block), block)
+        inverse = row_inverse(SINK_ITERS - 1, rows)
+        row = lax.broadcasted_iota(jnp.int32, (block, block), 0)
+        column = lax.broadcasted_iota(jnp.int32, (block, block), 1)
+        pick = (column == (row // CROPS) * CROPS + partner_ref[rows, :]).astype(jnp.bfloat16)
+        heat_part = jnp.zeros((block, 128), jnp.float32)
+        target_part = jnp.zeros((block, 128), jnp.float32)
+        loss_part = jnp.zeros((block, 128), jnp.float32)
+        for columns in chunks:
+            score = scores(rows, columns)
+            heat = keep(jnp.exp(score * (1.0 / SOFTMAX_HEAT)), columns)
+            heat_ref[:, columns] = heat
+            heat_part += fold(heat)
+            codes = divided(SINK_ITERS - 1, rows, columns) * inverse
+            high = codes.astype(jnp.bfloat16)
+            rest = (codes - high.astype(jnp.float32)).astype(jnp.bfloat16)
+            target = product(pick, high) + product(pick, rest)
+            codes_ref[rows, columns] = target
+            target_part += fold(target)
+            loss_part += fold(target * score)
+        heat_sum = jnp.sum(heat_part, 1, keepdims=True)
+        target_sum = jnp.sum(target_part, 1, keepdims=True)
+        row_loss = (
+            target_sum * jnp.log(heat_sum)
+            - jnp.sum(loss_part, 1, keepdims=True) * (1.0 / SOFTMAX_HEAT)
+        )
+        loss_ref[...] += jnp.broadcast_to(jnp.sum(row_loss, 0, keepdims=True), loss_ref.shape)
+        ratio = target_sum / heat_sum * factor
+        for columns in chunks:
+            grad = heat_ref[:, columns] * ratio - codes_ref[rows, columns] * factor
+            low = grad.astype(jnp.bfloat16)
+            score_ref[rows, columns] = low
+            proto_grad_ref[:, columns] += product_t(units_ref[rows, :], low)
+        return carry
+
+    lax.fori_loop(0, crops // block, last, 0)
+    mine = pl.ds(pl.multiple_of(first_row[0], own), own)
+    unit_grad_ref[...] = product(score_ref[mine, :], proto_ref[...])
+
+
+def gathered_loss(units, queue, partner, prototypes, first_row, own, loss_factor_weight):
+    crops, dim = units.shape
+    width = -(-PROTOS // LANES) * LANES
+    rows_all = crops + queue.shape[0]
+    padded = jnp.pad(prototypes, ((0, width - PROTOS), (0, 0)))
+    f32, bf16 = jnp.float32, jnp.bfloat16
+    loss, proto_grad, unit_grad = kernel_call(
+        lambda *refs: codes_kernel(crops, *refs, factor=loss_factor_weight / SOFTMAX_HEAT),
+        [((8, 128), f32), ((dim, width), f32), ((own, dim), f32)],
+        [first_row, jnp.concatenate([units, queue], 0), partner, padded],
+        smem=1,
+        scratch=[
+            pltpu.VMEM((rows_all, width), f32),
+            pltpu.VMEM((128, width), f32),
+            pltpu.VMEM((crops, width), bf16),
+            pltpu.VMEM((8, width), f32),
+            pltpu.VMEM((8, width), f32),
+            pltpu.VMEM((8, width), f32),
+        ],
+        flops=2 * width * (rows_all * dim + 6 * crops * dim),
+        transcendentals=width * (rows_all + crops),
+        limit=40,
+    )
+    return loss[0, 0], proto_grad.T[:PROTOS], unit_grad
 
 
 def sinkhorn(batch_codes, stored_codes, total):
@@ -263,14 +454,17 @@
     crop_sizes = jnp.sum(onehot, 2)
 
     gathered_codes = crop_count * PROTOS * 4 <= GATHERED_CODES_BYTES
+    chip_queue = jnp.concatenate([queue, swap_cores(queue)], 0)
     if gathered_codes:
-        all_queue = lax.all_gather(queue, BOTH, axis=0, tiled=True)
-        all_partner = lax.all_gather(partner, "dp", axis=0, tiled=True)
-    else:
-        all_queue = jnp.concatenate([queue, swap_cores(queue)], 0)
-        all_partner = partner
-    queue_codes = jnp.exp(product_bt(all_queue, prototypes) / SINK_EPS)
-    pick = (all_partner[:, :, None] == crop_ids[None, None, :]).astype(jnp.float32)
+        width = queue.shape[1]
+        partner_rows = -(-local_crops // width)
+        packed = jnp.pad(
+            partner.astype(jnp.bfloat16).reshape(-1), (0, partner_rows * width - local_crops)
+        ).reshape(partner_rows, width)
+        packed = spread_dp(jnp.concatenate([chip_queue, packed], 0), size)
+        all_queue = packed[:, : chip_queue.shape[0]].reshape(-1, width)
+        all_partner = packed[:, chip_queue.shape[0] :].reshape(size, -1)[:, :local_crops]
+        all_partner = all_partner.astype(jnp.int32).reshape(crop_count, 1)
 
     pre_one = product(input_rows, full_reduce)
     norm_one, unit_one, inv_one = norm_forward(
@@ -307,22 +501,27 @@
     unit_low = unit_embed.astype(jnp.bfloat16)
 
     if gathered_codes:
-        spread = jnp.broadcast_to(unit_low[None], (size,) + unit_low.shape)
-        all_units = lax.all_to_all(spread, "dp", 0, 0).reshape(crop_count, -1)
-        scores = product_bt(all_units, prototypes)
-        codes = sinkhorn(jnp.exp(scores / SINK_EPS), queue_codes, lambda sums: sums)
-        loss_part, score_low = swapped_loss(scores, codes, pick, loss_factor_weight)
-        proto_part = product_t(score_low, all_units)
-        score_low = lax.dynamic_slice_in_dim(score_low, me_dp * local_crops, local_crops, 0)
+        all_units = spread_dp(unit_low, size).reshape(crop_count, -1)
+        loss_part, proto_part, unit_grad = gathered_loss(
+            all_units,
+            all_queue,
+            all_partner,
+            prototypes,
+            (me_dp * local_crops).astype(jnp.int32).reshape(1),
+            local_crops,
+            loss_factor_weight,
+        )
     else:
+        queue_codes = jnp.exp(product_bt(chip_queue, prototypes) / SINK_EPS)
+        pick = (partner[:, :, None] == crop_ids[None, None, :]).astype(jnp.float32)
         scores = product_bt(unit_low, prototypes)
         codes = sinkhorn(
             jnp.exp(scores / SINK_EPS), queue_codes, lambda sums: sum_over_dp(sums, size)
         )
         loss_part, score_low = swapped_loss(scores, codes, pick, loss_factor_weight)
         proto_part, loss_part = lax.psum((product_t(score_low, unit_low), loss_part), "dp")
+        unit_grad = product(score_low, prototypes)
     proto_grad = proto_part + swap_cores(proto_part)
-    unit_grad = product(score_low, prototypes)
     embed_grad = inv_length * (
         unit_grad - unit_embed * jnp.sum(unit_grad * unit_embed, 1, keepdims=True)
     )

time: 591 us -> 475 us (0.80)
  blocking collectives: 77.7 us -> 0 us
  matrix products: 64.6 us -> 38.6 us
  other arithmetic: 74.8 us -> 49.3 us
  local copies, waits for them, and re-layouts: 142 us -> 123 us
  starting transfers between devices: 108 us -> 127 us
  Pallas kernels: 8.55 us -> 26.3 us
    all_gather x2 -> x0, blocking collectives: 77.7 us -> none  [the longest x1 47.6 us: per_device(): all_queue = lax.all_gather(queue, BOTH, axis=0, tiled=True)]
    reshape x3, local copies, waits for them, and re-layouts: 22.3 us -> 0.35 us  [the longest x1 0.26 us: per_device(): all_partner = all_partner.astype(jnp.int32).reshape(crop_count, 1)]
    reduce_sum x6 -> x1, other arithmetic: 19.5 us -> 0.18 us  [per_device(): jnp.sum(unit_grad * unit_embed, 1, keepdims=True)]
    pallas_call x0 -> x1, Pallas kernels: none -> 17.8 us  [kernel_call(): pl.pallas_call(body, out_shape=[jax.ShapeDtypeStruct(shape, dtype) for sh...]
    all_to_all x1 -> x2, starting transfers between devices: 4.17 us -> 18.8 us  [spread_dp(): lax.all_to_all(jnp.broadcast_to(values[None], (size,) + values.shape), 'd...]
    dot_general x7 -> x5, matrix products: 21.1 us -> 9.48 us  [product_bt(): lax.dot_general(left, right, (((1,), (1,)), ((), ())), preferred_element_...]
    dot_general x1 -> x0, matrix products: 11.3 us -> none  [swapped_loss(): jnp.einsum('cab,cbk->cak', pick, codes.reshape(rows // CROPS, CROPS, PROT...]
    ppermute x24, starting transfers between devices: 24.1 us -> 33.2 us  [flip_both(): return lax.ppermute(values, BOTH, pairs)]
  transfers between devices with their start and end apart: 89 -> 91, of which waited for: 26 -> 29; matrix products, arithmetic and copies ran while one was open for 44% -> 41% of each run, Pallas kernels for 1% -> 6%
where the time goes in v2:
time: 475 us; the launch traced here: 468 us
  starting transfers between devices  127 us (27%)
  local copies, waits for them, and re-layouts  123 us (26%)
  waiting for transfers between devices  86.4 us (18%)
  other arithmetic  49.3 us (10%)
  matrix products  38.6 us (8%)
  Pallas kernels  26.3 us (6%)
  between operations  17.7 us (4%)
    ppermute x24, waiting for transfers between devices, flip_both(): return lax.ppermute(values, BOTH, pairs)  65.9 us
    ppermute x48, starting transfers between devices, flip_dp(): return lax.ppermute(values, 'dp', [(i, i ^ bits) for i in range(size)])  47.4 us
    ppermute x24, starting transfers between devices, flip_both(): return lax.ppermute(values, BOTH, pairs)  33.2 us
    unnamed x216, local copies, waits for them, and re-layouts  32.5 us
    ppermute x14, starting transfers between devices, swap_cores(): return lax.ppermute(values, 'shard', [(0, 1), (1, 0)])  27.3 us
    all_to_all x2, starting transfers between devices, spread_dp(): lax.all_to_all(jnp.broadcast_to(values[None], (size,) + values.shape), 'd...  18.8 us
    pallas_call x1, Pallas kernels, kernel_call(): pl.pallas_call(body, out_shape=[jax.ShapeDtypeStruct(shape, dtype) for sh...  17.8 us
    ppermute x48, waiting for transfers between devices, flip_dp(): return lax.ppermute(values, 'dp', [(i, i ^ bits) for i in range(size)])  15.1 us
  transfers between devices with their start and end apart: 91, of which 29 were waited for; matrix products, arithmetic and copies ran while one was open for 41% of the time, Pallas kernels for 6%

profile of v2, /device:TPU:1, one launch (start us, length us, event | category | flops | bytes accessed | tf_op | source)
XLA Modules:
  0.0 468.2 jit_solution(7006984074977870255)
XLA Ops:
  13.1 3.7 collective-permute-start.23
  23.4 5.2 %collective-permute-start.2 = (bf16[2,64,512]{2,1,0:T(8,128)(2,1)S(1)}, bf16[2,64,512]{2,1,0:T(8,128)(2,1)S(1)}, u32[]{:S(2)}, u32[]{:S(2)}) collective-permute-start(bf16[2,64,512]{2,1,0:T(8,128)(2,1)S(1)} %pad_maximum_fusion.13), channel_id=1, source_target_pairs={{0,8},{1,9},{2,10},{3,11},{4,12},{5,13},{6,14},{7,15},{8,0},{9,1},... | collective-permute-start | bytes 393224 | tf_op jit(solution)/shard_map/ppermute | solution.py:59
  29.9 3.3 collective-permute-done.12
  48.9 17.1 %collective-permute-done.4 = bf16[8,64,512]{2,1,0:T(8,128)(2,1)S(1)} collective-permute-done((bf16[8,64,512]{2,1,0:T(8,128)(2,1)S(1)}, bf16[8,64,512]{2,1,0:T(8,128)(2,1)S(1)}, u32[]{:S(2)}, u32[]{:S(2)}) %collective-permute-start.4) | collective-permute-done | bytes 524320 | tf_op jit(solution)/shard_map/ppermute | solution.py:59
  88.7 17.3 %collective-permute-done.15 = bf16[8,144,512]{2,1,0:T(8,128)(2,1)} collective-permute-done((bf16[8,144,512]{2,1,0:T(8,128)(2,1)}, bf16[8,144,512]{2,1,0:T(8,128)(2,1)}, u32[]{:S(2)}, u32[]{:S(2)}) %collective-permute-start.15) | collective-permute-done | bytes 1179680 | tf_op jit(solution)/shard_map/ppermute | solution.py:59
  121.1 4.6 pad_slice_fusion
  144.7 4.2 constant_dynamic-update-slice_fusion.25.refs_1_
  178.8 14.1 %all-to-all-start.1 = ((bf16[16,33,128]{2,1,0:T(8,128)(2,1)}), bf16[16,33,128]{2,1,0:T(8,128)(2,1)}, u32[]{:S(2)}, u32[]{:S(2)}) async-start(bf16[16,33,128]{2,1,0:T(8,128)(2,1)} %broadcast_in_dim.28), calls=%async_computation.1 | async-start | bytes 327680 | tf_op jit(solution)/shard_map/all_to_all | solution.py:150
  193.7 4.0 fusion.4
  203.4 5.0 %fusion.56 = (f32[2048]{0:T(1024)S(1)}, f32[2048]{0:T(1024)S(1)}, f32[32,2048]{1,0:T(8,128)S(1)}) fusion(bf16[32,2048]{1,0:T(8,128)(2,1)S(1)} %convert_element_type.138, bf16[2048,2176]{1,0:T(8,128)(2,1)} %all-gather.4.cloned.1.call-done), kind=kOutput, calls=%fused_computation.287 | convolution fusion | flops 268627968 | bytes 8798208 | tf_op jit(solution)/shard_map/dot_general | solution.py:29
  224.9 4.7 %all-to-all-start = ((bf16[16,32,128]{2,1,0:T(8,128)(2,1)}), bf16[16,32,128]{2,1,0:T(8,128)(2,1)}, u32[]{:S(2)}, u32[]{:S(2)}) async-start(bf16[16,32,128]{2,1,0:T(8,128)(2,1)} %broadcast_in_dim.27), calls=%async_computation | async-start | bytes 262144 | tf_op jit(solution)/shard_map/all_to_all | solution.py:150
  231.4 4.9 %all-to-all-done = bf16[16,32,128]{2,1,0:T(8,128)(2,1)} async-done(((bf16[16,32,128]{2,1,0:T(8,128)(2,1)}), bf16[16,32,128]{2,1,0:T(8,128)(2,1)}, u32[]{:S(2)}, u32[]{:S(2)}) %all-to-all-start) | async-done | bytes 131104 | tf_op jit(solution)/shard_map/all_to_all | solution.py:150
  237.4 17.8 %shard_map.215 = (f32[8,128]{1,0:T(8,128)S(1)}, f32[128,3072]{1,0:T(8,128)S(1)}, f32[32,128]{1,0:T(8,128)S(1)}) custom-call(s32[1]{0:T(128)} %bitcast.37.refs_0_, bf16[1024,128]{1,0:T(8,128)(2,1)S(1)} %pad_maximum_fusion.10.refs_1_, s32[512,1]{1,0:T(8,128)S(1)} %reshape.155.refs_2_, bf16[3072,128]{1,0:T(8,128)(2,1)S(1)} %pad.54.refs_3_), custom_call_target="tpu_custom_call" | custom-call | flops 3221225472 | bytes 1050628 | tf_op jit(solution)/shard_map/pallas_call | solution.py:203
  277.4 5.3 %fusion.49 = (f32[2048]{0:T(1024)S(1)}, f32[2048]{0:T(1024)S(1)}, f32[288,2048]{1,0:T(8,128)}) fusion(f32[2048]{0:T(1024)S(1)} %bitcast.195, f32[288,2048]{1,0:T(8,128)} %get-tuple-element.178, f32[2048]{0:T(1024)S(1)} %bitcast.198, f32[288,2048]{1,0:T(8,128)} %reshape.142, bf16[288,2048]{1,0:T(8,128)(2,1)S(1)} %copy-done.15, f32[2048]{0:T(1024)S(1)} %bitcast.213, ...), kind=kLoop, calls=%fused_computation.280 | loop fusion | flops 10022912 | bytes 8306688 | tf_op jit(solution)/shard_map/reduce_sum | solution.py:162
  287.0 5.0 %copy.96 = bf16[4608,288]{1,0:T(8,128)(2,1)} copy(bf16[4608,288]{0,1:T(8,128)(2,1)} %bitcast.177) | data formatting | bytes 5308416 | tf_op jit(solution)/shard_map/dot_general | solution.py:33
  295.6 14.1 %collective-permute-start.85 = (f32[3000,128]{1,0:T(8,128)}, f32[3000,128]{1,0:T(8,128)}, u32[]{:S(2)}, u32[]{:S(2)}) collective-permute-start(f32[3000,128]{1,0:T(8,128)} %copy.97), channel_id=1, source_target_pairs={{0,1},{1,0},{2,3},{3,2},{4,5},{5,4},{6,7},{7,6},{8,9},{9,8},{10,11... | collective-permute-start | bytes 4608008 | tf_op jit(solution)/shard_map/ppermute | solution.py:50
  329.6 4.5 fusion.47
  334.5 4.0 fusion.17
  349.6 4.9 %collective-permute-start.78 = (bf16[16,16,2048]{2,1,0:T(8,128)(2,1)}, bf16[16,16,2048]{2,1,0:T(8,128)(2,1)}, u32[]{:S(2)}, u32[]{:S(2)}) collective-permute-start(bf16[16,16,2048]{2,1,0:T(8,128)(2,1)} %slice.453), channel_id=1, source_target_pairs={{0,1},{1,0},{2,3},{3,2},{4,5},{5,4},{6,7},{7,6},{8,9},{9,8},{10,11... | collective-permute-start | bytes 3145736 | tf_op jit(solution)/shard_map/ppermute | solution.py:50
  411.8 5.5 %collective-permute-done.80 = bf16[4,16,2048]{2,1,0:T(8,128)(2,1)S(1)} collective-permute-done((bf16[4,16,2048]{2,1,0:T(8,128)(2,1)S(1)}, bf16[4,16,2048]{2,1,0:T(8,128)(2,1)S(1)}, u32[]{:S(2)}, u32[]{:S(2)}) %collective-permute-start.80) | collective-permute-done | bytes 262176 | tf_op jit(solution)/shard_map/ppermute | solution.py:59
  419.2 3.7 collective-permute-done.70
  430.6 6.4 %collective-permute-done.75 = bf16[4,144,512]{2,1,0:T(8,128)(2,1)S(1)} collective-permute-done((bf16[4,144,512]{2,1,0:T(8,128)(2,1)S(1)}, bf16[4,144,512]{2,1,0:T(8,128)(2,1)S(1)}, u32[]{:S(2)}, u32[]{:S(2)}) %collective-permute-start.75) | collective-permute-done | bytes 589856 | tf_op jit(solution)/shard_map/ppermute | solution.py:59
  445.1 4.9 %fusion.57 = (bf16[512,2048]{1,0:T(8,128)(2,1)}, bf16[512,2048]{1,0:T(8,128)(2,1)}) fusion(bf16[512,4096]{1,0:T(8,128)(2,1)} %all-gather.6.cloned.1.call-done), kind=kLoop, calls=%fused_computation.288 | loop fusion | bytes 8388608 | tf_op jit(solution)/shard_map/slice | solution.py:551
  452.2 4.2 collective-permute-start.83
  (566 shorter events, 282.0 us)
Async XLA Ops:
  7.2 196.2 %all-gather.4.cloned.1.call-start = ((), (), s32[]{:S(2)}) async-start(), calls=%async_computation.2 | async-start | bytes 9191424 | tf_op jit(solution)/shard_map/all_gather | solution.py:445
  9.9 168.2 %collective-permute-start.41 = (bf16[16,128]{1,0:T(8,128)(2,1)}, bf16[16,128]{1,0:T(8,128)(2,1)S(1)}, u32[]{:S(2)}, u32[]{:S(2)}) collective-permute-start(bf16[16,128]{1,0:T(8,128)(2,1)} %param.16), channel_id=1, source_target_pairs={{0,1},{1,0},{2,3},{3,2},{4,5},{5,4},{6,7},{7,6},{8,9},{9,8},{10,11... | collective-permute-start | bytes 12296 | tf_op jit(solution)/shard_map/ppermute | solution.py:50
  13.0 59.2 %collective-permute-start = (bf16[4,6,6,2048]{3,0,2,1:T(4,128)(2,1)}, bf16[4,6,6,2048]{3,0,2,1:T(4,128)(2,1)}, u32[]{:S(2)}, u32[]{:S(2)}) collective-permute-start(bf16[4,6,6,2048]{3,0,2,1:T(4,128)(2,1)} %get-tuple-element.105), channel_id=1, source_target_pairs={{0,1},{1,0},{2,3},{3,2},{4,5},{5,4},{6,7},{7,6},{8,9},{9,8},{10,11... | collective-permute-start | bytes 1769480 | tf_op jit(solution)/shard_map/ppermute | solution.py:50
  40.6 27.2 %collective-permute-start.25 = (bf16[4,16,2048]{2,1,0:T(8,128)(2,1)S(1)}, bf16[4,16,2048]{2,1,0:T(8,128)(2,1)S(1)}, u32[]{:S(2)}, u32[]{:S(2)}) collective-permute-start(bf16[4,16,2048]{2,1,0:T(8,128)(2,1)S(1)} %pad_maximum_fusion.9), channel_id=1, source_target_pairs={{0,2},{1,5},{2,0},{3,7},{4,6},{5,1},{6,4},{7,3},{8,10},{9,13},{10,... | collective-permute-start | bytes 786440 | tf_op jit(solution)/shard_map/ppermute | solution.py:59
  44.1 22.0 %collective-permute-start.4 = (bf16[8,64,512]{2,1,0:T(8,128)(2,1)S(1)}, bf16[8,64,512]{2,1,0:T(8,128)(2,1)S(1)}, u32[]{:S(2)}, u32[]{:S(2)}) collective-permute-start(bf16[8,64,512]{2,1,0:T(8,128)(2,1)S(1)} %pad_maximum_fusion.4), channel_id=1, source_target_pairs={{0,4},{1,3},{2,6},{3,1},{4,0},{5,7},{6,2},{7,5},{8,12},{9,11},{10,... | collective-permute-start | bytes 1572872 | tf_op jit(solution)/shard_map/ppermute | solution.py:59
  46.9 22.3 %collective-permute-start.14 = (bf16[4,144,512]{2,1,0:T(8,128)(2,1)S(1)}, bf16[4,144,512]{2,1,0:T(8,128)(2,1)S(1)}, u32[]{:S(2)}, u32[]{:S(2)}) collective-permute-start(bf16[4,144,512]{2,1,0:T(8,128)(2,1)S(1)} %pad_maximum_fusion.3), channel_id=1, source_target_pairs={{0,2},{1,5},{2,0},{3,7},{4,6},{5,1},{6,4},{7,3},{8,10},{9,13},{10,... | collective-permute-start | bytes 1769480 | tf_op jit(solution)/shard_map/ppermute | solution.py:59
  68.7 46.1 %collective-permute-start.26 = (bf16[8,16,2048]{2,1,0:T(8,128)(2,1)}, bf16[8,16,2048]{2,1,0:T(8,128)(2,1)}, u32[]{:S(2)}, u32[]{:S(2)}) collective-permute-start(bf16[8,16,2048]{2,1,0:T(8,128)(2,1)} %pad_maximum_fusion.5), channel_id=1, source_target_pairs={{0,4},{1,3},{2,6},{3,1},{4,0},{5,7},{6,2},{7,5},{8,12},{9,11},{10,... | collective-permute-start | bytes 1572872 | tf_op jit(solution)/shard_map/ppermute | solution.py:59
  70.4 35.6 %collective-permute-start.15 = (bf16[8,144,512]{2,1,0:T(8,128)(2,1)}, bf16[8,144,512]{2,1,0:T(8,128)(2,1)}, u32[]{:S(2)}, u32[]{:S(2)}) collective-permute-start(bf16[8,144,512]{2,1,0:T(8,128)(2,1)} %pad_maximum_fusion.2), channel_id=1, source_target_pairs={{0,4},{1,3},{2,6},{3,1},{4,0},{5,7},{6,2},{7,5},{8,12},{9,11},{10,... | collective-permute-start | bytes 3538952 | tf_op jit(solution)/shard_map/ppermute | solution.py:59
  87.0 22.5 %collective-permute-start.7 = (f32[2,512]{1,0:T(2,128)S(1)}, f32[2,512]{1,0:T(2,128)S(1)}, u32[]{:S(2)}, u32[]{:S(2)}) collective-permute-start(f32[2,512]{1,0:T(2,128)S(1)} %pad_maximum_fusion.21), channel_id=1, source_target_pairs={{0,4},{2,6},{4,0},{6,2},{8,12},{10,14},{12,8},{14,10},{16,20},{18,... | collective-permute-start | bytes 12296 | tf_op jit(solution)/shard_map/ppermute | solution.py:54
  88.3 22.7 %collective-permute-start.8 = (f32[2,512]{1,0:T(2,128)S(1)}, f32[2,512]{1,0:T(2,128)S(1)}, u32[]{:S(2)}, u32[]{:S(2)}) collective-permute-start(f32[2,512]{1,0:T(2,128)S(1)} %pad_maximum_fusion.21), channel_id=1, source_target_pairs={{0,6},{2,4},{4,2},{6,0},{8,14},{10,12},{12,10},{14,8},{16,22},{18,... | collective-permute-start | bytes 12296 | tf_op jit(solution)/shard_map/ppermute | solution.py:54
  109.5 35.2 %collective-permute-start.16 = (bf16[16,144,512]{2,1,0:T(8,128)(2,1)}, bf16[16,144,512]{2,1,0:T(8,128)(2,1)}, u32[]{:S(2)}, u32[]{:S(2)}) collective-permute-start(bf16[16,144,512]{2,1,0:T(8,128)(2,1)} %get-tuple-element.102), channel_id=1, source_target_pairs={{0,1},{1,0},{2,3},{3,2},{4,5},{5,4},{6,7},{7,6},{8,9},{9,8},{10,11... | collective-permute-start | bytes 7077896 | tf_op jit(solution)/shard_map/ppermute | solution.py:50
  117.1 45.1 %collective-permute-start.27 = (bf16[16,16,2048]{2,1,0:T(8,128)(2,1)}, bf16[16,16,2048]{2,1,0:T(8,128)(2,1)}, u32[]{:S(2)}, u32[]{:S(2)}) collective-permute-start(bf16[16,16,2048]{2,1,0:T(8,128)(2,1)} %get-tuple-element.110), channel_id=1, source_target_pairs={{0,1},{1,0},{2,3},{3,2},{4,5},{5,4},{6,7},{7,6},{8,9},{9,8},{10,11... | collective-permute-start | bytes 3145736 | tf_op jit(solution)/shard_map/ppermute | solution.py:50
  178.8 33.5 %all-to-all-start.1 = ((bf16[16,33,128]{2,1,0:T(8,128)(2,1)}), bf16[16,33,128]{2,1,0:T(8,128)(2,1)}, u32[]{:S(2)}, u32[]{:S(2)}) async-start(bf16[16,33,128]{2,1,0:T(8,128)(2,1)} %broadcast_in_dim.28), calls=%async_computation.1 | async-start | bytes 327680 | tf_op jit(solution)/shard_map/all_to_all | solution.py:150
  229.6 215.5 %all-gather.6.cloned.1.call-start = ((), (), s32[]{:S(2)}) async-start(), calls=%async_computation.3 | async-start | bytes 4456448 | tf_op jit(solution)/shard_map/all_gather | solution.py:541
  231.3 218.6 %all-gather.8.cloned.1.call-start = ((), (), s32[]{:S(2)}) async-start(), calls=%async_computation.4 | async-start | bytes 2367488 | tf_op jit(solution)/shard_map/all_gather | solution.py:544
  282.7 27.0 %collective-permute-start.49 = (f32[2,2048]{1,0:T(2,128)S(1)}, f32[2,2048]{1,0:T(2,128)S(1)}, u32[]{:S(2)}, u32[]{:S(2)}) collective-permute-start(f32[2,2048]{1,0:T(2,128)S(1)} %pad_maximum_fusion.19), channel_id=1, source_target_pairs={{0,4},{2,6},{4,0},{6,2},{8,12},{10,14},{12,8},{14,10},{16,20},{18,... | collective-permute-start | bytes 49160 | tf_op jit(solution)/shard_map/ppermute | solution.py:54
  283.3 26.4 %collective-permute-start.50 = (f32[2,2048]{1,0:T(2,128)S(1)}, f32[2,2048]{1,0:T(2,128)S(1)}, u32[]{:S(2)}, u32[]{:S(2)}) collective-permute-start(f32[2,2048]{1,0:T(2,128)S(1)} %pad_maximum_fusion.19), channel_id=1, source_target_pairs={{0,6},{2,4},{4,2},{6,0},{8,14},{10,12},{12,10},{14,8},{16,22},{18,... | collective-permute-start | bytes 49160 | tf_op jit(solution)/shard_map/ppermute | solution.py:54
  284.9 24.8 %collective-permute-start.48 = (f32[2,2048]{1,0:T(2,128)S(1)}, f32[2,2048]{1,0:T(2,128)S(1)}, u32[]{:S(2)}, u32[]{:S(2)}) collective-permute-start(f32[2,2048]{1,0:T(2,128)S(1)} %pad_maximum_fusion.19), channel_id=1, source_target_pairs={{0,2},{2,0},{4,6},{6,4},{8,10},{10,8},{12,14},{14,12},{16,18},{18,... | collective-permute-start | bytes 49160 | tf_op jit(solution)/shard_map/ppermute | solution.py:54
  295.6 98.6 %collective-permute-start.85 = (f32[3000,128]{1,0:T(8,128)}, f32[3000,128]{1,0:T(8,128)}, u32[]{:S(2)}, u32[]{:S(2)}) collective-permute-start(f32[3000,128]{1,0:T(8,128)} %copy.97), channel_id=1, source_target_pairs={{0,1},{1,0},{2,3},{3,2},{4,5},{5,4},{6,7},{7,6},{8,9},{9,8},{10,11... | collective-permute-start | bytes 4608008 | tf_op jit(solution)/shard_map/ppermute | solution.py:50
  349.6 32.3 %collective-permute-start.78 = (bf16[16,16,2048]{2,1,0:T(8,128)(2,1)}, bf16[16,16,2048]{2,1,0:T(8,128)(2,1)}, u32[]{:S(2)}, u32[]{:S(2)}) collective-permute-start(bf16[16,16,2048]{2,1,0:T(8,128)(2,1)} %slice.453), channel_id=1, source_target_pairs={{0,1},{1,0},{2,3},{3,2},{4,5},{5,4},{6,7},{7,6},{8,9},{9,8},{10,11... | collective-permute-start | bytes 3145736 | tf_op jit(solution)/shard_map/ppermute | solution.py:50
  364.8 38.3 %collective-permute-start.73 = (bf16[16,144,512]{2,1,0:T(8,128)(2,1)}, bf16[16,144,512]{2,1,0:T(8,128)(2,1)}, u32[]{:S(2)}, u32[]{:S(2)}) collective-permute-start(bf16[16,144,512]{2,1,0:T(8,128)(2,1)} %slice.443), channel_id=1, source_target_pairs={{0,1},{1,0},{2,3},{3,2},{4,5},{5,4},{6,7},{7,6},{8,9},{9,8},{10,11... | collective-permute-start | bytes 7077896 | tf_op jit(solution)/shard_map/ppermute | solution.py:50
  384.6 22.0 %collective-permute-start.79 = (bf16[8,16,2048]{2,1,0:T(8,128)(2,1)}, bf16[8,16,2048]{2,1,0:T(8,128)(2,1)}, u32[]{:S(2)}, u32[]{:S(2)}) collective-permute-start(bf16[8,16,2048]{2,1,0:T(8,128)(2,1)} %slice.582), channel_id=1, source_target_pairs={{0,4},{1,3},{2,6},{3,1},{4,0},{5,7},{6,2},{7,5},{8,12},{9,11},{10,... | collective-permute-start | bytes 1572872 | tf_op jit(solution)/shard_map/ppermute | solution.py:59
  387.2 21.8 %collective-permute-start.69 = (bf16[8,64,512]{2,1,0:T(8,128)(2,1)}, bf16[8,64,512]{2,1,0:T(8,128)(2,1)}, u32[]{:S(2)}, u32[]{:S(2)}) collective-permute-start(bf16[8,64,512]{2,1,0:T(8,128)(2,1)} %slice.583), channel_id=1, source_target_pairs={{0,4},{1,3},{2,6},{3,1},{4,0},{5,7},{6,2},{7,5},{8,12},{9,11},{10,... | collective-permute-start | bytes 1572872 | tf_op jit(solution)/shard_map/ppermute | solution.py:59
  406.4 21.0 %collective-permute-start.74 = (bf16[8,144,512]{2,1,0:T(8,128)(2,1)S(1)}, bf16[8,144,512]{2,1,0:T(8,128)(2,1)S(1)}, u32[]{:S(2)}, u32[]{:S(2)}) collective-permute-start(bf16[8,144,512]{2,1,0:T(8,128)(2,1)S(1)} %slice.580), channel_id=1, source_target_pairs={{0,4},{1,3},{2,6},{3,1},{4,0},{5,7},{6,2},{7,5},{8,12},{9,11},{10,... | collective-permute-start | bytes 3538952 | tf_op jit(solution)/shard_map/ppermute | solution.py:59
  (163 other events, 1532.9 us)
Sparse Core Ops, SparseCore 0:
  10.9 105.5 all-gather.3
  233.2 86.4 all-gather.5
  325.0 61.5 all-gather.7

commit v3 on v2

v3 whole, which is shorter than its diff:
```python
import dataclasses

import jax
import jax.numpy as jnp
import numpy as np
from jax import lax
from jax.experimental import pallas as pl
from jax.experimental.pallas import tpu as pltpu
from jax.sharding import PartitionSpec as P

D = 2048
MID = 512
PROTOS = 3000
SIDE = 6
CROPS = 4
SINK_ITERS = 3
MICRO = 2


EPS_NORM = 1e-05
EPS_UNIT = 1e-06
SOFTMAX_HEAT = 0.1
SINK_EPS = 0.05
HIGH = lax.Precision.HIGHEST
BOTH = ("dp", "shard")
GATHERED_CODES_BYTES = 32 * 2**20
MIB = 2**20
LANES = 512
CHUNKS = 4


def product(left, right):
    return jnp.dot(left, right, preferred_element_type=jnp.float32)


def product_t(left, right):
    return lax.dot_general(
        left, right, (((0,), (0,)), ((), ())), preferred_element_type=jnp.float32
    )


def product_bt(left, right):
    return lax.dot_general(
        left, right, (((1,), (1,)), ((), ())), preferred_element_type=jnp.float32
    )


def silu_slope(values):
    sigmoid_value = jax.nn.sigmoid(values)
    return sigmoid_value * (1.0 + values * (1.0 - sigmoid_value))


@dataclasses.dataclass
class Scalars:
    array: jax.Array


@dataclasses.dataclass
class Left:
    array: jax.Array


@dataclasses.dataclass
class Loaded:
    array: jax.Array


@dataclasses.dataclass
class Streamed:
    array: jax.Array


class Arriving:
    def __init__(self, ref, copy):
        self.ref, self.copy = ref, copy
        self.shape = ref.shape

    def __getitem__(self, index):
        if self.copy is not None:
            self.copy.wait()
            self.copy = None
        return self.ref[index]


FAR, PUT_FAR = "far", "put far"


def kernel_call(body, outs, args, scratch=(), flops=0, transcendentals=0, limit=17, after=()):
    spaces = {Scalars: pltpu.SMEM, Left: pltpu.HBM, Streamed: pltpu.HBM}
    in_spaces = [spaces.get(type(a), pltpu.VMEM) for a in args] + [pl.ANY] * len(after)
    arrays = []
    for a in args:
        if isinstance(a, (Left, Loaded, Streamed)):
            a = pltpu.with_memory_space_constraint(a.array, pltpu.HBM)
        arrays.append(a.array if isinstance(a, Scalars) else a)
    used = len(arrays)
    out_spaces = [pltpu.HBM if FAR in out else pltpu.VMEM for out in outs]

    streamed = [i for i, a in enumerate(args) if isinstance(a, Streamed)]
    scratch = list(scratch)
    own_scratch = len(scratch)
    for i in streamed:
        scratch += [pltpu.VMEM(arrays[i].shape, arrays[i].dtype), pltpu.SemaphoreType.DMA]

    def kernel(*refs):
        inputs, refs = list(refs[:used]), refs[used + len(after) :]
        mine = len(outs) + own_scratch
        for k, i in enumerate(streamed):
            buffer, sem = refs[mine + 2 * k : mine + 2 * k + 2]
            copy = pltpu.make_async_copy(inputs[i], buffer, sem)
            copy.start()
            inputs[i] = Arriving(buffer, copy)
        body(*inputs, *refs[:mine])

    moved = sum(a.size * a.dtype.itemsize for a in arrays)
    return pl.pallas_call(
        kernel,
        out_shape=[
            jax.ShapeDtypeStruct(*out) if len(out) == 2 else pltpu.HBM(*out[:2]) for out in outs
        ],
        in_specs=[pl.BlockSpec(memory_space=space) for space in in_spaces],
        out_specs=[pl.BlockSpec(memory_space=space) for space in out_spaces],
        scratch_shapes=list(scratch),
        compiler_params=pltpu.CompilerParams(vmem_limit_bytes=limit * MIB),
        cost_estimate=pl.CostEstimate(
            flops=int(flops), bytes_accessed=int(moved), transcendentals=int(transcendentals)
        ),
    )(*arrays, *after)


def join_kernel(counts, *refs):
    outs = refs[sum(counts) :]
    start = 0
    for count, joined in zip(counts, outs):
        parts = refs[start : start + count]
        start += count
        length = parts[0].shape[0]

        def move(i, carry):
            for k, part in enumerate(parts):
                joined[i + k * length] = part[i]
            return carry

        lax.fori_loop(0, length, move, 0)


def join(groups, after=()):
    counts = [len(group) for group in groups]
    outs = [
        ((len(group) * group[0].shape[0],) + group[0].shape[1:], group[0].dtype)
        for group in groups
    ]
    return kernel_call(
        lambda *refs: join_kernel(counts, *refs),
        outs,
        [part for group in groups for part in group],
        after=after,
    )


def hold_kernel(source, target):
    target[...] = source[...]


def hold(values, after=()):
    return kernel_call(hold_kernel, [(values.shape, values.dtype)], [values], after=after)[0]


def add_parts_kernel(parts, *refs):
    ins, outs = refs[: 2 * len(parts)], refs[2 * len(parts) :]
    for k, count in enumerate(parts):
        kept, received = ins[2 * k : 2 * k + 2]
        kept_out, *sent = outs[: count]
        outs = outs[count:]
        length = kept_out.shape[0]

        def move(i, carry):
            kept_out[i] = kept[i].astype(jnp.float32) + received[i].astype(jnp.float32)
            for j, sent_out in enumerate(sent):
                place = i + (j + 1) * length
                total = kept[place].astype(jnp.float32) + received[place].astype(jnp.float32)
                sent_out[i] = total.astype(jnp.bfloat16)
            return carry

        lax.fori_loop(0, length, move, 0)


def add_parts(pairs, parts, after=()):
    outs = []
    for (kept, _), count in zip(pairs, parts):
        shape = (kept.shape[0] // count,) + kept.shape[1:]
        outs += [(shape, jnp.float32, PUT_FAR)] + [(shape, jnp.bfloat16, PUT_FAR)] * (count - 1)
    found = kernel_call(
        lambda *refs: add_parts_kernel(parts, *refs),
        outs,
        [Loaded(array) for pair in pairs for array in pair],
        after=after,
    )
    result = []
    for count in parts:
        result.append((found[0], list(found[1:count])))
        found = found[count:]
    return result


def swap_cores(values):
    return lax.ppermute(values, "shard", [(0, 1), (1, 0)])


def flip_dp(values, bits, size):
    return lax.ppermute(values, "dp", [(i, i ^ bits) for i in range(size)])


def flip_both(values, dp_bits, size):
    pairs = [(2 * i + c, 2 * (i ^ dp_bits[c]) + c) for i in range(size) for c in range(2)]
    return lax.ppermute(values, BOTH, pairs)


def copies_of(size):
    return size if size <= STEPS_DP else 1


def terms_over_dp(copies):
    if copies.shape[0] > 1:
        return lax.all_to_all(copies, "dp", 0, 0)
    return lax.psum(copies, "dp")


Z_BITS = (8, 4, 12)
XY_BITS = ((1, 2), (2, 1))
STEPS_DP = 16


def relative_slots(size):
    me_dp, me_core = lax.axis_index("dp"), lax.axis_index("shard")
    device = jnp.arange(2 * size, dtype=jnp.int32)
    apart_dp, apart_core = (device // 2) ^ me_dp, (device % 2) ^ me_core
    holder = device % 2
    on = lambda bit: jnp.where((apart_dp & bit) != 0, 1, 0)
    low, high = (jnp.where(holder == 0, on(zero), on(one)) for zero, one in XY_BITS)
    slot = on(Z_BITS[0]) + 2 * on(Z_BITS[1]) + 4 * low + 8 * high + size * apart_core
    return slot.astype(jnp.int32)


class Gathering:
    def __init__(self, shard, size):
        self.size = size
        self.held = shard[None]
        self.step = 0

    def send(self):
        step, held = self.step, self.held
        self.step += 1
        if step == 0:
            return [held] + [flip_dp(held, bits, self.size) for bits in Z_BITS]
        return [held, flip_both(held, XY_BITS[step - 1], self.size)]

    def finish(self, slots):
        return Gathered(self.held, swap_cores(self.held), slots)


def gather_step(parts, after=()):
    joined = join([part.send() for part in parts], after)
    for part, held in zip(parts, joined):
        part.held = held


def other_core_dp(held, size):
    device = jnp.arange(2 * size, dtype=jnp.int32)
    other = (device % 2) != lax.axis_index("shard")
    slots = jnp.where(other, size, 0) + device // 2
    return Gathered(held, swap_cores(held), slots.astype(jnp.int32))


class Scattering:
    def __init__(self, kept, sent, size, before):
        self.size = size
        self.kept = kept
        sent, _ = lax.optimization_barrier((sent, before))
        self.received = flip_both(sent, XY_BITS[1], size)
        self.step = 0

    @property
    def parts(self):
        return (2, 4)[self.step]

    def send(self, kept, sent):
        self.kept = kept
        if self.step == 0:
            self.received = flip_both(sent[0], XY_BITS[0], self.size)
        else:
            self.received = [flip_dp(part, bits, self.size) for part, bits in zip(sent, Z_BITS)]
        self.step += 1

    def finish(self):
        one, two, three = (part[0].astype(jnp.float32) for part in self.received)
        return (self.kept[0] + one) + (two + three)


def scatter_step(sums, after=()):
    found = add_parts(
        [(one.kept, one.received) for one in sums], [one.parts for one in sums], after
    )
    for one, (kept, sent) in zip(sums, found):
        one.send(kept, sent)


@dataclasses.dataclass
class Gathered:
    held: jax.Array
    other: jax.Array | None = None
    slots: jax.Array | None = None

    @property
    def count(self):
        return 1 if self.other is None else 3

    @property
    def shape(self):
        if self.other is None:
            return self.held.shape
        half, rows, width = self.held.shape
        return (2 * half * rows, width)

    def inputs(self):
        if self.other is None:
            return [Left(self.held)]
        return [Scalars(self.slots), Left(self.held), Left(self.other)]

    def scratch(self, chunks=1):
        copies = chunks if self.other is None else 2 * self.held.shape[0]
        return [pltpu.VMEM(self.shape, jnp.bfloat16), pltpu.SemaphoreType.DMA((copies,))]


def fetch_weight(inputs, weight, sems, chunks=1):
    count = sems.shape[0]
    rows = weight.shape[0] // count
    each = count // chunks

    def copy(source, i):
        target = weight.at[pl.ds(pl.multiple_of(i * rows, rows), rows)]
        return pltpu.make_async_copy(source, target, sems.at[i])

    if len(inputs) == 1:
        copies = [copy(inputs[0].at[pl.ds(i * rows, rows)], i) for i in range(count)]
        for one in copies:
            one.start()

        def wait_ordered(chunk):
            for one in copies[chunk * each : (chunk + 1) * each]:
                one.wait()

        return wait_ordered

    table, held, other = inputs
    half = held.shape[0]

    def begin(i, carry):
        slot = table[i]

        @pl.when(slot < half)
        def _():
            copy(held.at[slot], i).start()

        @pl.when(slot >= half)
        def _():
            copy(other.at[slot - half], i).start()

        return carry

    lax.fori_loop(0, count, begin, 0)

    def wait(chunk):
        def finish(i, carry):
            copy(held.at[0], i).wait()
            return carry

        lax.fori_loop(chunk * each, (chunk + 1) * each, finish, 0)

    return wait


def weight_grad_kernel(beside, table, *refs):
    left, left_peer, right, right_peer = refs[:4]
    if beside:
        second, second_peer, second_right, second_right_peer, core = refs[4:9]
        kept_ref, sent_ref, total_ref, second_ref = refs[9:]
    else:
        kept_ref, sent_ref, total_ref = refs[4:]
    half, rows, _ = kept_ref.shape
    width = right.shape[1]
    for k in range(0, total_ref.shape[0], 512):
        total_ref[k : k + 512, :] = product_t(left[:, k : k + 512], right[...]) + product_t(
            left_peer[:, k : k + 512], right_peer[...]
        )
    if beside:
        second_ref[...] = product_t(second[...], second_right[...]) + product_t(
            second_peer[...], second_right_peer[...]
        )

    def place(out_ref, slot, i):
        found = total_ref[pl.ds(pl.multiple_of(i * rows, rows), rows), :]
        out_ref[slot, :, :width] = found.astype(out_ref.dtype)
        for part in range(beside):
            start = ((2 * i + core[0]) * beside + part) * rows
            across = second_ref.shape[1]
            columns = slice(width + part * across, width + (part + 1) * across)
            found = second_ref[pl.ds(pl.multiple_of(start, rows), rows), :]
            out_ref[slot, :, columns] = found.astype(out_ref.dtype)

    def move(i, carry):
        slot = table[i]

        @pl.when(slot < half)
        def _():
            place(kept_ref, slot, i)

        @pl.when(slot >= half)
        def _():
            place(sent_ref, slot - half, i)

        return carry

    lax.fori_loop(0, 2 * half, move, 0)


def weight_grad(left, right, slots, size, before, second=None, after=()):
    depth, width = left[0].shape[1], right[0].shape[1]
    rows = depth // size
    args = [Scalars(slots), *left, *right]
    scratch, beside, extra = [pltpu.VMEM((depth, width), jnp.float32)], 0, 0
    if second is not None:
        (second_left, second_right, core) = second
        args += [*second_left, *second_right, core]
        second_shape = (second_left[0].shape[1], second_right[0].shape[1])
        beside = second_shape[0] // (2 * depth)
        extra = beside * second_shape[1]
        scratch.append(pltpu.VMEM(second_shape, jnp.float32))
    shape = (size // 2, rows, width + extra)
    kept, sent = kernel_call(
        lambda *refs: weight_grad_kernel(beside, *refs),
        [(shape, jnp.float32, PUT_FAR), (shape, jnp.bfloat16, PUT_FAR)],
        args,
        scratch=scratch,
        flops=4 * left[0].shape[0] * depth * width,
        after=after,
    )
    return Scattering(kept, sent, size, before)


def swap_columns(total):
    me = lax.axis_index("shard")
    half = total.shape[0] // 2
    mine = lax.dynamic_slice_in_dim(total, me * half, half, 0)
    other = swap_cores(lax.dynamic_slice_in_dim(total, (1 - me) * half, half, 0))
    first, second = jnp.where(me == 0, mine, other), jnp.where(me == 0, other, mine)
    return jnp.concatenate([first, second], 1)


def tiles(rows, width, high, wide):
    for r in range(0, rows, high):
        for k in range(0, width, wide):
            yield slice(r, r + high), slice(k, k + wide)


def norm_factors(terms, norm_ref, row, count):
    totals = jnp.sum(terms[...], 0)
    average = totals[0:1] / count
    inverse = lax.rsqrt(totals[1:2] / count - average * average + EPS_NORM)
    return average, inverse, norm_ref[row : row + 1, :], norm_ref[row + 1 : row + 2, :]


def normalize(values, factors, columns):
    average, inverse, gain, shift = (part[:, columns] for part in factors)
    unit = (values - average) * inverse
    return unit, gain * unit + shift


def silu(values):
    return values * jax.nn.sigmoid(values)


def norm_backward(grad, unit, factors, totals, count, columns):
    _, inverse, gain, _ = (part[:, columns] for part in factors)
    mean_grad = totals[0:1, columns] / count
    mean_product = totals[1:2, columns] / count
    return gain * inverse * (grad - mean_grad - unit * mean_product)


class Sums:
    def __init__(self, out_ref):
        self.out_ref = out_ref
        self.parts = {}

    def add(self, columns, first, second):
        key = (columns.start, columns.stop)
        fold = lambda v: jnp.sum(v.reshape(v.shape[0] // 8, 8, v.shape[1]), 0)
        first, second = fold(first), fold(second)
        if key in self.parts:
            first, second = self.parts[key][0] + first, self.parts[key][1] + second
        self.parts[key] = (first, second)

    def store(self):
        for (start, stop), (first, second) in self.parts.items():
            first = jnp.sum(first, 0, keepdims=True)
            second = jnp.sum(second, 0, keepdims=True)
            for copy in range(self.out_ref.shape[0]):
                self.out_ref[copy, 0:1, start:stop] = first
                self.out_ref[copy, 1:2, start:stop] = second


def reduce_kernel(weights, x_ref, *refs):
    inputs, refs = refs[:weights], refs[weights:]
    pre_ref, sums_ref, weight_out, weight, sems, out_sem = refs
    fetch_weight(inputs, weight, sems)(0)
    copy_out = pltpu.make_async_copy(weight, weight_out, out_sem)
    copy_out.start()
    sums = Sums(sums_ref)
    for columns in (slice(k, k + 256) for k in range(0, MID, 256)):
        pre = product(x_ref[...], weight[:, columns])
        pre_ref[:, columns] = pre
        sums.add(columns, pre, pre * pre)
    sums.store()
    copy_out.wait()


def spatial_kernel(weights, count, pre_ref, norm_ref, valid_ref, *refs):
    term_refs, *refs = refs
    inputs, refs = refs[:weights], refs[weights:]
    out_ref, sums_ref, patches_out, weight_out, padded, patches, sem, weight, sems, out_sem = refs
    wait = fetch_weight(inputs, weight, sems)
    rows = pre_ref.shape[0]
    factors = norm_factors(term_refs, norm_ref, 0, count)
    edge = jnp.zeros((EDGE, MID), jnp.float32)
    padded[0:EDGE, :] = edge
    padded[EDGE + rows :, :] = edge
    for high, columns in tiles(rows, MID, 48, 512):
        _, shifted = normalize(pre_ref[high, columns], factors, columns)
        low = silu(shifted).astype(jnp.bfloat16)
        padded[EDGE + high.start : EDGE + high.stop, columns] = low.astype(jnp.float32)
    for place in range(9):
        offset = EDGE + neighbour(place, rows // (2 * SIDE * SIDE))
        for high, columns in tiles(rows, MID, 48, 512):
            values = padded[offset + high.start : offset + high.stop, columns]
            values = values * valid_ref[high, place : place + 1]
            patches[high, place * MID : (place + 1) * MID] = values.astype(jnp.bfloat16)
    copy = pltpu.make_async_copy(patches, patches_out, sem)
    copy.start()
    wait(0)
    copy_out = pltpu.make_async_copy(weight, weight_out, out_sem)
    copy_out.start()
    sums = Sums(sums_ref)
    for columns in (slice(k, k + 256) for k in range(0, MID, 256)):
        pre = product(patches[...], weight[:, columns])
        out_ref[:, columns] = pre
        sums.add(columns, pre, pre * pre)
    sums.store()
    copy.wait()
    copy_out.wait()


def expand_kernel(weights, count, pre_ref, norm_ref, *refs):
    term_refs, *refs = refs
    inputs, refs = refs[:weights], refs[weights:]
    act_ref, out_ref, sums_ref, weight_out, side_ref, weight, sems, out_sem = refs
    wait = fetch_weight(inputs, weight, sems)
    factors = norm_factors(term_refs, norm_ref, 2, count)
    for high, columns in tiles(pre_ref.shape[0], MID, 48, 512):
        _, shifted = normalize(pre_ref[high, columns], factors, columns)
        act_ref[high, columns] = silu(shifted).astype(jnp.bfloat16)
    wait(0)
    copy_out = pltpu.make_async_copy(weight, weight_out, out_sem)
    copy_out.start()
    if weight.shape[1] > D:
        side_ref[...] = weight[:, D:]
    else:
        side_ref[...] = jnp.zeros_like(side_ref)
    sums = Sums(sums_ref)
    for columns in (slice(k, k + 256) for k in range(0, D, 256)):
        pre = product(act_ref[...], weight[:, columns])
        out_ref[:, columns] = pre
        sums.add(columns, pre, pre * pre)
    sums.store()
    copy_out.wait()


def split(values):
    high = values.astype(jnp.bfloat16)
    return high, (values - high.astype(jnp.float32)).astype(jnp.bfloat16)


def pool_kernel(weights, count, pre_ref, x_ref, norm_ref, pool_ref, size_ref, *refs):
    term_refs, *refs = refs
    inputs, refs = refs[:weights], refs[weights:]
    pooled_ref, out_ref, sums_ref, project_ref, high_ref, rest_ref, weight, sems = refs
    wait = fetch_weight(inputs, weight, sems, CHUNKS)
    factors = norm_factors(term_refs, norm_ref, 0, count)
    rows = pre_ref.shape[0]
    for k in range(0, D, 256):
        for high, columns in tiles(rows, 256, 96, 256):
            across = slice(k + columns.start, k + columns.stop)
            _, shifted = normalize(pre_ref[high, across], factors, across)
            block = silu(shifted + x_ref[high, across].astype(jnp.float32))
            high_ref[high, columns], rest_ref[high, columns] = split(block)
        pooled = product(pool_ref[...], high_ref[...]) + product(pool_ref[...], rest_ref[...])
        pooled_ref[:, k : k + 256] = (pooled / size_ref[...]).astype(jnp.bfloat16)
    step = D // CHUNKS
    total = 0.0
    for chunk in range(CHUNKS):
        wait(chunk)
        part = slice(chunk * step, (chunk + 1) * step)
        total = total + product(pooled_ref[:, part], weight[part, :D])
    out_ref[...] = total
    project_ref[...] = weight[:, D:]
    sums = Sums(sums_ref)
    for columns in (slice(k, k + 512) for k in range(0, D, 512)):
        pre = out_ref[:, columns]
        sums.add(columns, pre, pre * pre)
    sums.store()


def embed_kernel(count, pre_ref, norm_ref, project_ref, bias_ref, *refs):
    term_refs, *refs = refs
    act_ref, unit_ref, inverse_ref, low_ref = refs
    factors = norm_factors(term_refs, norm_ref, 2, count)
    for high, columns in tiles(pre_ref.shape[0], D, pre_ref.shape[0], 512):
        _, shifted = normalize(pre_ref[high, columns], factors, columns)
        act_ref[high, columns] = silu(shifted).astype(jnp.bfloat16)
    embed = product(act_ref[...], project_ref[...]) + bias_ref[...]
    inverse = lax.rsqrt(jnp.sum(embed * embed, 1, keepdims=True) + EPS_UNIT)
    unit = embed * inverse
    unit_ref[...] = unit
    inverse_ref[...] = jnp.broadcast_to(inverse, inverse_ref.shape)
    low_ref[...] = jnp.broadcast_to(unit.astype(jnp.bfloat16)[None], low_ref.shape)


def embed_back_kernel(
    count, grad_ref, unit_ref, inverse_ref, project_ref, pre_ref, norm_ref, *refs
):
    term_refs, *refs = refs
    low_ref, out_ref, sums_ref, bias_ref = refs
    grad, unit = grad_ref[...], unit_ref[...]
    embed_grad = inverse_ref[...] * (grad - unit * jnp.sum(grad * unit, 1, keepdims=True))
    low_ref[...] = embed_grad.astype(jnp.bfloat16)
    bias_ref[...] = jnp.sum(embed_grad, 0, keepdims=True)
    factors = norm_factors(term_refs, norm_ref, 2, count)
    sums = Sums(sums_ref)
    for columns in (slice(k, k + 512) for k in range(0, D, 512)):
        back = product_bt(low_ref[...], project_ref[columns, :])
        head_unit, shifted = normalize(pre_ref[:, columns], factors, columns)
        back = back * silu_slope(shifted)
        out_ref[:, columns] = back
        sums.add(columns, back, back * head_unit)
    sums.store()


def pool_back_kernel(
    weights,
    crop_count,
    count,
    grad_ref,
    head_pre_ref,
    pre_ref,
    x_ref,
    norm_ref,
    spread_ref,
    size_ref,
    *refs,
):
    head_terms, head_back, pre_terms, *refs = refs
    inputs, refs = refs[:weights], refs[weights:]
    low_ref, own_ref, other_ref, sums_ref, weight, sems = refs
    wait = fetch_weight(inputs, weight, sems, CHUNKS)
    step = D // CHUNKS
    head_factors = norm_factors(head_terms, norm_ref, 2, crop_count)
    totals = jnp.sum(head_back[...], 0)
    for columns in (slice(k, k + 512) for k in range(0, D, 512)):
        unit, _ = normalize(head_pre_ref[:, columns], head_factors, columns)
        grad = norm_backward(
            grad_ref[:, columns], unit, head_factors, totals, crop_count, columns
        )
        low_ref[:, columns] = grad.astype(jnp.bfloat16)
    factors = norm_factors(pre_terms, norm_ref, 0, count)
    sums = Sums(sums_ref)
    own_rows = own_ref.shape[0]
    for chunk in range(CHUNKS):
        wait(chunk)
        part = slice(chunk * step, (chunk + 1) * step)
        pooled = product_bt(low_ref[...], weight[part, :D]) / size_ref[...]
        high_part, rest_part = split(pooled)
        for rows, columns in tiles(2 * own_rows, part.stop - part.start, 48, 256):
            across = slice(part.start + columns.start, part.start + columns.stop)
            spread = spread_ref[rows, :]
            out_grad = product(spread, high_part[:, columns]) + product(
                spread, rest_part[:, columns]
            )
            unit, shifted = normalize(pre_ref[rows, across], factors, across)
            joined = shifted + x_ref[rows, across].astype(jnp.float32)
            joined_grad = out_grad * silu_slope(joined)
            if rows.start < own_rows:
                own_ref[rows, across] = joined_grad
            else:
                other_ref[rows.start - own_rows : rows.stop - own_rows, across] = joined_grad
            sums.add(across, joined_grad, joined_grad * unit)
    sums.store()


def column_halves(low_ref, core, kept_ref, sent_ref):
    half = kept_ref.shape[1]
    for out_ref, which in ((kept_ref, core[0]), (sent_ref, 1 - core[0])):
        out_ref[...] = low_ref[:, pl.ds(pl.multiple_of(which * half, half), half)]


def expand_back_kernel(
    count, core, own_ref, other_ref, pre_ref, wide_ref, weight_ref, before_ref, mid_ref, bias_ref, *refs
):
    pre_terms, back_terms, before_terms, kept_ref, sent_ref, out_ref, sums_ref, low_ref = refs
    factors = norm_factors(pre_terms, wide_ref, 0, count)
    totals = jnp.sum(back_terms[...], 0)
    own_rows = own_ref.shape[0]
    for rows, columns in tiles(2 * own_rows, D, 48, 512):
        unit, _ = normalize(pre_ref[rows, columns], factors, columns)
        if rows.start < own_rows:
            grad = own_ref[rows, columns]
        else:
            grad = other_ref[rows.start - own_rows : rows.stop - own_rows, columns]
        grad = norm_backward(grad, unit, factors, totals, count, columns)
        low_ref[rows, columns] = grad.astype(jnp.bfloat16)
    column_halves(low_ref, core, kept_ref, sent_ref)
    factors = norm_factors(before_terms, mid_ref, 2, count)
    sums = Sums(sums_ref)
    for columns in (slice(k, k + 256) for k in range(0, MID, 256)):
        back = product_bt(low_ref[...], weight_ref[columns, :D])
        unit, shifted = normalize(before_ref[:, columns], factors, columns)
        back = back * silu_slope(shifted)
        out_ref[:, columns] = back
        sums.add(columns, back, back * unit)
    sums.store()
    bias = jnp.concatenate([bias_ref[...], jnp.zeros_like(bias_ref)], 0)
    for copy in range(sums_ref.shape[0]):
        sums_ref[copy, :, MID:] = bias


def spatial_back_kernel(
    count, core, grad_ref, pre_ref, norm_ref, weight_ref, before_ref, valid_ref, *refs
):
    pre_terms, back_terms, before_terms, kept_ref, sent_ref, out_ref, sums_ref, slots, low_ref = refs
    rows = grad_ref.shape[0]
    factors = norm_factors(pre_terms, norm_ref, 2, count)
    totals = jnp.sum(back_terms[...], 0)
    for high, columns in tiles(rows, MID, 48, 512):
        unit, _ = normalize(pre_ref[high, columns], factors, columns)
        grad = norm_backward(grad_ref[high, columns], unit, factors, totals, count, columns)
        low_ref[high, columns] = grad.astype(jnp.bfloat16)
    column_halves(low_ref, core, kept_ref, sent_ref)
    edge = jnp.zeros((EDGE, MID), jnp.float32)
    for place in range(9):
        slots[place, 0:EDGE, :] = edge
        slots[place, EDGE + rows :, :] = edge
        for columns in (slice(k, k + 256) for k in range(0, MID, 256)):
            patch = product_bt(
                low_ref[...],
                weight_ref[place * MID + columns.start : place * MID + columns.stop, :],
            )
            slots[place, EDGE : EDGE + rows, columns] = patch * valid_ref[:, place : place + 1]
    factors = norm_factors(before_terms, norm_ref, 0, count)
    sums = Sums(sums_ref)
    for high, columns in tiles(rows, MID, 48, 256):
        back = 0.0
        for place in range(9):
            start = EDGE - neighbour(place, rows // (2 * SIDE * SIDE)) + high.start
            back = back + slots[place, start : start + high.stop - high.start, columns]
        unit, shifted = normalize(before_ref[high, columns], factors, columns)
        back = back * silu_slope(shifted)
        out_ref[high, columns] = back
        sums.add(columns, back, back * unit)
    sums.store()


def reduce_back_kernel(
    count,
    core,
    grad_ref,
    pre_ref,
    norm_ref,
    pre_terms,
    back_terms,
    low_ref,
    other_ref,
    kept_ref,
    sent_ref,
):
    rows = grad_ref.shape[0]
    factors = norm_factors(pre_terms, norm_ref, 0, count)
    totals = jnp.sum(back_terms[...], 0)
    for high, columns in tiles(rows, MID, 48, 512):
        unit, _ = normalize(pre_ref[high, columns], factors, columns)
        grad = norm_backward(grad_ref[high, columns], unit, factors, totals, count, columns)
        low_ref[high, columns] = grad.astype(jnp.bfloat16)
    other_ref[...] = low_ref[rows // 2 :, :]
    column_halves(low_ref, core, kept_ref, sent_ref)


def arrange_kernel(core, canvases_ref, own_ref, other_ref, rows_ref):
    _, _, _, canvas_count, _ = canvases_ref.shape
    for which, out_ref in enumerate((own_ref, other_ref)):
        micro = core[0] if which == 0 else 1 - core[0]
        for pixel in range(SIDE * SIDE):
            rows = slice(pixel * canvas_count, (pixel + 1) * canvas_count)
            values = canvases_ref[micro, pixel // SIDE, pixel % SIDE]
            rows_ref[rows, :] = values.astype(jnp.float32)
        out_ref[...] = rows_ref[...].astype(jnp.bfloat16)


def input_grad_kernel(
    core, own_ref, other_ref, low_ref, other_low_ref, weight_ref, out_ref, rows_ref
):
    own_rows = own_ref.shape[0]
    canvas_count = out_ref.shape[3]
    for which in range(2):
        micro = core[0] if which == 0 else 1 - core[0]
        grad_ref = own_ref if which == 0 else other_ref
        low = low_ref[:own_rows, :] if which == 0 else other_low_ref[...]
        for columns in (slice(k, k + 512) for k in range(0, D, 512)):
            rows_ref[:, columns] = grad_ref[:, columns] + product_bt(low, weight_ref[columns, :])
        for pixel in range(SIDE * SIDE):
            rows = slice(pixel * canvas_count, (pixel + 1) * canvas_count)
            out_ref[micro, pixel // SIDE, pixel % SIDE] = rows_ref[rows, :]


def inside_canvas(own_canvases):
    valid = np.zeros((2, SIDE, SIDE, own_canvases, 16), np.float32)
    for place in range(9):
        down, right = place // 3 - 1, place % 3 - 1
        for y in range(SIDE):
            for x in range(SIDE):
                valid[:, y, x, :, place] = 0 <= y + down < SIDE and 0 <= x + right < SIDE
    return jnp.asarray(valid.reshape(-1, 16))


def neighbour(place, own_canvases):
    return ((place // 3 - 1) * SIDE + place % 3 - 1) * own_canvases


EDGE = 32


def add_columns(total_ref, columns, values):
    rows, width = values.shape
    total_ref[:, columns] += jnp.sum(values.reshape(rows // 8, 8, width), 0)


def codes_kernel(
    crops,
    device_crops,
    place,
    units_ref,
    side_ref,
    prototypes_ref,
    loss_ref,
    proto_grad_ref,
    unit_grad_ref,
    proto_ref,
    partner_ref,
    codes_ref,
    heat_ref,
    score_ref,
    total_ref,
    scale_ref,
    inverse_ref,
    *,
    factor,
):
    rows_all, width = codes_ref.shape
    own = unit_grad_ref.shape[0]
    chunks = [slice(k, k + LANES) for k in range(0, width, LANES)]
    real = lax.broadcasted_iota(jnp.int32, (1, width), 1) < PROTOS

    dim = units_ref.shape[1]
    proto_ref[PROTOS // 16 * 16 :, :] = jnp.zeros((width - PROTOS // 16 * 16, dim), jnp.bfloat16)
    proto_ref[:PROTOS, :] = prototypes_ref[...]

    queue_rows = side_ref.shape[0]
    device_rows = queue_rows // (crops // device_crops)
    crop = lax.broadcasted_iota(jnp.int32, (crops, queue_rows), 0)
    holder = crop // device_crops ^ place[1]
    row = lax.broadcasted_iota(jnp.int32, (crops, queue_rows), 1)
    holds = (row == holder * device_rows).astype(jnp.bfloat16)
    found = product(holds, side_ref[:, dim:])
    crop = lax.broadcasted_iota(jnp.int32, found.shape, 0)
    lane = lax.broadcasted_iota(jnp.int32, found.shape, 1)
    here = lane == place[1] * device_crops + crop % device_crops
    partner = jnp.sum(jnp.where(here, found, 0.0), 1, keepdims=True)
    partner_ref[...] = partner.astype(jnp.int32)

    def scores(rows, columns, queue=False):
        left = side_ref[rows, :dim] if queue else units_ref[rows, :]
        return product_bt(left, proto_ref[columns, :])

    def keep(values, columns):
        if columns.stop <= PROTOS:
            return values
        lanes = columns.start + lax.broadcasted_iota(jnp.int32, values.shape, 1)
        return jnp.where(lanes < PROTOS, values, 0.0)

    def fold(values):
        return sum(values[:, k : k + 128] for k in range(0, values.shape[1], 128))

    total_ref[...] = jnp.zeros_like(total_ref)

    for queue, start, count in ((False, 0, crops), (True, crops, queue_rows)):

        def first(i, carry):
            rows = pl.ds(pl.multiple_of(i * 128, 128), 128)
            target = pl.ds(pl.multiple_of(start + i * 128, 128), 128)
            for columns in chunks:
                score = scores(rows, columns, queue)
                powers = keep(jnp.exp(score * (1.0 / SINK_EPS)), columns)
                codes_ref[target, columns] = powers
                add_columns(total_ref, columns, powers)
            return carry

        lax.fori_loop(0, count // 128, first, 0)

    def column_factors(turn):
        total = jnp.sum(total_ref[...], 0, keepdims=True)
        total = jnp.where(real, total, 1.0)
        if turn == 0:
            scale = jnp.where(total > 1e30, 2.0**-64, 1.0)
            scale_ref[...] = jnp.broadcast_to(scale, scale_ref.shape)
            total = total * scale
        inverse_ref[...] = jnp.broadcast_to(1.0 / total, inverse_ref.shape)

    def divided(turn, rows, columns):
        values = codes_ref[rows, columns]
        if turn == 0:
            values = values * scale_ref[0:1, columns]
        return values * inverse_ref[0:1, columns]

    def row_inverse(turn, rows):
        part = sum(fold(divided(turn, rows, columns)) for columns in chunks)
        return 1.0 / jnp.sum(part, 1, keepdims=True)

    for turn in range(SINK_ITERS - 1):
        column_factors(turn)
        total_ref[...] = jnp.zeros_like(total_ref)

        def both(i, carry):
            rows = pl.ds(pl.multiple_of(i * 64, 64), 64)
            inverse = row_inverse(turn, rows)
            for columns in chunks:
                values = divided(turn, rows, columns) * inverse
                codes_ref[rows, columns] = values
                add_columns(total_ref, columns, values)
            return carry

        lax.fori_loop(0, rows_all // 64, both, 0)

    column_factors(SINK_ITERS - 1)
    proto_grad_ref[...] = jnp.zeros_like(proto_grad_ref)
    loss_ref[...] = jnp.zeros_like(loss_ref)
    block = 128

    def last(i, carry):
        rows = pl.ds(pl.multiple_of(i * block, block), block)
        inverse = row_inverse(SINK_ITERS - 1, rows)
        row = lax.broadcasted_iota(jnp.int32, (block, block), 0)
        column = lax.broadcasted_iota(jnp.int32, (block, block), 1)
        pick = (column == (row // CROPS) * CROPS + partner_ref[rows, :]).astype(jnp.bfloat16)
        heat_part = jnp.zeros((block, 128), jnp.float32)
        target_part = jnp.zeros((block, 128), jnp.float32)
        loss_part = jnp.zeros((block, 128), jnp.float32)
        for columns in chunks:
            score = scores(rows, columns)
            heat = keep(jnp.exp(score * (1.0 / SOFTMAX_HEAT)), columns)
            heat_ref[:, columns] = heat
            heat_part += fold(heat)
            codes = divided(SINK_ITERS - 1, rows, columns) * inverse
            high = codes.astype(jnp.bfloat16)
            rest = (codes - high.astype(jnp.float32)).astype(jnp.bfloat16)
            target = product(pick, high) + product(pick, rest)
            codes_ref[rows, columns] = target
            target_part += fold(target)
            loss_part += fold(target * score)
        heat_sum = jnp.sum(heat_part, 1, keepdims=True)
        target_sum = jnp.sum(target_part, 1, keepdims=True)
        row_loss = (
            target_sum * jnp.log(heat_sum)
            - jnp.sum(loss_part, 1, keepdims=True) * (1.0 / SOFTMAX_HEAT)
        )
        loss_ref[...] += jnp.broadcast_to(jnp.sum(row_loss, 0, keepdims=True), loss_ref.shape)
        ratio = target_sum / heat_sum * factor
        for columns in chunks:
            grad = heat_ref[:, columns] * ratio - codes_ref[rows, columns] * factor
            low = grad.astype(jnp.bfloat16)
            score_ref[rows, columns] = low
            proto_grad_ref[:, columns] += product_t(units_ref[rows, :], low)
        return carry

    lax.fori_loop(0, crops // block, last, 0)
    mine = pl.ds(pl.multiple_of(place[0], own), own)
    unit_grad_ref[...] = product(score_ref[mine, :], proto_ref[...])


def gathered_loss(units, side, prototypes, place, own, device_crops, loss_factor_weight):
    crops, dim = units.shape
    width = -(-PROTOS // LANES) * LANES
    rows_all = crops + side.shape[0]
    f32, bf16 = jnp.float32, jnp.bfloat16
    loss, proto_grad, unit_grad = kernel_call(
        lambda *refs: codes_kernel(
            crops, device_crops, *refs, factor=loss_factor_weight / SOFTMAX_HEAT
        ),
        [((8, 128), f32), ((dim, width), f32), ((own, dim), f32)],
        [Scalars(place), units, side, prototypes],
        scratch=[
            pltpu.VMEM((width, dim), bf16),
            pltpu.VMEM((crops, 1), jnp.int32),
            pltpu.VMEM((rows_all, width), f32),
            pltpu.VMEM((128, width), f32),
            pltpu.VMEM((crops, width), bf16),
            pltpu.VMEM((8, width), f32),
            pltpu.VMEM((8, width), f32),
            pltpu.VMEM((8, width), f32),
        ],
        flops=2 * width * (rows_all * dim + 6 * crops * dim),
        transcendentals=width * (rows_all + crops),
        limit=24,
    )
    return loss[0, 0], proto_grad, unit_grad


def sinkhorn(batch_codes, stored_codes, total):
    for turn in range(SINK_ITERS):
        column_totals = total(jnp.sum(batch_codes, 0) + jnp.sum(stored_codes, 0))
        batch_codes = batch_codes / column_totals
        stored_codes = stored_codes / column_totals
        batch_codes = batch_codes / jnp.sum(batch_codes, 1, keepdims=True)
        stored_codes = stored_codes / jnp.sum(stored_codes, 1, keepdims=True)
    return batch_codes


def swapped_loss(scores, codes, pick, loss_factor_weight):
    rows = scores.shape[0]
    target = jnp.einsum(
        "cab,cbk->cak", pick, codes.reshape(rows // CROPS, CROPS, PROTOS), precision=HIGH
    ).reshape(rows, PROTOS)
    log_likelihoods = jax.nn.log_softmax(scores / SOFTMAX_HEAT, axis=1)
    score_grad = (jnp.exp(log_likelihoods) * jnp.sum(target, 1, keepdims=True) - target) * (
        loss_factor_weight / SOFTMAX_HEAT
    )
    return -jnp.sum(target * log_likelihoods), score_grad.astype(jnp.bfloat16)


def per_device(
    canvases,
    crop_map,
    partner,
    queue,
    w_reduce,
    w_spatial,
    w_expand,
    w_hidden,
    w_project,
    norm_mid,
    norm_wide,
    bias_out,
    prototypes,
):
    f32, bf16 = jnp.float32, jnp.bfloat16
    size = lax.axis_size("dp")
    me_dp, me_core = lax.axis_index("dp"), lax.axis_index("shard")
    core = Scalars(me_core.astype(jnp.int32).reshape(1))
    own_canvases = canvases.shape[1]
    canvas_count = 2 * own_canvases
    pixels = SIDE * SIDE
    own_rows = own_canvases * pixels
    local_rows = canvas_count * pixels
    local_crops = canvas_count * CROPS
    pixel_total = float(local_rows * size)
    crop_count = local_crops * size
    crop_total = float(crop_count)
    loss_factor_weight = 1.0 / (MICRO * crop_total)
    crop_ids = jnp.arange(CROPS, dtype=jnp.int32)
    valid = inside_canvas(own_canvases)
    proj = bias_out.shape[0]
    partner_size = partner.size
    copies = copies_of(size)
    by_steps = size == STEPS_DP
    if by_steps:
        slots = relative_slots(size)
        chip_slots = lax.dynamic_slice_in_dim(slots.reshape(size, 2), me_core, 1, 1)[:, 0]

    def both_cores(values):
        mine = lax.dynamic_index_in_dim(values, me_core, 0, keepdims=False)
        other = lax.dynamic_index_in_dim(values, 1 - me_core, 0, keepdims=False)
        return jnp.concatenate([mine, swap_cores(other)], 0)

    def gather_whole(shard):
        return Gathered(lax.all_gather(shard, BOTH, axis=0, tiled=True))

    head_shard = jnp.concatenate([w_hidden, w_project], 1)
    beside = queue.shape[1]
    gathered_codes = (
        crop_count * PROTOS * 4 <= GATHERED_CODES_BYTES
        and queue.shape[0] == w_expand.shape[0]
        and partner_size <= beside
    )
    if gathered_codes:
        partners = jnp.pad(
            partner.astype(bf16).reshape(1, -1),
            ((0, 0), (0, beside - partner_size)),
        )
        partners = jnp.broadcast_to(partners, (queue.shape[0], beside))
        w_expand = jnp.concatenate([w_expand, queue, partners], 1)

    labels = both_cores(jnp.concatenate([crop_map, partner], 2))
    crop_map, partner = labels[:, :pixels], labels[:, pixels:]
    crop_of = jnp.arange(local_crops, dtype=jnp.int32)
    pixel_crop = crop_map + CROPS * jnp.arange(canvas_count, dtype=jnp.int32)[:, None]
    pixel_crop = pixel_crop.reshape(2, own_canvases, pixels).swapaxes(1, 2).reshape(local_rows)
    pool = (crop_of[:, None] == pixel_crop[None, :]).astype(bf16)
    spread = (pixel_crop[:, None] == crop_of[None, :]).astype(bf16)
    crop_sizes = jnp.sum(pool.astype(f32), 1, keepdims=True)

    half_rows = ((own_rows, D), bf16)
    own_x, other_x = kernel_call(
        arrange_kernel,
        [half_rows, half_rows],
        [core, canvases.transpose(0, 2, 3, 1, 4)],
        scratch=[pltpu.VMEM((own_rows, D), f32)],
    )
    input_rows = join([(own_x[None], swap_cores(other_x)[None])])[0].reshape(local_rows, D)

    if by_steps:
        reduce_part = Gathering(w_reduce, size)
        gather_step([reduce_part])
        spatial_part = Gathering(hold(w_spatial, [reduce_part.held]), size)
        gather_step([reduce_part], [pool, spread, crop_sizes, input_rows])
        head_held = lax.all_gather(hold(head_shard, [reduce_part.held]), "dp", axis=0)
        gather_step([reduce_part, spatial_part])
        expand_part = Gathering(hold(w_expand, [spatial_part.held]), size)
        reduce_all = reduce_part.finish(slots)
    else:
        reduce_all = gather_whole(w_reduce)

    mid_rows, wide_rows = ((local_rows, MID), f32), ((local_rows, D), f32)
    mid_sums, wide_sums = ((copies, 2, MID), f32), ((copies, 2, D), f32)

    def weight_out(weight):
        return (weight.shape, bf16, FAR)

    pre_one, sums, full_reduce = kernel_call(
        lambda *refs: reduce_kernel(reduce_all.count, *refs),
        [mid_rows, mid_sums, weight_out(reduce_all)],
        [input_rows] + reduce_all.inputs(),
        scratch=reduce_all.scratch() + [pltpu.SemaphoreType.DMA],
        flops=2 * local_rows * D * MID,
    )
    terms_one = terms_over_dp(sums)
    if by_steps:
        gather_step([spatial_part, expand_part], [sums])
        gather_step([spatial_part], [terms_one])
        spatial_all = spatial_part.finish(slots)
    else:
        spatial_all, expand_all = gather_whole(w_spatial), gather_whole(w_expand)

    pre_two, sums, image_patches, full_spatial = kernel_call(
        lambda *refs: spatial_kernel(spatial_all.count, pixel_total, *refs),
        [
            mid_rows,
            mid_sums,
            ((local_rows, 9 * MID), bf16, FAR),
            weight_out(spatial_all),
        ],
        [pre_one, norm_mid, valid, terms_one] + spatial_all.inputs(),
        scratch=[
            pltpu.VMEM((local_rows + 2 * EDGE, MID), f32),
            pltpu.VMEM((local_rows, 9 * MID), bf16),
            pltpu.SemaphoreType.DMA,
        ]
        + spatial_all.scratch()
        + [pltpu.SemaphoreType.DMA],
        flops=2 * local_rows * 9 * MID * MID,
    )
    terms_two = terms_over_dp(sums)
    if by_steps:
        gather_step([expand_part], [sums])
        gather_step([expand_part], [terms_two])
        expand_all = expand_part.finish(slots)

    side = ((expand_all.shape[0], max(expand_all.shape[1] - D, 128)), bf16)
    act_two, pre_three, sums, full_expand, side = kernel_call(
        lambda *refs: expand_kernel(expand_all.count, pixel_total, *refs),
        [((local_rows, MID), bf16), wide_rows, wide_sums, weight_out(expand_all), side],
        [pre_two, norm_mid, terms_two] + expand_all.inputs(),
        scratch=expand_all.scratch() + [pltpu.SemaphoreType.DMA],
        flops=2 * local_rows * D * MID,
    )
    terms_three = terms_over_dp(sums)
    if by_steps:
        head_held, _ = lax.optimization_barrier((head_held, sums))
        head = other_core_dp(head_held, size)
    else:
        head = gather_whole(head_shard)

    crop_rows = ((local_crops, D), f32)
    pooled_low, pre_head, sums, full_project = kernel_call(
        lambda *refs: pool_kernel(head.count, pixel_total, *refs),
        [((local_crops, D), bf16), crop_rows, wide_sums, ((D, proj), bf16)],
        [pre_three, input_rows, norm_wide, pool, crop_sizes, terms_three] + head.inputs(),
        scratch=[pltpu.VMEM((local_rows, 256), bf16), pltpu.VMEM((local_rows, 256), bf16)]
        + head.scratch(CHUNKS),
        flops=2 * local_crops * D * D,
        transcendentals=local_rows * D,
    )
    terms_head = terms_over_dp(sums)

    embed_rows = ((local_crops, proj), f32)
    act_head, unit_embed, inv_length, unit_low = kernel_call(
        lambda *refs: embed_kernel(crop_total, *refs),
        [
            ((local_crops, D), bf16),
            embed_rows,
            embed_rows,
            ((copies, local_crops, proj), bf16),
        ],
        [pre_head, norm_wide, Streamed(full_project), bias_out.reshape(1, proj), terms_head],
        flops=2 * local_crops * D * proj,
    )

    if gathered_codes:
        all_units = lax.all_to_all(unit_low, "dp", 0, 0).reshape(crop_count, proj)
        loss_part, proto_part, unit_grad = gathered_loss(
            all_units,
            side,
            prototypes,
            jnp.stack([me_dp * local_crops, me_core]).astype(jnp.int32),
            local_crops,
            own_canvases * CROPS,
            loss_factor_weight,
        )
    else:
        chip_queue = jnp.concatenate([queue, swap_cores(queue)], 0)
        queue_codes = jnp.exp(product_bt(chip_queue, prototypes) / SINK_EPS)
        pick = (partner[:, :, None] == crop_ids[None, None, :]).astype(f32)
        all_units = unit_low
        scores = product_bt(unit_low[0], prototypes)
        codes = sinkhorn(
            jnp.exp(scores / SINK_EPS), queue_codes, lambda sums: lax.psum(sums, "dp")
        )
        loss_part, score_low = swapped_loss(scores, codes, pick, loss_factor_weight)
        proto_part, loss_part = lax.psum((product_t(unit_low[0], score_low), loss_part), "dp")
        unit_grad = product(score_low, prototypes)

    embed_low, head_act_grad, sums, bias_part = kernel_call(
        lambda *refs: embed_back_kernel(crop_total, *refs),
        [((local_crops, proj), bf16), crop_rows, wide_sums, ((1, proj), f32)],
        [
            unit_grad,
            unit_embed,
            inv_length,
            Streamed(full_project),
            Streamed(pre_head),
            norm_wide,
            terms_head,
        ],
        flops=2 * local_crops * D * proj,
    )
    back_head = terms_over_dp(sums)

    left = lax.all_gather(pooled_low, "dp", axis=0, tiled=True)

    own_part = ((own_rows, D), f32)
    head_low, own_grad, other_grad, sums = kernel_call(
        lambda *refs: pool_back_kernel(head.count, crop_total, pixel_total, *refs),
        [((local_crops, D), bf16), own_part, own_part, wide_sums],
        [
            head_act_grad,
            pre_head,
            Streamed(pre_three),
            Streamed(input_rows),
            norm_wide,
            spread,
            crop_sizes,
            terms_head,
            back_head,
            terms_three,
        ]
        + head.inputs(),
        scratch=head.scratch(CHUNKS),
        flops=2 * local_crops * D * D,
        transcendentals=local_rows * D,
        after=[left],
    )
    back_three = terms_over_dp(sums)
    other_grad, _ = lax.optimization_barrier((other_grad, back_three))
    peer_grad = swap_cores(other_grad)

    right = lax.all_gather(head_low, "dp", axis=0, tiled=True)

    def low_halves(width):
        return [((local_rows, width // 2), bf16)] * 2

    three_kept, three_sent, two_act_grad, sums = kernel_call(
        lambda *refs: expand_back_kernel(pixel_total, *refs),
        [*low_halves(D), mid_rows, ((copies, 2, MID + proj), f32)],
        [
            core,
            own_grad,
            other_grad,
            Streamed(pre_three),
            norm_wide,
            Streamed(full_expand),
            Streamed(pre_two),
            norm_mid,
            bias_part,
            terms_three,
            back_three,
            terms_two,
        ],
        scratch=[pltpu.VMEM((local_rows, D), bf16)],
        flops=2 * local_rows * D * MID,
    )
    back_two = terms_over_dp(sums)
    before_two = []
    if by_steps:
        expand_sum = weight_grad(
            (act_two, swap_cores(act_two)),
            (three_kept, swap_cores(three_sent)),
            chip_slots,
            size,
            back_two,
            (
                (act_head, swap_cores(act_head)),
                (embed_low, swap_cores(embed_low)),
                core,
            ),
            after=[sums],
        )
        before_two = [expand_sum.kept]

    two_kept, two_sent, one_act_grad, sums = kernel_call(
        lambda *refs: spatial_back_kernel(pixel_total, *refs),
        [*low_halves(MID), mid_rows, mid_sums],
        [
            core,
            two_act_grad,
            Streamed(pre_two),
            norm_mid,
            Streamed(full_spatial),
            Streamed(pre_one),
            valid,
            terms_two,
            back_two,
            terms_one,
        ],
        scratch=[
            pltpu.VMEM((9, local_rows + 2 * EDGE, MID), f32),
            pltpu.VMEM((local_rows, MID), bf16),
        ],
        flops=2 * local_rows * 9 * MID * MID,
        after=before_two,
    )
    back_one = terms_over_dp(sums)
    before_one = []
    if by_steps:
        spatial_sum = weight_grad(
            (image_patches, swap_cores(image_patches)),
            (two_kept, swap_cores(two_sent)),
            chip_slots,
            size,
            two_kept,
            after=[sums],
        )
        before_one = [spatial_sum.kept]

    one_low, other_low, one_kept, one_sent = kernel_call(
        lambda *refs: reduce_back_kernel(pixel_total, *refs),
        [((local_rows, MID), bf16), ((own_rows, MID), bf16), *low_halves(MID)],
        [core, one_act_grad, Streamed(pre_one), norm_mid, terms_one, back_one],
        after=before_one,
    )
    if by_steps:
        scatter_step([expand_sum])
        reduce_sum = weight_grad(
            (input_rows, swap_cores(input_rows)),
            (one_kept, swap_cores(one_sent)),
            chip_slots,
            size,
            one_low,
        )
        scatter_step([spatial_sum, expand_sum])
        scatter_step([reduce_sum])
        last = reduce_sum.kept
        other_low, _ = lax.optimization_barrier((other_low, last))
    else:
        last = one_low

    proto_part, left, right, _ = lax.optimization_barrier((proto_part, left, right, last))
    if gathered_codes:
        proto_part = proto_part[:, :PROTOS]
    proto_grad = (proto_part + swap_cores(proto_part)).T
    chip_rows = 2 * w_hidden.shape[0]
    hidden_part = product_t(
        lax.dynamic_slice_in_dim(left, me_dp * chip_rows, chip_rows, 1), right
    )

    def own_half(part):
        half = chip_rows // 2
        mine = lax.dynamic_slice_in_dim(part, me_core * half, half, 0)
        other = lax.dynamic_slice_in_dim(part, (1 - me_core) * half, half, 0)
        return mine + swap_cores(other)

    grad_hidden = own_half(hidden_part)
    by_pixel = kernel_call(
        input_grad_kernel,
        [((MICRO, SIDE, SIDE, own_canvases, D), f32)],
        [core, own_grad, peer_grad, one_low, swap_cores(other_low), full_reduce],
        scratch=[pltpu.VMEM((own_rows, D), f32)],
        flops=2 * local_rows * D * MID,
    )[0]

    if by_steps:
        scatter_step([spatial_sum, reduce_sum], [by_pixel, proto_grad])
        grad_reduce = swap_columns(reduce_sum.finish())
        grad_spatial = swap_columns(spatial_sum.finish())
        total = expand_sum.finish()
        grad_expand = swap_columns(total[:, : D // 2])
        grad_project = jnp.concatenate(
            [total[:, k : k + proj] for k in range(D // 2, total.shape[1], proj)], 0
        )
    else:

        def scatter(first, kept, sent):
            lows = jnp.concatenate(
                [jnp.where(me_core == 0, kept, sent), jnp.where(me_core == 0, sent, kept)], 1
            )
            return lax.psum_scatter(
                product_t(first, lows), BOTH, scatter_dimension=0, tiled=True
            )

        grad_reduce = scatter(input_rows, one_kept, one_sent)
        grad_spatial = scatter(image_patches, two_kept, two_sent)
        grad_expand = scatter(act_two, three_kept, three_sent)
        grad_project = lax.psum_scatter(
            product_t(act_head, embed_low), BOTH, scatter_dimension=0, tiled=True
        )

    backs, _ = lax.optimization_barrier(((back_one, back_two, back_three, back_head), last))
    total_one, total_two, total_three, total_head = (jnp.sum(back, 0) for back in backs)
    narrow = jnp.concatenate(
        [
            jnp.stack([total_one[1], total_one[0], total_two[1, :MID], total_two[0, :MID]])
            .reshape(-1),
            jnp.stack([total_three[1], total_three[0], total_head[1], total_head[0]]).reshape(-1),
            total_two[0, MID:],
            jnp.broadcast_to(loss_part, (128,)),
        ]
    )
    narrow = narrow + swap_cores(narrow)
    mid_end, wide_end = norm_mid.size, norm_mid.size + norm_wide.size
    bias_end = wide_end + proj
    return (
        narrow[bias_end] * loss_factor_weight,
        by_pixel.transpose(0, 3, 1, 2, 4),
        grad_reduce,
        grad_spatial,
        grad_expand,
        grad_hidden,
        grad_project,
        narrow[:mid_end].reshape(norm_mid.shape),
        narrow[mid_end:wide_end].reshape(norm_wide.shape),
        narrow[wide_end:bias_end],
        proto_grad,
    )


def solution(mesh):
    return jax.shard_map(
        per_device,
        mesh=mesh,
        in_specs=(
            P(None, ("dp", "shard"), None, None, None),
            P(None, ("dp", "shard"), None),
            P(None, ("dp", "shard"), None),
            P(("dp", "shard"), None),
            P(("dp", "shard"), None),
            P(("dp", "shard"), None),
            P(("dp", "shard"), None),
            P(("dp", "shard"), None),
            P(("dp", "shard"), None),
            P(),
            P(),
            P(),
            P(),
        ),
        out_specs=(
            P(),
            P(None, ("dp", "shard"), None, None, None),
            P(("dp", "shard"), None),
            P(("dp", "shard"), None),
            P(("dp", "shard"), None),
            P(("dp", "shard"), None),
            P(("dp", "shard"), None),
            P(),
            P(),
            P(),
            P(),
        ),
        check_vma=False,
    )
```

time: 475 us -> 385 us (0.81)
  local copies, waits for them, and re-layouts: 123 us -> 37.7 us
  Pallas kernels: 26.3 us -> 98.3 us
  blocking collectives: 0 us -> 52.7 us
  other arithmetic: 49.3 us -> 9.4 us
  matrix products: 38.6 us -> 1.37 us
  starting transfers between devices: 127 us -> 95.4 us
  waiting for transfers between devices: 86.4 us -> 70.8 us
    pallas_call x7 -> x31, Pallas kernels: 26.3 us -> 98.3 us  [kernel_call(): pl.pallas_call(kernel, out_shape=[jax.ShapeDtypeStruct(*out) if len(out)...]
    all_to_all x0 -> x3, blocking collectives: none -> 52.7 us  [terms_over_dp(): return lax.all_to_all(copies, 'dp', 0, 0)]
    ppermute x24 -> x12, waiting for transfers between devices: 65.9 us -> 15.7 us  [flip_both(): return lax.ppermute(values, BOTH, pairs)]
    concatenate x16 -> x1, local copies, waits for them, and re-layouts: 30.2 us -> 0.01 us  [per_device(): w_expand = jnp.concatenate([w_expand, queue, partners], 1)]
    dot_general x12 -> x0, matrix products: 26.9 us -> none  [the longest x5 11.8 us: product(): return jnp.dot(left, right, preferred_element_type=jnp.float32)]
    all_to_all x2 -> x6, waiting for transfers between devices: 4.95 us -> 27.5 us  [the longest x5 20.8 us: terms_over_dp(): return lax.all_to_all(copies, 'dp', 0, 0)]
    slice x24 -> x6, local copies, waits for them, and re-layouts: 23.2 us -> 0.66 us  [the longest x1 0.51 us: gathered_loss(): return (loss[0, 0], proto_grad, unit_grad)]
    ppermute x48 -> x18, starting transfers between devices: 47.4 us -> 27.8 us  [flip_dp(): return lax.ppermute(values, 'dp', [(i, i ^ bits) for i in range(size)])]
  transfers between devices with their start and end apart: 91 -> 61, of which waited for: 29 -> 20; matrix products, arithmetic and copies ran while one was open for 41% -> 4% of each run, Pallas kernels for 6% -> 24%
where the time goes in v3:
time: 385 us; the launch traced here: 382 us
  Pallas kernels  98.3 us (26%)
  starting transfers between devices  95.4 us (25%)
  waiting for transfers between devices  70.8 us (18%)
  blocking collectives  52.7 us (14%)
  local copies, waits for them, and re-layouts  37.7 us (10%)
  between operations  16.5 us (4%)
  other arithmetic  9.4 us (2%)
    pallas_call x31, Pallas kernels, kernel_call(): pl.pallas_call(kernel, out_shape=[jax.ShapeDtypeStruct(*out) if len(out)...  98.3 us
    all_to_all x3, blocking collectives, terms_over_dp(): return lax.all_to_all(copies, 'dp', 0, 0)  52.7 us
    unnamed x150, local copies, waits for them, and re-layouts  31.7 us
    ppermute x18, starting transfers between devices, flip_dp(): return lax.ppermute(values, 'dp', [(i, i ^ bits) for i in range(size)])  27.8 us
    ppermute x22, starting transfers between devices, swap_cores(): return lax.ppermute(values, 'shard', [(0, 1), (1, 0)])  24.4 us
    all_to_all x5, starting transfers between devices, terms_over_dp(): return lax.all_to_all(copies, 'dp', 0, 0)  23.4 us
    all_to_all x5, waiting for transfers between devices, terms_over_dp(): return lax.all_to_all(copies, 'dp', 0, 0)  20.8 us
    ppermute x18, waiting for transfers between devices, flip_dp(): return lax.ppermute(values, 'dp', [(i, i ^ bits) for i in range(size)])  17.5 us
  transfers between devices with their start and end apart: 61, of which 20 were waited for; matrix products, arithmetic and copies ran while one was open for 4% of the time, Pallas kernels for 24%

profile of v3, /device:TPU:1, one launch (start us, length us, event | category | flops | bytes accessed | tf_op | source)
XLA Modules:
  0.0 382.1 jit_solution(9462847846089497408)
XLA Ops:
  42.3 7.3 %collective-permute-start.12 = (bf16[1,16,2304]{2,1,0:T(8,128)(2,1)S(1)}, bf16[1,16,2304]{2,1,0:T(8,128)(2,1)S(1)}, u32[]{:S(2)}, u32[]{:S(2)}) collective-permute-start(bf16[1,16,2304]{2,1,0:T(8,128)(2,1)S(1)} %bitcast.64), channel_id=1, source_target_pairs={{0,16},{2,18},{4,20},{6,22},{8,24},{10,26},{12,28},{14,30},{16,0},... | collective-permute-start | bytes 221192 | tf_op jit(solution)/shard_map/ppermute | solution.py:211
  57.1 21.8 %all_to_all.45.refs_2_.refs_3_.refs_9_.refs_4_ = f32[16,2,512]{2,1,0:T(2,128)S(1)} all-to-all(f32[16,2,512]{2,1,0:T(2,128)S(1)} %get-tuple-element.101.refs_6_), channel_id=1, replica_groups=mesh['dp'=16,'shard'=2] {'dp'}, dimensions={0} | all-to-all | bytes 131072 | tf_op jit(solution)/shard_map/all_to_all | solution.py:225
  85.2 6.5 %shard_map.231 = (f32[288,512]{1,0:T(8,128)S(1)}, f32[16,2,512]{2,1,0:T(2,128)S(1)}, bf16[288,4608]{1,0:T(8,128)(2,1)}, bf16[4608,512]{1,0:T(8,128)(2,1)}) custom-call(f32[288,512]{1,0:T(8,128)S(1)} %get-tuple-element.100.refs_0_.refs_5_.refs_2_, f32[4,512]{1,0:T(4,128)S(1)} %copy-done.42, f32[288,16]{1,0:T(8,128)S(1)} %copy-done.34, ...), custom_call_target="tpu_custom_call" | custom-call | flops 1358954496 | bytes 5400704 | tf_op jit(solution)/shard_map/pallas_call | solution.py:116
  92.5 16.9 %all_to_all.46.refs_2_.refs_11_.refs_7_ = f32[16,2,512]{2,1,0:T(2,128)S(1)} all-to-all(f32[16,2,512]{2,1,0:T(2,128)S(1)} %get-tuple-element.105.refs_2_), channel_id=1, replica_groups=mesh['dp'=16,'shard'=2] {'dp'}, dimensions={0} | all-to-all | bytes 131072 | tf_op jit(solution)/shard_map/all_to_all | solution.py:225
  113.5 4.7 %shard_map.234 = (bf16[288,512]{1,0:T(8,128)(2,1)}, f32[288,2048]{1,0:T(8,128)S(1)}, f32[16,2,2048]{2,1,0:T(2,128)S(1)}, bf16[512,2304]{1,0:T(8,128)(2,1)}, bf16[512,256]{1,0:T(8,128)(2,1)S(1)}) custom-call(f32[288,512]{1,0:T(8,128)S(1)} %get-tuple-element.104.refs_0_.refs_6_.refs_2_, f32[4,512]{1,0:T(4,128)S(1)} %copy-done.42, ...), custom_call_target="tpu_custom_call" | custom-call | flops 603979776 | bytes 3022976 | tf_op jit(solution)/shard_map/pallas_call | solution.py:116
  119.9 4.8 %all-to-all-start.2 = ((f32[16,2,2048]{2,1,0:T(2,128)}), f32[16,2,2048]{2,1,0:T(2,128)}, u32[]{:S(2)}, u32[]{:S(2)}) async-start(f32[16,2,2048]{2,1,0:T(2,128)} %copy-done.38), calls=%async_computation.2 | async-start | bytes 524288 | tf_op jit(solution)/shard_map/all_to_all | solution.py:225
  125.3 7.9 %all-to-all-done.2.refs_5_.refs_9_ = f32[16,2,2048]{2,1,0:T(2,128)} async-done(((f32[16,2,2048]{2,1,0:T(2,128)}), f32[16,2,2048]{2,1,0:T(2,128)}, u32[]{:S(2)}, u32[]{:S(2)}) %all-to-all-start.2) | async-done | bytes 262176 | tf_op jit(solution)/shard_map/all_to_all | solution.py:225
  135.3 5.3 %shard_map.236 = (bf16[32,2048]{1,0:T(8,128)(2,1)S(1)}, f32[32,2048]{1,0:T(8,128)S(1)}, f32[16,2,2048]{2,1,0:T(2,128)S(1)}, bf16[2048,128]{1,0:T(8,128)(2,1)S(1)}) custom-call(f32[288,2048]{1,0:T(8,128)S(1)} %get-tuple-element.107.refs_0_.refs_2_.refs_3_, bf16[288,2048]{1,0:T(8,128)(2,1)S(1)} %bitcast.52, f32[4,2048]{1,0:T(4,128)S(1)} %copy-done.25, ...), custom_call_target="tpu_custom_call" | custom-call | flops 268435456 | bytes 12765440 | tf_op jit(solution)/shard_map/pallas_call | solution.py:116
  143.5 4.7 %all-to-all-start.3 = ((f32[16,2,2048]{2,1,0:T(2,128)}), f32[16,2,2048]{2,1,0:T(2,128)S(1)}, u32[]{:S(2)}, u32[]{:S(2)}) async-start(f32[16,2,2048]{2,1,0:T(2,128)} %copy-done.39), calls=%async_computation.3 | async-start | bytes 524288 | tf_op jit(solution)/shard_map/all_to_all | solution.py:225
  149.7 6.1 %all-to-all-done.3.refs_4_.refs_6_.refs_7_ = f32[16,2,2048]{2,1,0:T(2,128)S(1)} async-done(((f32[16,2,2048]{2,1,0:T(2,128)}), f32[16,2,2048]{2,1,0:T(2,128)S(1)}, u32[]{:S(2)}, u32[]{:S(2)}) %all-to-all-start.3) | async-done | bytes 262176 | tf_op jit(solution)/shard_map/all_to_all | solution.py:225
  160.2 6.1 %all-to-all-start.4 = ((bf16[16,32,128]{2,1,0:T(8,128)(2,1)}), bf16[16,32,128]{2,1,0:T(8,128)(2,1)S(1)}, u32[]{:S(2)}, u32[]{:S(2)}) async-start(bf16[16,32,128]{2,1,0:T(8,128)(2,1)} %get-tuple-element.113), calls=%async_computation.4 | async-start | bytes 262144 | tf_op jit(solution)/shard_map/all_to_all | solution.py:1233
  166.4 6.7 %all-to-all-done.4 = bf16[16,32,128]{2,1,0:T(8,128)(2,1)S(1)} async-done(((bf16[16,32,128]{2,1,0:T(8,128)(2,1)}), bf16[16,32,128]{2,1,0:T(8,128)(2,1)S(1)}, u32[]{:S(2)}, u32[]{:S(2)}) %all-to-all-start.4) | async-done | bytes 131104 | tf_op jit(solution)/shard_map/all_to_all | solution.py:1233
  174.3 17.2 %shard_map.238 = (f32[8,128]{1,0:T(8,128)S(1)}, f32[128,3072]{1,0:T(8,128)S(1)}, f32[32,128]{1,0:T(8,128)S(1)}) custom-call(s32[2]{0:T(128)S(1)} %pad_add_fusion.1.refs_0_, bf16[512,128]{1,0:T(8,128)(2,1)S(1)} %bitcast.68, bf16[512,256]{1,0:T(8,128)(2,1)S(1)} %copy-done.54, bf16[3000,128]{1,0:T(8,128)(2,1)S(1)} %copy-done.50), custom_call_target="tpu_custom_call" | custom-call | flops 3221225472 | bytes 1161224 | tf_op jit(solution)/shard_map/pallas_call | solution.py:116
  194.2 14.0 %all_to_all.47.refs_8_ = f32[16,2,2048]{2,1,0:T(2,128)S(1)} all-to-all(f32[16,2,2048]{2,1,0:T(2,128)S(1)} %get-tuple-element.119), channel_id=1, replica_groups=mesh['dp'=16,'shard'=2] {'dp'}, dimensions={0} | all-to-all | bytes 524288 | tf_op jit(solution)/shard_map/all_to_all | solution.py:225
  211.0 9.7 %shard_map.240 = (bf16[32,2048]{1,0:T(8,128)(2,1)}, f32[144,2048]{1,0:T(8,128)S(1)}, f32[144,2048]{1,0:T(8,128)}, f32[16,2,2048]{2,1,0:T(2,128)}) custom-call(f32[32,2048]{1,0:T(8,128)S(1)} %get-tuple-element.118.refs_0_, f32[32,2048]{1,0:T(8,128)S(1)} %copy-done.15, f32[288,2048]{1,0:T(8,128)} %copy-done.2, bf16[288,2048]{1,0:T(8,128)(2,1)} %bitcast.53, ...), custom_call_target="tpu_custom_call" | custom-call | flops 268435456 | bytes 13814016 | tf_op jit(solution)/shard_map/pallas_call | solution.py:116
  225.7 6.8 %all-to-all-done.6.refs_10_ = f32[16,2,2048]{2,1,0:T(2,128)S(1)} async-done(((f32[16,2,2048]{2,1,0:T(2,128)}), f32[16,2,2048]{2,1,0:T(2,128)S(1)}, u32[]{:S(2)}, u32[]{:S(2)}) %all-to-all-start.6) | async-done | bytes 262176 | tf_op jit(solution)/shard_map/all_to_all | solution.py:225
  232.5 6.2 %shard_map.241 = (bf16[288,1024]{1,0:T(8,128)(2,1)S(1)}, bf16[288,1024]{1,0:T(8,128)(2,1)}, f32[288,512]{1,0:T(8,128)S(1)}, f32[16,2,640]{2,1,0:T(2,128)}) custom-call(s32[1]{0:T(128)} %bitcast.refs_0_.refs_9_, f32[144,2048]{1,0:T(8,128)S(1)} %get-tuple-element.121.refs_1_, f32[144,2048]{1,0:T(8,128)} %get-tuple-element.124.refs_2_, f32[288,2048]{1,0:T(8,128)} %copy-done.2, ...), custom_call_target="tpu_custom_call" | custom-call | flops 603979776 | bytes 8299012 | tf_op jit(solution)/shard_map/pallas_call | solution.py:116
  250.5 4.5 %shard_map.242 = (f32[8,32,1280]{2,1,0:T(8,128)}, bf16[8,32,1280]{2,1,0:T(8,128)(2,1)}) custom-call(s32[16]{0:T(128)S(1)} %fusion.21.refs_0_, bf16[288,512]{1,0:T(8,128)(2,1)} %get-tuple-element.130.refs_1_, bf16[288,512]{1,0:T(8,128)(2,1)} %collective-permute-done.21.refs_2_, bf16[288,1024]{1,0:T(8,128)(2,1)S(1)} %copy-done.52, ...), custom_call_target="tpu_custom_call" | custom-call | flops 603979776 | bytes 2048068 | tf_op jit(solution)/shard_map/pallas_call | solution.py:116
  257.4 5.5 %shard_map.243 = (bf16[288,256]{1,0:T(8,128)(2,1)S(1)}, bf16[288,256]{1,0:T(8,128)(2,1)}, f32[288,512]{1,0:T(8,128)S(1)}, f32[16,2,512]{2,1,0:T(2,128)}) custom-call(s32[1]{0:T(128)} %bitcast.refs_0_.refs_9_, f32[288,512]{1,0:T(8,128)S(1)} %copy-done.31, f32[288,512]{1,0:T(8,128)} %copy-done.7, f32[4,512]{1,0:T(4,128)S(1)} %copy-done.43, ...), custom_call_target="tpu_custom_call" | custom-call | flops 1358954496 | bytes 6727684 | tf_op jit(solution)/shard_map/pallas_call | solution.py:116
  264.7 5.8 %all-to-all-start.8 = ((f32[16,2,512]{2,1,0:T(2,128)}), f32[16,2,512]{2,1,0:T(2,128)S(1)}, u32[]{:S(2)}, u32[]{:S(2)}) async-start(f32[16,2,512]{2,1,0:T(2,128)} %get-tuple-element.136.refs_5_), calls=%async_computation.8 | async-start | bytes 131072 | tf_op jit(solution)/shard_map/all_to_all | solution.py:225
  272.3 6.8 %shard_map.244 = (f32[8,288,256]{2,1,0:T(8,128)}, bf16[8,288,256]{2,1,0:T(8,128)(2,1)}) custom-call(s32[16]{0:T(128)S(1)} %fusion.21.refs_0_, bf16[288,4608]{1,0:T(8,128)(2,1)S(1)} %copy-done.11, bf16[288,4608]{1,0:T(8,128)(2,1)} %collective-permute-done.26.refs_2_, bf16[288,256]{1,0:T(8,128)(2,1)S(1)} %get-tuple-element.139.refs_3_, ...), custom_call_target="tpu_custom_call" | custom-call | flops 1358954496 | bytes 5603392 | tf_op jit(solution)/shard_map/pallas_call | solution.py:116
  307.8 8.2 %collective-permute-done.33.refs_1_ = bf16[8,288,256]{2,1,0:T(8,128)(2,1)S(1)} collective-permute-done((bf16[8,288,256]{2,1,0:T(8,128)(2,1)}, bf16[8,288,256]{2,1,0:T(8,128)(2,1)S(1)}, u32[]{:S(2)}, u32[]{:S(2)}) %collective-permute-start.33) | collective-permute-done | bytes 1179680 | tf_op jit(solution)/shard_map/ppermute | solution.py:216
  357.3 5.9 %collective-permute-start.42 = (f32[64,256]{1,0:T(8,128)S(1)}, f32[64,256]{1,0:T(8,128)S(1)}, u32[]{:S(2)}, u32[]{:S(2)}) collective-permute-start(f32[64,256]{1,0:T(8,128)S(1)} %dynamic-slice_bitcast_fusion.1), channel_id=1, source_target_pairs={{0,1},{1,0},{2,3},{3,2},{4,5},{5,4},{6,7},{7,6},{8,9},{9,8},{10,11... | collective-permute-start | bytes 196616 | tf_op jit(solution)/shard_map/ppermute | solution.py:207
  363.2 8.0 %collective-permute-done.43 = bf16[1,288,256]{2,1,0:T(8,128)(2,1)S(1)} collective-permute-done((bf16[1,288,256]{2,1,0:T(8,128)(2,1)S(1)}, bf16[1,288,256]{2,1,0:T(8,128)(2,1)S(1)}, u32[]{:S(2)}, u32[]{:S(2)}) %collective-permute-start.43) | collective-permute-done | bytes 147488 | tf_op jit(solution)/shard_map/ppermute | solution.py:211
  (346 shorter events, 168.1 us)
Async XLA Ops:
  7.2 112.4 %all-gather.9.cloned.1.call-start = ((), (), s32[]{:S(2)}) async-start(), calls=%async_computation.11 | async-start | bytes 4734976 | tf_op jit(solution)/shard_map/all_gather | solution.py:1140
  24.3 13.6 %collective-permute-start.6 = (bf16[8,64,512]{2,1,0:T(8,128)(2,1)S(1)}, bf16[8,64,512]{2,1,0:T(8,128)(2,1)S(1)}, u32[]{:S(2)}, u32[]{:S(2)}) collective-permute-start(bf16[8,64,512]{2,1,0:T(8,128)(2,1)S(1)} %shard_map.224.refs_0_.refs_1_), channel_id=1, source_target_pairs={{0,4},{1,3},{2,6},{3,1},{4,0},{5,7},{6,2},{7,5},{8,12},{9,11},{10,... | collective-permute-start | bytes 1572872 | tf_op jit(solution)/shard_map/ppermute | solution.py:216
  38.1 12.8 %collective-permute-start.10 = (bf16[16,64,512]{2,1,0:T(8,128)(2,1)S(1)}, bf16[16,64,512]{2,1,0:T(8,128)(2,1)}, u32[]{:S(2)}, u32[]{:S(2)}) collective-permute-start(bf16[16,64,512]{2,1,0:T(8,128)(2,1)S(1)} %get-tuple-element.99.refs_2_), channel_id=1, source_target_pairs={{0,1},{1,0},{2,3},{3,2},{4,5},{5,4},{6,7},{7,6},{8,9},{9,8},{10,11... | collective-permute-start | bytes 3145736 | tf_op jit(solution)/shard_map/ppermute | solution.py:207
  41.4 14.4 %collective-permute-start.11 = (bf16[4,144,512]{2,1,0:T(8,128)(2,1)S(1)}, bf16[4,144,512]{2,1,0:T(8,128)(2,1)S(1)}, u32[]{:S(2)}, u32[]{:S(2)}) collective-permute-start(bf16[4,144,512]{2,1,0:T(8,128)(2,1)S(1)} %get-tuple-element.102.refs_1_.refs_0_), channel_id=1, source_target_pairs={{0,2},{1,5},{2,0},{3,7},{4,6},{5,1},{6,4},{7,3},{8,10},{9,13},{10,... | collective-permute-start | bytes 1769480 | tf_op jit(solution)/shard_map/ppermute | solution.py:216
  55.9 23.0 %collective-permute-start.15 = (bf16[8,144,512]{2,1,0:T(8,128)(2,1)S(1)}, bf16[8,144,512]{2,1,0:T(8,128)(2,1)S(1)}, u32[]{:S(2)}, u32[]{:S(2)}) collective-permute-start(bf16[8,144,512]{2,1,0:T(8,128)(2,1)S(1)} %get-tuple-element.103.refs_0_), channel_id=1, source_target_pairs={{0,4},{1,3},{2,6},{3,1},{4,0},{5,7},{6,2},{7,5},{8,12},{9,11},{10,... | collective-permute-start | bytes 3538952 | tf_op jit(solution)/shard_map/ppermute | solution.py:216
  91.8 17.6 %collective-permute-start.18 = (bf16[8,16,2304]{2,1,0:T(8,128)(2,1)S(1)}, bf16[8,16,2304]{2,1,0:T(8,128)(2,1)S(1)}, u32[]{:S(2)}, u32[]{:S(2)}) collective-permute-start(bf16[8,16,2304]{2,1,0:T(8,128)(2,1)S(1)} %shard_map.232.refs_0_), channel_id=1, source_target_pairs={{0,4},{1,3},{2,6},{3,1},{4,0},{5,7},{6,2},{7,5},{8,12},{9,11},{10,... | collective-permute-start | bytes 1769480 | tf_op jit(solution)/shard_map/ppermute | solution.py:216
  119.6 13.6 %collective-permute-start.20 = (bf16[16,64,2176]{2,1,0:T(8,128)(2,1)}, bf16[16,64,2176]{2,1,0:T(8,128)(2,1)}, u32[]{:S(2)}, u32[]{:S(2)}) collective-permute-start(bf16[16,64,2176]{2,1,0:T(8,128)(2,1)} %bitcast.74), channel_id=1, source_target_pairs={{0,1},{1,0},{2,3},{3,2},{4,5},{5,4},{6,7},{7,6},{8,9},{9,8},{10,11... | collective-permute-start | bytes 13369352 | tf_op jit(solution)/shard_map/ppermute | solution.py:207
  119.9 13.3 %all-to-all-start.2 = ((f32[16,2,2048]{2,1,0:T(2,128)}), f32[16,2,2048]{2,1,0:T(2,128)}, u32[]{:S(2)}, u32[]{:S(2)}) async-start(f32[16,2,2048]{2,1,0:T(2,128)} %copy-done.38), calls=%async_computation.2 | async-start | bytes 524288 | tf_op jit(solution)/shard_map/all_to_all | solution.py:225
  124.7 84.7 %all-gather.5.cloned.1.call-start = ((), (), s32[]{:S(2)}) async-start(), calls=%async_computation.9 | async-start | bytes 2228224 | tf_op jit(solution)/shard_map/all_gather | solution.py:1272
  148.3 122.3 %collective-permute-start.26 = (bf16[288,4608]{1,0:T(8,128)(2,1)}, bf16[288,4608]{1,0:T(8,128)(2,1)}, u32[]{:S(2)}, u32[]{:S(2)}) collective-permute-start(bf16[288,4608]{1,0:T(8,128)(2,1)} %get-tuple-element.138.refs_1_), channel_id=1, source_target_pairs={{0,1},{1,0},{2,3},{3,2},{4,5},{5,4},{6,7},{7,6},{8,9},{9,8},{10,11... | collective-permute-start | bytes 7962632 | tf_op jit(solution)/shard_map/ppermute | solution.py:207
  160.2 12.9 %all-to-all-start.4 = ((bf16[16,32,128]{2,1,0:T(8,128)(2,1)}), bf16[16,32,128]{2,1,0:T(8,128)(2,1)S(1)}, u32[]{:S(2)}, u32[]{:S(2)}) async-start(bf16[16,32,128]{2,1,0:T(8,128)(2,1)} %get-tuple-element.113), calls=%async_computation.4 | async-start | bytes 262144 | tf_op jit(solution)/shard_map/all_to_all | solution.py:1233
  225.0 110.1 %all-gather.7.cloned.1.call-start = ((), (), s32[]{:S(2)}) async-start(), calls=%async_computation.10 | async-start | bytes 2228224 | tf_op jit(solution)/shard_map/all_gather | solution.py:1300
  243.7 42.3 %collective-permute-start.25 = (bf16[288,2048]{1,0:T(8,128)(2,1)S(1)}, bf16[288,2048]{1,0:T(8,128)(2,1)}, u32[]{:S(2)}, u32[]{:S(2)}) collective-permute-start(bf16[288,2048]{1,0:T(8,128)(2,1)S(1)} %bitcast.54), channel_id=1, source_target_pairs={{0,1},{1,0},{2,3},{3,2},{4,5},{5,4},{6,7},{7,6},{8,9},{9,8},{10,11... | collective-permute-start | bytes 3538952 | tf_op jit(solution)/shard_map/ppermute | solution.py:207
  264.7 14.4 %all-to-all-start.8 = ((f32[16,2,512]{2,1,0:T(2,128)}), f32[16,2,512]{2,1,0:T(2,128)S(1)}, u32[]{:S(2)}, u32[]{:S(2)}) async-start(f32[16,2,512]{2,1,0:T(2,128)} %get-tuple-element.136.refs_5_), calls=%async_computation.8 | async-start | bytes 131072 | tf_op jit(solution)/shard_map/all_to_all | solution.py:225
  291.6 36.6 %collective-permute-start.31 = (f32[144,2048]{1,0:T(8,128)}, f32[144,2048]{1,0:T(8,128)}, u32[]{:S(2)}, u32[]{:S(2)}) collective-permute-start(f32[144,2048]{1,0:T(8,128)} %get-tuple-element.124.refs_2_), channel_id=1, source_target_pairs={{0,1},{1,0},{2,3},{3,2},{4,5},{5,4},{6,7},{7,6},{8,9},{9,8},{10,11... | collective-permute-start | bytes 3538952 | tf_op jit(solution)/shard_map/ppermute | solution.py:207
  292.3 23.7 %collective-permute-start.33 = (bf16[8,288,256]{2,1,0:T(8,128)(2,1)}, bf16[8,288,256]{2,1,0:T(8,128)(2,1)S(1)}, u32[]{:S(2)}, u32[]{:S(2)}) collective-permute-start(bf16[8,288,256]{2,1,0:T(8,128)(2,1)} %get-tuple-element.158), channel_id=1, source_target_pairs={{0,4},{1,3},{2,6},{3,1},{4,0},{5,7},{6,2},{7,5},{8,12},{9,11},{10,... | collective-permute-start | bytes 3538952 | tf_op jit(solution)/shard_map/ppermute | solution.py:216
  304.7 19.5 %collective-permute-start.30 = (f32[10496]{0:T(1024)}, f32[10496]{0:T(1024)}, u32[]{:S(2)}, u32[]{:S(2)}) collective-permute-start(f32[10496]{0:T(1024)} %pad_maximum_fusion.4), channel_id=1, source_target_pairs={{0,1},{1,0},{2,3},{3,2},{4,5},{5,4},{6,7},{7,6},{8,9},{9,8},{10,11... | collective-permute-start | bytes 125960 | tf_op jit(solution)/shard_map/ppermute | solution.py:207
  305.5 24.3 %collective-permute-start.32 = (bf16[144,512]{1,0:T(8,128)(2,1)}, bf16[144,512]{1,0:T(8,128)(2,1)S(1)}, u32[]{:S(2)}, u32[]{:S(2)}) collective-permute-start(bf16[144,512]{1,0:T(8,128)(2,1)} %get-tuple-element.155), channel_id=1, source_target_pairs={{0,1},{1,0},{2,3},{3,2},{4,5},{5,4},{6,7},{7,6},{8,9},{9,8},{10,11... | collective-permute-start | bytes 442376 | tf_op jit(solution)/shard_map/ppermute | solution.py:207
  321.0 16.1 %collective-permute-start.49 = (bf16[1,32,1280]{2,1,0:T(8,128)(2,1)}, bf16[1,32,1280]{2,1,0:T(8,128)(2,1)S(1)}, u32[]{:S(2)}, u32[]{:S(2)}) collective-permute-start(bf16[1,32,1280]{2,1,0:T(8,128)(2,1)} %get-tuple-element.180), channel_id=1, source_target_pairs={{0,24},{2,26},{4,28},{6,30},{8,16},{10,18},{12,20},{14,22},{16,8},... | collective-permute-start | bytes 245768 | tf_op jit(solution)/shard_map/ppermute | solution.py:211
  324.2 15.0 %collective-permute-start.48 = (bf16[1,32,1280]{2,1,0:T(8,128)(2,1)}, bf16[1,32,1280]{2,1,0:T(8,128)(2,1)}, u32[]{:S(2)}, u32[]{:S(2)}) collective-permute-start(bf16[1,32,1280]{2,1,0:T(8,128)(2,1)} %get-tuple-element.179), channel_id=1, source_target_pairs={{0,8},{2,10},{4,12},{6,14},{8,0},{10,2},{12,4},{14,6},{16,24},{18,... | collective-permute-start | bytes 245768 | tf_op jit(solution)/shard_map/ppermute | solution.py:211
  324.2 15.0 %collective-permute-start.47 = (bf16[1,32,1280]{2,1,0:T(8,128)(2,1)}, bf16[1,32,1280]{2,1,0:T(8,128)(2,1)}, u32[]{:S(2)}, u32[]{:S(2)}) collective-permute-start(bf16[1,32,1280]{2,1,0:T(8,128)(2,1)} %get-tuple-element.178), channel_id=1, source_target_pairs={{0,16},{2,18},{4,20},{6,22},{8,24},{10,26},{12,28},{14,30},{16,0},... | collective-permute-start | bytes 245768 | tf_op jit(solution)/shard_map/ppermute | solution.py:211
  328.3 16.8 %collective-permute-start.37 = (bf16[4,128,256]{2,1,0:T(8,128)(2,1)}, bf16[4,128,256]{2,1,0:T(8,128)(2,1)}, u32[]{:S(2)}, u32[]{:S(2)}) collective-permute-start(bf16[4,128,256]{2,1,0:T(8,128)(2,1)} %get-tuple-element.165), channel_id=1, source_target_pairs={{0,2},{1,5},{2,0},{3,7},{4,6},{5,1},{6,4},{7,3},{8,10},{9,13},{10,... | collective-permute-start | bytes 786440 | tf_op jit(solution)/shard_map/ppermute | solution.py:216
  356.8 14.3 %collective-permute-start.43 = (bf16[1,288,256]{2,1,0:T(8,128)(2,1)S(1)}, bf16[1,288,256]{2,1,0:T(8,128)(2,1)S(1)}, u32[]{:S(2)}, u32[]{:S(2)}) collective-permute-start(bf16[1,288,256]{2,1,0:T(8,128)(2,1)S(1)} %copy-done.71), channel_id=1, source_target_pairs={{0,16},{2,18},{4,20},{6,22},{8,24},{10,26},{12,28},{14,30},{16,0},... | collective-permute-start | bytes 442376 | tf_op jit(solution)/shard_map/ppermute | solution.py:211
  357.3 15.4 %collective-permute-start.42 = (f32[64,256]{1,0:T(8,128)S(1)}, f32[64,256]{1,0:T(8,128)S(1)}, u32[]{:S(2)}, u32[]{:S(2)}) collective-permute-start(f32[64,256]{1,0:T(8,128)S(1)} %dynamic-slice_bitcast_fusion.1), channel_id=1, source_target_pairs={{0,1},{1,0},{2,3},{3,2},{4,5},{5,4},{6,7},{7,6},{8,9},{9,8},{10,11... | collective-permute-start | bytes 196616 | tf_op jit(solution)/shard_map/ppermute | solution.py:207
  (111 other events, 884.3 us)
Sparse Core Ops, SparseCore 0:
  24.4 94.9 all-gather.8
  143.7 65.6 all-gather.4
  229.2 62.9 all-gather.6

commit v4 on v3

--- a/solution.py
+++ b/solution.py
@@ -166,41 +166,28 @@
     return kernel_call(hold_kernel, [(values.shape, values.dtype)], [values], after=after)[0]
 
 
-def add_parts_kernel(parts, *refs):
-    ins, outs = refs[: 2 * len(parts)], refs[2 * len(parts) :]
-    for k, count in enumerate(parts):
-        kept, received = ins[2 * k : 2 * k + 2]
-        kept_out, *sent = outs[: count]
-        outs = outs[count:]
-        length = kept_out.shape[0]
-
-        def move(i, carry):
-            kept_out[i] = kept[i].astype(jnp.float32) + received[i].astype(jnp.float32)
-            for j, sent_out in enumerate(sent):
-                place = i + (j + 1) * length
-                total = kept[place].astype(jnp.float32) + received[place].astype(jnp.float32)
-                sent_out[i] = total.astype(jnp.bfloat16)
-            return carry
-
-        lax.fori_loop(0, length, move, 0)
-
-
-def add_parts(pairs, parts, after=()):
-    outs = []
-    for (kept, _), count in zip(pairs, parts):
-        shape = (kept.shape[0] // count,) + kept.shape[1:]
-        outs += [(shape, jnp.float32, PUT_FAR)] + [(shape, jnp.bfloat16, PUT_FAR)] * (count - 1)
-    found = kernel_call(
-        lambda *refs: add_parts_kernel(parts, *refs),
-        outs,
-        [Loaded(array) for pair in pairs for array in pair],
+def add_parts_kernel(kept, received, *totals):
+    length = totals[0].shape[0]
+
+    def move(i, carry):
+        for k, out_ref in enumerate(totals):
+            place = i + k * length
+            total = kept[place].astype(jnp.float32) + received[place].astype(jnp.float32)
+            out_ref[i] = total.astype(out_ref.dtype)
+        return carry
+
+    lax.fori_loop(0, length, move, 0)
+
+
+def add_parts(kept, received, count, after=()):
+    shape = (kept.shape[0] // count,) + kept.shape[1:]
+    kept, *sent = kernel_call(
+        add_parts_kernel,
+        [(shape, jnp.float32, PUT_FAR)] + [(shape, jnp.bfloat16, PUT_FAR)] * (count - 1),
+        [Loaded(kept), Loaded(received)],
         after=after,
     )
-    result = []
-    for count in parts:
-        result.append((found[0], list(found[1:count])))
-        found = found[count:]
-    return result
+    return kept, sent
 
 
 def swap_cores(values):
@@ -278,31 +265,18 @@
         self.kept = kept
         sent, _ = lax.optimization_barrier((sent, before))
         self.received = flip_both(sent, XY_BITS[1], size)
-        self.step = 0
-
-    @property
-    def parts(self):
-        return (2, 4)[self.step]
-
-    def send(self, kept, sent):
-        self.kept = kept
-        if self.step == 0:
-            self.received = flip_both(sent[0], XY_BITS[0], self.size)
-        else:
-            self.received = [flip_dp(part, bits, self.size) for part, bits in zip(sent, Z_BITS)]
-        self.step += 1
+
+    def second(self, after=()):
+        self.kept, sent = add_parts(self.kept, self.received, 2, after)
+        self.received = flip_both(sent[0], XY_BITS[0], self.size)
+
+    def third(self, after=()):
+        self.kept, sent = add_parts(self.kept, self.received, 4, after)
+        self.received = [flip_dp(part, bits, self.size) for part, bits in zip(sent, Z_BITS)]
 
     def finish(self):
         one, two, three = (part[0].astype(jnp.float32) for part in self.received)
         return (self.kept[0] + one) + (two + three)
-
-
-def scatter_step(sums, after=()):
-    found = add_parts(
-        [(one.kept, one.received) for one in sums], [one.parts for one in sums], after
-    )
-    for one, (kept, sent) in zip(sums, found):
-        one.send(kept, sent)
 
 
 @dataclasses.dataclass
@@ -448,13 +422,25 @@
     return Scattering(kept, sent, size, before)
 
 
-def swap_columns(total):
+def swap_columns(*totals):
     me = lax.axis_index("shard")
-    half = total.shape[0] // 2
-    mine = lax.dynamic_slice_in_dim(total, me * half, half, 0)
-    other = swap_cores(lax.dynamic_slice_in_dim(total, (1 - me) * half, half, 0))
+
+    def half_of(core):
+        halves = [total.shape[0] // 2 for total in totals]
+        return jnp.concatenate(
+            [
+                lax.dynamic_slice_in_dim(total, core * half, half, 0)
+                for total, half in zip(totals, halves)
+            ]
+        )
+
+    mine, other = half_of(me), swap_cores(half_of(1 - me))
     first, second = jnp.where(me == 0, mine, other), jnp.where(me == 0, other, mine)
-    return jnp.concatenate([first, second], 1)
+    both, found, start = jnp.concatenate([first, second], 1), [], 0
+    for total in totals:
+        found.append(both[start : start + total.shape[0] // 2])
+        start += total.shape[0] // 2
+    return found
 
 
 def tiles(rows, width, high, wide):
@@ -669,11 +655,12 @@
 ):
     head_terms, head_back, pre_terms, *refs = refs
     inputs, refs = refs[:weights], refs[weights:]
-    low_ref, own_ref, other_ref, sums_ref, weight, sems = refs
+    low_ref, own_ref, other_ref, sums_ref, total_ref, weight, sems = refs
     wait = fetch_weight(inputs, weight, sems, CHUNKS)
     step = D // CHUNKS
     head_factors = norm_factors(head_terms, norm_ref, 2, crop_count)
     totals = jnp.sum(head_back[...], 0)
+    total_ref[...] = totals
     for columns in (slice(k, k + 512) for k in range(0, D, 512)):
         unit, _ = normalize(head_pre_ref[:, columns], head_factors, columns)
         grad = norm_backward(
@@ -714,9 +701,11 @@
 def expand_back_kernel(
     count, core, own_ref, other_ref, pre_ref, wide_ref, weight_ref, before_ref, mid_ref, bias_ref, *refs
 ):
-    pre_terms, back_terms, before_terms, kept_ref, sent_ref, out_ref, sums_ref, low_ref = refs
+    pre_terms, back_terms, before_terms, *refs = refs
+    kept_ref, sent_ref, out_ref, sums_ref, total_ref, low_ref = refs
     factors = norm_factors(pre_terms, wide_ref, 0, count)
     totals = jnp.sum(back_terms[...], 0)
+    total_ref[...] = totals
     own_rows = own_ref.shape[0]
     for rows, columns in tiles(2 * own_rows, D, 48, 512):
         unit, _ = normalize(pre_ref[rows, columns], factors, columns)
@@ -744,10 +733,12 @@
 def spatial_back_kernel(
     count, core, grad_ref, pre_ref, norm_ref, weight_ref, before_ref, valid_ref, *refs
 ):
-    pre_terms, back_terms, before_terms, kept_ref, sent_ref, out_ref, sums_ref, slots, low_ref = refs
+    pre_terms, back_terms, before_terms, *refs = refs
+    kept_ref, sent_ref, out_ref, sums_ref, total_ref, slots, low_ref = refs
     rows = grad_ref.shape[0]
     factors = norm_factors(pre_terms, norm_ref, 2, count)
     totals = jnp.sum(back_terms[...], 0)
+    total_ref[...] = totals
     for high, columns in tiles(rows, MID, 48, 512):
         unit, _ = normalize(pre_ref[high, columns], factors, columns)
         grad = norm_backward(grad_ref[high, columns], unit, factors, totals, count, columns)
@@ -789,10 +780,12 @@
     other_ref,
     kept_ref,
     sent_ref,
+    total_ref,
 ):
     rows = grad_ref.shape[0]
     factors = norm_factors(pre_terms, norm_ref, 0, count)
     totals = jnp.sum(back_terms[...], 0)
+    total_ref[...] = totals
     for high, columns in tiles(rows, MID, 48, 512):
         unit, _ = normalize(pre_ref[high, columns], factors, columns)
         grad = norm_backward(grad_ref[high, columns], unit, factors, totals, count, columns)
@@ -826,6 +819,14 @@
         for pixel in range(SIDE * SIDE):
             rows = slice(pixel * canvas_count, (pixel + 1) * canvas_count)
             out_ref[micro, pixel // SIDE, pixel % SIDE] = rows_ref[rows, :]
+
+
+def proto_grad_kernel(first_ref, second_ref, out_ref):
+    rows = out_ref.shape[0]
+    for k in range(0, rows, 128):
+        stop = min(k + 128, rows)
+        total = first_ref[:, k : k + 128] + second_ref[:, k : k + 128]
+        out_ref[k:stop, :] = total.T[: stop - k, :]
 
 
 def inside_canvas(own_canvases):
@@ -957,7 +958,6 @@
         lax.fori_loop(0, rows_all // 64, both, 0)
 
     column_factors(SINK_ITERS - 1)
-    proto_grad_ref[...] = jnp.zeros_like(proto_grad_ref)
     loss_ref[...] = jnp.zeros_like(loss_ref)
     block = 128
 
@@ -967,6 +967,7 @@
         row = lax.broadcasted_iota(jnp.int32, (block, block), 0)
         column = lax.broadcasted_iota(jnp.int32, (block, block), 1)
         pick = (column == (row // CROPS) * CROPS + partner_ref[rows, :]).astype(jnp.bfloat16)
+        pick = jnp.concatenate([pick, pick], 1)
         heat_part = jnp.zeros((block, 128), jnp.float32)
         target_part = jnp.zeros((block, 128), jnp.float32)
         loss_part = jnp.zeros((block, 128), jnp.float32)
@@ -978,7 +979,7 @@
             codes = divided(SINK_ITERS - 1, rows, columns) * inverse
             high = codes.astype(jnp.bfloat16)
             rest = (codes - high.astype(jnp.float32)).astype(jnp.bfloat16)
-            target = product(pick, high) + product(pick, rest)
+            target = product(pick, jnp.concatenate([high, rest], 0))
             codes_ref[rows, columns] = target
             target_part += fold(target)
             loss_part += fold(target * score)
@@ -992,12 +993,12 @@
         ratio = target_sum / heat_sum * factor
         for columns in chunks:
             grad = heat_ref[:, columns] * ratio - codes_ref[rows, columns] * factor
-            low = grad.astype(jnp.bfloat16)
-            score_ref[rows, columns] = low
-            proto_grad_ref[:, columns] += product_t(units_ref[rows, :], low)
+            score_ref[rows, columns] = grad.astype(jnp.bfloat16)
         return carry
 
     lax.fori_loop(0, crops // block, last, 0)
+    for columns in chunks:
+        proto_grad_ref[:, columns] = product_t(units_ref[...], score_ref[:, columns])
     mine = pl.ds(pl.multiple_of(place[0], own), own)
     unit_grad_ref[...] = product(score_ref[mine, :], proto_ref[...])
 
@@ -1272,9 +1273,9 @@
     left = lax.all_gather(pooled_low, "dp", axis=0, tiled=True)
 
     own_part = ((own_rows, D), f32)
-    head_low, own_grad, other_grad, sums = kernel_call(
+    head_low, own_grad, other_grad, sums, total_head = kernel_call(
         lambda *refs: pool_back_kernel(head.count, crop_total, pixel_total, *refs),
-        [((local_crops, D), bf16), own_part, own_part, wide_sums],
+        [((local_crops, D), bf16), own_part, own_part, wide_sums, ((2, D), f32)],
         [
             head_act_grad,
             pre_head,
@@ -1302,9 +1303,9 @@
     def low_halves(width):
         return [((local_rows, width // 2), bf16)] * 2
 
-    three_kept, three_sent, two_act_grad, sums = kernel_call(
+    three_kept, three_sent, two_act_grad, sums, total_three = kernel_call(
         lambda *refs: expand_back_kernel(pixel_total, *refs),
-        [*low_halves(D), mid_rows, ((copies, 2, MID + proj), f32)],
+        [*low_halves(D), mid_rows, ((copies, 2, MID + proj), f32), ((2, D), f32)],
         [
             core,
             own_grad,
@@ -1340,9 +1341,9 @@
         )
         before_two = [expand_sum.kept]
 
-    two_kept, two_sent, one_act_grad, sums = kernel_call(
+    two_kept, two_sent, one_act_grad, sums, total_two = kernel_call(
         lambda *refs: spatial_back_kernel(pixel_total, *refs),
-        [*low_halves(MID), mid_rows, mid_sums],
+        [*low_halves(MID), mid_rows, mid_sums, ((2, MID + proj), f32)],
         [
             core,
             two_act_grad,
@@ -1362,7 +1363,6 @@
         flops=2 * local_rows * 9 * MID * MID,
         after=before_two,
     )
-    back_one = terms_over_dp(sums)
     before_one = []
     if by_steps:
         spatial_sum = weight_grad(
@@ -1371,36 +1371,64 @@
             chip_slots,
             size,
             two_kept,
-            after=[sums],
+            after=[expand_sum.received],
         )
-        before_one = [spatial_sum.kept]
-
-    one_low, other_low, one_kept, one_sent = kernel_call(
+        expand_sum.second(after=[spatial_sum.kept])
+        sums, _ = lax.optimization_barrier((sums, spatial_sum.kept))
+        before_one = [expand_sum.kept]
+
+    back_one = terms_over_dp(sums)
+    one_low, other_low, one_kept, one_sent, total_one = kernel_call(
         lambda *refs: reduce_back_kernel(pixel_total, *refs),
-        [((local_rows, MID), bf16), ((own_rows, MID), bf16), *low_halves(MID)],
+        [
+            ((local_rows, MID), bf16),
+            ((own_rows, MID), bf16),
+            *low_halves(MID),
+            ((2, MID), f32),
+        ],
         [core, one_act_grad, Streamed(pre_one), norm_mid, terms_one, back_one],
         after=before_one,
     )
     if by_steps:
-        scatter_step([expand_sum])
+        spatial_sum.second([one_low])
         reduce_sum = weight_grad(
             (input_rows, swap_cores(input_rows)),
             (one_kept, swap_cores(one_sent)),
             chip_slots,
             size,
             one_low,
+            after=[spatial_sum.kept, right],
         )
-        scatter_step([spatial_sum, expand_sum])
-        scatter_step([reduce_sum])
-        last = reduce_sum.kept
-        other_low, _ = lax.optimization_barrier((other_low, last))
+
+    proto_other = swap_cores(proto_part)
+    other_low = swap_cores(other_low)
+    late = []
+    if by_steps:
+        expand_sum.third([reduce_sum.kept])
+        spatial_sum.third([expand_sum.kept])
+        reduce_sum.second([spatial_sum.kept])
+        late = [reduce_sum.kept]
+    by_pixel = kernel_call(
+        input_grad_kernel,
+        [((MICRO, SIDE, SIDE, own_canvases, D), f32)],
+        [core, own_grad, peer_grad, one_low, other_low, full_reduce],
+        scratch=[pltpu.VMEM((own_rows, D), f32)],
+        flops=2 * local_rows * D * MID,
+        after=late,
+    )[0]
+    if by_steps:
+        reduce_sum.third([by_pixel])
+        late = [reduce_sum.kept]
+    left, right, _ = lax.optimization_barrier((left, right, late))
+    if gathered_codes:
+        proto_grad = kernel_call(
+            proto_grad_kernel,
+            [(prototypes.shape, f32)],
+            [Loaded(proto_part), Loaded(proto_other)],
+            after=late,
+        )[0]
     else:
-        last = one_low
-
-    proto_part, left, right, _ = lax.optimization_barrier((proto_part, left, right, last))
-    if gathered_codes:
-        proto_part = proto_part[:, :PROTOS]
-    proto_grad = (proto_part + swap_cores(proto_part)).T
+        proto_grad = (proto_part + proto_other).T
     chip_rows = 2 * w_hidden.shape[0]
     hidden_part = product_t(
         lax.dynamic_slice_in_dim(left, me_dp * chip_rows, chip_rows, 1), right
@@ -1413,20 +1441,10 @@
         return mine + swap_cores(other)
 
     grad_hidden = own_half(hidden_part)
-    by_pixel = kernel_call(
-        input_grad_kernel,
-        [((MICRO, SIDE, SIDE, own_canvases, D), f32)],
-        [core, own_grad, peer_grad, one_low, swap_cores(other_low), full_reduce],
-        scratch=[pltpu.VMEM((own_rows, D), f32)],
-        flops=2 * local_rows * D * MID,
-    )[0]
-
     if by_steps:
-        scatter_step([spatial_sum, reduce_sum], [by_pixel, proto_grad])
-        grad_reduce = swap_columns(reduce_sum.finish())
-        grad_spatial = swap_columns(spatial_sum.finish())
+        grad_spatial, grad_reduce = swap_columns(spatial_sum.finish(), reduce_sum.finish())
         total = expand_sum.finish()
-        grad_expand = swap_columns(total[:, : D // 2])
+        (grad_expand,) = swap_columns(total[:, : D // 2])
         grad_project = jnp.concatenate(
             [total[:, k : k + proj] for k in range(D // 2, total.shape[1], proj)], 0
         )
@@ -1447,8 +1465,8 @@
             product_t(act_head, embed_low), BOTH, scatter_dimension=0, tiled=True
         )
 
-    backs, _ = lax.optimization_barrier(((back_one, back_two, back_three, back_head), last))
-    total_one, total_two, total_three, total_head = (jnp.sum(back, 0) for back in backs)
+    totals = (total_one, total_two, total_three, total_head)
+    (total_one, total_two, total_three, total_head), _ = lax.optimization_barrier((totals, late))
     narrow = jnp.concatenate(
         [
             jnp.stack([total_one[1], total_one[0], total_two[1, :MID], total_two[0, :MID]])

time: 385 us -> 379 us (0.984)
  waiting for transfers between devices: 70.8 us -> 52.3 us
  local copies, waits for them, and re-layouts: 37.7 us -> 45.2 us
  blocking collectives: 52.7 us -> 59.5 us
    ppermute x12, waiting for transfers between devices: 15.7 us -> 3.64 us  [flip_both(): return lax.ppermute(values, BOTH, pairs)]
    ppermute x22 -> x21, starting transfers between devices: 24.4 us -> 35.4 us  [swap_cores(): return lax.ppermute(values, 'shard', [(0, 1), (1, 0)])]
    unnamed x150 -> x156, local copies, waits for them, and re-layouts: 31.7 us -> 39.7 us
    ppermute x12, starting transfers between devices: 13.6 us -> 6.65 us  [flip_both(): return lax.ppermute(values, BOTH, pairs)]
    all_to_all x5 -> x4, starting transfers between devices: 23.4 us -> 16.4 us  [terms_over_dp(): return lax.all_to_all(copies, 'dp', 0, 0)]
    all_to_all x3 -> x4, blocking collectives: 52.7 us -> 59.5 us  [terms_over_dp(): return lax.all_to_all(copies, 'dp', 0, 0)]
    pallas_call x31 -> x34, Pallas kernels: 98.3 us -> 101 us  [kernel_call(): pl.pallas_call(kernel, out_shape=[jax.ShapeDtypeStruct(*out) if len(out)...]
    all_to_all x5 -> x4, waiting for transfers between devices: 20.8 us -> 18.5 us  [terms_over_dp(): return lax.all_to_all(copies, 'dp', 0, 0)]
  transfers between devices with their start and end apart: 61 -> 59, of which waited for: 20 -> 16; matrix products, arithmetic and copies ran while one was open for 4% -> 4% of each run, Pallas kernels for 24% -> 25%
where the time goes in v4:
time: 379 us; the launch traced here: 377 us
  Pallas kernels  101 us (27%)
  starting transfers between devices  93.8 us (25%)
  blocking collectives  59.5 us (16%)
  waiting for transfers between devices  52.3 us (14%)
  local copies, waits for them, and re-layouts  45.2 us (12%)
  between operations  16.5 us (4%)
  other arithmetic  7.46 us (2%)
    pallas_call x34, Pallas kernels, kernel_call(): pl.pallas_call(kernel, out_shape=[jax.ShapeDtypeStruct(*out) if len(out)...  101 us
    all_to_all x4, blocking collectives, terms_over_dp(): return lax.all_to_all(copies, 'dp', 0, 0)  59.5 us
    unnamed x156, local copies, waits for them, and re-layouts  39.7 us
    ppermute x21, starting transfers between devices, swap_cores(): return lax.ppermute(values, 'shard', [(0, 1), (1, 0)])  35.4 us
    ppermute x18, starting transfers between devices, flip_dp(): return lax.ppermute(values, 'dp', [(i, i ^ bits) for i in range(size)])  29.2 us
    all_to_all x4, waiting for transfers between devices, terms_over_dp(): return lax.all_to_all(copies, 'dp', 0, 0)  18.5 us
    all_to_all x4, starting transfers between devices, terms_over_dp(): return lax.all_to_all(copies, 'dp', 0, 0)  16.4 us
    ppermute x18, waiting for transfers between devices, flip_dp(): return lax.ppermute(values, 'dp', [(i, i ^ bits) for i in range(size)])  14 us
  transfers between devices with their start and end apart: 59, of which 16 were waited for; matrix products, arithmetic and copies ran while one was open for 4% of the time, Pallas kernels for 25%

profile of v4, /device:TPU:1, one launch (start us, length us, event | category | flops | bytes accessed | tf_op | source)
XLA Modules:
  0.0 376.8 jit_solution(4549702793540021201)
XLA Ops:
  32.8 5.2 %collective-permute-done.9.refs_5_ = bf16[1,144,512]{2,1,0:T(8,128)(2,1)S(1)} collective-permute-done((bf16[1,144,512]{2,1,0:T(8,128)(2,1)S(1)}, bf16[1,144,512]{2,1,0:T(8,128)(2,1)S(1)}, u32[]{:S(2)}, u32[]{:S(2)}) %collective-permute-start.9) | collective-permute-done | bytes 147488 | tf_op jit(solution)/shard_map/ppermute | solution.py:198
  38.1 4.6 %collective-permute-start.10 = (bf16[16,64,512]{2,1,0:T(8,128)(2,1)S(1)}, bf16[16,64,512]{2,1,0:T(8,128)(2,1)}, u32[]{:S(2)}, u32[]{:S(2)}) collective-permute-start(bf16[16,64,512]{2,1,0:T(8,128)(2,1)S(1)} %get-tuple-element.102.refs_2_), channel_id=1, source_target_pairs={{0,1},{1,0},{2,3},{3,2},{4,5},{5,4},{6,7},{7,6},{8,9},{9,8},{10,11... | collective-permute-start | bytes 3145736 | tf_op jit(solution)/shard_map/ppermute | solution.py:194
  43.0 9.0 %collective-permute-start.12 = (bf16[1,16,2304]{2,1,0:T(8,128)(2,1)S(1)}, bf16[1,16,2304]{2,1,0:T(8,128)(2,1)S(1)}, u32[]{:S(2)}, u32[]{:S(2)}) collective-permute-start(bf16[1,16,2304]{2,1,0:T(8,128)(2,1)S(1)} %bitcast.60), channel_id=1, source_target_pairs={{0,16},{2,18},{4,20},{6,22},{8,24},{10,26},{12,28},{14,30},{16,0},... | collective-permute-start | bytes 221192 | tf_op jit(solution)/shard_map/ppermute | solution.py:198
  60.4 18.7 %all_to_all.45.refs_2_.refs_3_.refs_9_.refs_4_ = f32[16,2,512]{2,1,0:T(2,128)S(1)} all-to-all(f32[16,2,512]{2,1,0:T(2,128)S(1)} %get-tuple-element.104.refs_6_), channel_id=1, replica_groups=mesh['dp'=16,'shard'=2] {'dp'}, dimensions={0} | all-to-all | bytes 131072 | tf_op jit(solution)/shard_map/all_to_all | solution.py:212
  85.4 6.4 %shard_map.231 = (f32[288,512]{1,0:T(8,128)S(1)}, f32[16,2,512]{2,1,0:T(2,128)S(1)}, bf16[288,4608]{1,0:T(8,128)(2,1)}, bf16[4608,512]{1,0:T(8,128)(2,1)}) custom-call(f32[288,512]{1,0:T(8,128)S(1)} %get-tuple-element.103.refs_0_.refs_5_.refs_2_, f32[4,512]{1,0:T(4,128)S(1)} %copy-done.53, f32[288,16]{1,0:T(8,128)S(1)} %copy-done.43, ...), custom_call_target="tpu_custom_call" | custom-call | flops 1358954496 | bytes 5400704 | tf_op jit(solution)/shard_map/pallas_call | solution.py:116
  92.3 16.1 %all_to_all.46.refs_2_.refs_11_.refs_7_ = f32[16,2,512]{2,1,0:T(2,128)S(1)} all-to-all(f32[16,2,512]{2,1,0:T(2,128)S(1)} %get-tuple-element.108.refs_2_), channel_id=1, replica_groups=mesh['dp'=16,'shard'=2] {'dp'}, dimensions={0} | all-to-all | bytes 131072 | tf_op jit(solution)/shard_map/all_to_all | solution.py:212
  118.7 4.9 %all-to-all-start.2 = ((f32[16,2,2048]{2,1,0:T(2,128)}), f32[16,2,2048]{2,1,0:T(2,128)}, u32[]{:S(2)}, u32[]{:S(2)}) async-start(f32[16,2,2048]{2,1,0:T(2,128)} %copy-done.48), calls=%async_computation.2 | async-start | bytes 524288 | tf_op jit(solution)/shard_map/all_to_all | solution.py:212
  124.2 7.9 %all-to-all-done.2.refs_5_.refs_9_ = f32[16,2,2048]{2,1,0:T(2,128)} async-done(((f32[16,2,2048]{2,1,0:T(2,128)}), f32[16,2,2048]{2,1,0:T(2,128)}, u32[]{:S(2)}, u32[]{:S(2)}) %all-to-all-start.2) | async-done | bytes 262176 | tf_op jit(solution)/shard_map/all_to_all | solution.py:212
  134.2 5.3 %shard_map.236 = (bf16[32,2048]{1,0:T(8,128)(2,1)S(1)}, f32[32,2048]{1,0:T(8,128)S(1)}, f32[16,2,2048]{2,1,0:T(2,128)S(1)}, bf16[2048,128]{1,0:T(8,128)(2,1)S(1)}) custom-call(f32[288,2048]{1,0:T(8,128)S(1)} %get-tuple-element.110.refs_0_.refs_2_.refs_3_, bf16[288,2048]{1,0:T(8,128)(2,1)S(1)} %bitcast.48, f32[4,2048]{1,0:T(4,128)S(1)} %copy-done.33, ...), custom_call_target="tpu_custom_call" | custom-call | flops 268435456 | bytes 12765440 | tf_op jit(solution)/shard_map/pallas_call | solution.py:116
  142.4 12.2 %all_to_all.47.refs_4_.refs_6_.refs_7_ = f32[16,2,2048]{2,1,0:T(2,128)S(1)} all-to-all(f32[16,2,2048]{2,1,0:T(2,128)} %copy-done.50), channel_id=1, replica_groups=mesh['dp'=16,'shard'=2] {'dp'}, dimensions={0} | all-to-all | bytes 524288 | tf_op jit(solution)/shard_map/all_to_all | solution.py:212
  159.0 6.1 %all-to-all-start.4 = ((bf16[16,32,128]{2,1,0:T(8,128)(2,1)}), bf16[16,32,128]{2,1,0:T(8,128)(2,1)S(1)}, u32[]{:S(2)}, u32[]{:S(2)}) async-start(bf16[16,32,128]{2,1,0:T(8,128)(2,1)} %get-tuple-element.116), calls=%async_computation.4 | async-start | bytes 262144 | tf_op jit(solution)/shard_map/all_to_all | solution.py:1234
  165.1 6.7 %all-to-all-done.4 = bf16[16,32,128]{2,1,0:T(8,128)(2,1)S(1)} async-done(((bf16[16,32,128]{2,1,0:T(8,128)(2,1)}), bf16[16,32,128]{2,1,0:T(8,128)(2,1)S(1)}, u32[]{:S(2)}, u32[]{:S(2)}) %all-to-all-start.4) | async-done | bytes 131104 | tf_op jit(solution)/shard_map/all_to_all | solution.py:1234
  174.0 16.4 %shard_map.238 = (f32[8,128]{1,0:T(8,128)S(1)}, f32[128,3072]{1,0:T(8,128)S(1)}, f32[32,128]{1,0:T(8,128)S(1)}) custom-call(s32[2]{0:T(128)S(1)} %pad_add_fusion.1.refs_0_, bf16[512,128]{1,0:T(8,128)(2,1)S(1)} %bitcast.64, bf16[512,256]{1,0:T(8,128)(2,1)S(1)} %copy-done.67, bf16[3000,128]{1,0:T(8,128)(2,1)S(1)} %copy-done.61), custom_call_target="tpu_custom_call" | custom-call | flops 3221225472 | bytes 1161224 | tf_op jit(solution)/shard_map/pallas_call | solution.py:116
  201.9 5.5 %all-to-all-done.5.refs_8_ = f32[16,2,2048]{2,1,0:T(2,128)S(1)} async-done(((f32[16,2,2048]{2,1,0:T(2,128)}), f32[16,2,2048]{2,1,0:T(2,128)S(1)}, u32[]{:S(2)}, u32[]{:S(2)}) %all-to-all-start.5) | async-done | bytes 262176 | tf_op jit(solution)/shard_map/all_to_all | solution.py:212
  210.0 8.7 %shard_map.240 = (bf16[32,2048]{1,0:T(8,128)(2,1)}, f32[144,2048]{1,0:T(8,128)S(1)}, f32[144,2048]{1,0:T(8,128)S(1)}, f32[16,2,2048]{2,1,0:T(2,128)S(1)}, f32[2,2048]{1,0:T(2,128)S(1)}) custom-call(f32[32,2048]{1,0:T(8,128)S(1)} %copy-done.47, f32[32,2048]{1,0:T(8,128)S(1)} %copy-done.19, f32[288,2048]{1,0:T(8,128)} %copy-done.2, ...), custom_call_target="tpu_custom_call" | custom-call | flops 268435456 | bytes 13814016 | tf_op jit(solution)/shard_map/pallas_call | solution.py:116
  219.4 12.5 %all_to_all.48.refs_10_ = f32[16,2,2048]{2,1,0:T(2,128)S(1)} all-to-all(f32[16,2,2048]{2,1,0:T(2,128)} %copy-done.49), channel_id=1, replica_groups=mesh['dp'=16,'shard'=2] {'dp'}, dimensions={0} | all-to-all | bytes 524288 | tf_op jit(solution)/shard_map/all_to_all | solution.py:212
  232.0 5.8 %shard_map.241 = (bf16[288,1024]{1,0:T(8,128)(2,1)S(1)}, bf16[288,1024]{1,0:T(8,128)(2,1)}, f32[288,512]{1,0:T(8,128)S(1)}, f32[16,2,640]{2,1,0:T(2,128)}, f32[2,2048]{1,0:T(2,128)S(1)}) custom-call(s32[1]{0:T(128)} %bitcast.refs_0_.refs_9_, f32[144,2048]{1,0:T(8,128)S(1)} %get-tuple-element.124.refs_1_, f32[144,2048]{1,0:T(8,128)S(1)} %get-tuple-element.127.refs_2_, ...), custom_call_target="tpu_custom_call" | custom-call | flops 603979776 | bytes 8299012 | tf_op jit(solution)/shard_map/pallas_call | solution.py:116
  243.5 4.2 %all-to-all-start.7 = ((f32[16,2,640]{2,1,0:T(2,128)}), f32[16,2,640]{2,1,0:T(2,128)S(1)}, u32[]{:S(2)}, u32[]{:S(2)}) async-start(f32[16,2,640]{2,1,0:T(2,128)} %get-tuple-element.132.refs_10_), calls=%async_computation.7 | async-start | bytes 163840 | tf_op jit(solution)/shard_map/all_to_all | solution.py:212
  248.8 4.3 %shard_map.242 = (f32[8,32,1280]{2,1,0:T(8,128)}, bf16[8,32,1280]{2,1,0:T(8,128)(2,1)}) custom-call(s32[16]{0:T(128)S(1)} %fusion.23.refs_0_, bf16[288,512]{1,0:T(8,128)(2,1)S(1)} %copy-done.65, bf16[288,512]{1,0:T(8,128)(2,1)S(1)} %collective-permute-done.21.refs_2_, bf16[288,1024]{1,0:T(8,128)(2,1)S(1)} %copy-done.63, ...), custom_call_target="tpu_custom_call" | custom-call | flops 603979776 | bytes 2048068 | tf_op jit(solution)/shard_map/pallas_call | solution.py:116
  256.8 5.5 %shard_map.243 = (bf16[288,256]{1,0:T(8,128)(2,1)S(1)}, bf16[288,256]{1,0:T(8,128)(2,1)S(1)}, f32[288,512]{1,0:T(8,128)S(1)}, f32[16,2,512]{2,1,0:T(2,128)}, f32[2,640]{1,0:T(2,128)S(1)}) custom-call(s32[1]{0:T(128)} %bitcast.refs_0_.refs_9_, f32[288,512]{1,0:T(8,128)S(1)} %copy-done.40, f32[288,512]{1,0:T(8,128)} %copy-done.8, f32[4,512]{1,0:T(4,128)S(1)} %copy-done.54, ...), custom_call_target="tpu_custom_call" | custom-call | flops 1358954496 | bytes 6727684 | tf_op jit(solution)/shard_map/pallas_call | solution.py:116
  266.4 7.9 %shard_map.244 = (f32[8,288,256]{2,1,0:T(8,128)}, bf16[8,288,256]{2,1,0:T(8,128)(2,1)}) custom-call(s32[16]{0:T(128)S(1)} %fusion.23.refs_0_, bf16[288,4608]{1,0:T(8,128)(2,1)} %get-tuple-element.141.refs_1_, bf16[288,4608]{1,0:T(8,128)(2,1)} %collective-permute-done.25.refs_2_, bf16[288,256]{1,0:T(8,128)(2,1)S(1)} %get-tuple-element.142.refs_3_, ...), custom_call_target="tpu_custom_call" | custom-call | flops 1358954496 | bytes 5603392 | tf_op jit(solution)/shard_map/pallas_call | solution.py:116
  274.3 4.7 %collective-permute-start.28 = (bf16[288,2048]{1,0:T(8,128)(2,1)S(1)}, bf16[288,2048]{1,0:T(8,128)(2,1)}, u32[]{:S(2)}, u32[]{:S(2)}) collective-permute-start(bf16[288,2048]{1,0:T(8,128)(2,1)S(1)} %bitcast.50), channel_id=1, source_target_pairs={{0,1},{1,0},{2,3},{3,2},{4,5},{5,4},{6,7},{7,6},{8,9},{9,8},{10,11... | collective-permute-start | bytes 3538952 | tf_op jit(solution)/shard_map/ppermute | solution.py:194
  307.0 4.1 %shard_map.248 = (f32[8,128,256]{2,1,0:T(8,128)}, bf16[8,128,256]{2,1,0:T(8,128)(2,1)}) custom-call(s32[16]{0:T(128)S(1)} %fusion.23.refs_0_, bf16[288,2048]{1,0:T(8,128)(2,1)S(1)} %bitcast.51, bf16[288,2048]{1,0:T(8,128)(2,1)} %collective-permute-done.28.refs_2_, bf16[288,256]{1,0:T(8,128)(2,1)S(1)} %get-tuple-element.153.refs_3_, ...), custom_call_target="tpu_custom_call" | custom-call | flops 603979776 | bytes 2654272 | tf_op jit(solution)/shard_map/pallas_call | solution.py:116
  318.4 4.5 %collective-permute-start.35 = (f32[144,2048]{1,0:T(8,128)}, f32[144,2048]{1,0:T(8,128)S(1)}, u32[]{:S(2)}, u32[]{:S(2)}) collective-permute-start(f32[144,2048]{1,0:T(8,128)} %copy-done.29), channel_id=1, source_target_pairs={{0,1},{1,0},{2,3},{3,2},{4,5},{5,4},{6,7},{7,6},{8,9},{9,8},{10,11... | collective-permute-start | bytes 3538952 | tf_op jit(solution)/shard_map/ppermute | solution.py:194
  (345 shorter events, 173.0 us)
Async XLA Ops:
  7.2 111.3 %all-gather.9.cloned.1.call-start = ((), (), s32[]{:S(2)}) async-start(), calls=%async_computation.11 | async-start | bytes 4734976 | tf_op jit(solution)/shard_map/all_gather | solution.py:1141
  24.3 13.6 %collective-permute-start.6 = (bf16[8,64,512]{2,1,0:T(8,128)(2,1)S(1)}, bf16[8,64,512]{2,1,0:T(8,128)(2,1)S(1)}, u32[]{:S(2)}, u32[]{:S(2)}) collective-permute-start(bf16[8,64,512]{2,1,0:T(8,128)(2,1)S(1)} %shard_map.224.refs_0_.refs_1_), channel_id=1, source_target_pairs={{0,4},{1,3},{2,6},{3,1},{4,0},{5,7},{6,2},{7,5},{8,12},{9,11},{10,... | collective-permute-start | bytes 1572872 | tf_op jit(solution)/shard_map/ppermute | solution.py:203
  38.1 15.1 %collective-permute-start.10 = (bf16[16,64,512]{2,1,0:T(8,128)(2,1)S(1)}, bf16[16,64,512]{2,1,0:T(8,128)(2,1)}, u32[]{:S(2)}, u32[]{:S(2)}) collective-permute-start(bf16[16,64,512]{2,1,0:T(8,128)(2,1)S(1)} %get-tuple-element.102.refs_2_), channel_id=1, source_target_pairs={{0,1},{1,0},{2,3},{3,2},{4,5},{5,4},{6,7},{7,6},{8,9},{9,8},{10,11... | collective-permute-start | bytes 3145736 | tf_op jit(solution)/shard_map/ppermute | solution.py:194
  42.8 17.4 %collective-permute-start.11 = (bf16[4,144,512]{2,1,0:T(8,128)(2,1)S(1)}, bf16[4,144,512]{2,1,0:T(8,128)(2,1)S(1)}, u32[]{:S(2)}, u32[]{:S(2)}) collective-permute-start(bf16[4,144,512]{2,1,0:T(8,128)(2,1)S(1)} %get-tuple-element.105.refs_1_.refs_0_), channel_id=1, source_target_pairs={{0,2},{1,5},{2,0},{3,7},{4,6},{5,1},{6,4},{7,3},{8,10},{9,13},{10,... | collective-permute-start | bytes 1769480 | tf_op jit(solution)/shard_map/ppermute | solution.py:203
  43.0 14.1 %collective-permute-start.12 = (bf16[1,16,2304]{2,1,0:T(8,128)(2,1)S(1)}, bf16[1,16,2304]{2,1,0:T(8,128)(2,1)S(1)}, u32[]{:S(2)}, u32[]{:S(2)}) collective-permute-start(bf16[1,16,2304]{2,1,0:T(8,128)(2,1)S(1)} %bitcast.60), channel_id=1, source_target_pairs={{0,16},{2,18},{4,20},{6,22},{8,24},{10,26},{12,28},{14,30},{16,0},... | collective-permute-start | bytes 221192 | tf_op jit(solution)/shard_map/ppermute | solution.py:198
  60.3 18.7 %collective-permute-start.15 = (bf16[8,144,512]{2,1,0:T(8,128)(2,1)S(1)}, bf16[8,144,512]{2,1,0:T(8,128)(2,1)S(1)}, u32[]{:S(2)}, u32[]{:S(2)}) collective-permute-start(bf16[8,144,512]{2,1,0:T(8,128)(2,1)S(1)} %get-tuple-element.106.refs_0_), channel_id=1, source_target_pairs={{0,4},{1,3},{2,6},{3,1},{4,0},{5,7},{6,2},{7,5},{8,12},{9,11},{10,... | collective-permute-start | bytes 3538952 | tf_op jit(solution)/shard_map/ppermute | solution.py:203
  79.4 12.4 %collective-permute-start.17 = (bf16[4,16,2304]{2,1,0:T(8,128)(2,1)S(1)}, bf16[4,16,2304]{2,1,0:T(8,128)(2,1)S(1)}, u32[]{:S(2)}, u32[]{:S(2)}) collective-permute-start(bf16[4,16,2304]{2,1,0:T(8,128)(2,1)S(1)} %get-tuple-element.109.refs_0_), channel_id=1, source_target_pairs={{0,2},{1,5},{2,0},{3,7},{4,6},{5,1},{6,4},{7,3},{8,10},{9,13},{10,... | collective-permute-start | bytes 884744 | tf_op jit(solution)/shard_map/ppermute | solution.py:203
  91.9 16.5 %collective-permute-start.18 = (bf16[8,16,2304]{2,1,0:T(8,128)(2,1)S(1)}, bf16[8,16,2304]{2,1,0:T(8,128)(2,1)S(1)}, u32[]{:S(2)}, u32[]{:S(2)}) collective-permute-start(bf16[8,16,2304]{2,1,0:T(8,128)(2,1)S(1)} %shard_map.232.refs_0_), channel_id=1, source_target_pairs={{0,4},{1,3},{2,6},{3,1},{4,0},{5,7},{6,2},{7,5},{8,12},{9,11},{10,... | collective-permute-start | bytes 1769480 | tf_op jit(solution)/shard_map/ppermute | solution.py:203
  118.5 13.5 %collective-permute-start.20 = (bf16[16,64,2176]{2,1,0:T(8,128)(2,1)}, bf16[16,64,2176]{2,1,0:T(8,128)(2,1)}, u32[]{:S(2)}, u32[]{:S(2)}) collective-permute-start(bf16[16,64,2176]{2,1,0:T(8,128)(2,1)} %bitcast.70), channel_id=1, source_target_pairs={{0,1},{1,0},{2,3},{3,2},{4,5},{5,4},{6,7},{7,6},{8,9},{9,8},{10,11... | collective-permute-start | bytes 13369352 | tf_op jit(solution)/shard_map/ppermute | solution.py:194
  118.7 13.4 %all-to-all-start.2 = ((f32[16,2,2048]{2,1,0:T(2,128)}), f32[16,2,2048]{2,1,0:T(2,128)}, u32[]{:S(2)}, u32[]{:S(2)}) async-start(f32[16,2,2048]{2,1,0:T(2,128)} %copy-done.48), calls=%async_computation.2 | async-start | bytes 524288 | tf_op jit(solution)/shard_map/all_to_all | solution.py:212
  123.6 83.8 %all-gather.5.cloned.1.call-start = ((), (), s32[]{:S(2)}) async-start(), calls=%async_computation.9 | async-start | bytes 2228224 | tf_op jit(solution)/shard_map/all_gather | solution.py:1273
  159.0 12.9 %all-to-all-start.4 = ((bf16[16,32,128]{2,1,0:T(8,128)(2,1)}), bf16[16,32,128]{2,1,0:T(8,128)(2,1)S(1)}, u32[]{:S(2)}, u32[]{:S(2)}) async-start(bf16[16,32,128]{2,1,0:T(8,128)(2,1)} %get-tuple-element.116), calls=%async_computation.4 | async-start | bytes 262144 | tf_op jit(solution)/shard_map/all_to_all | solution.py:1234
  194.5 12.9 %all-to-all-start.5 = ((f32[16,2,2048]{2,1,0:T(2,128)}), f32[16,2,2048]{2,1,0:T(2,128)S(1)}, u32[]{:S(2)}, u32[]{:S(2)}) async-start(f32[16,2,2048]{2,1,0:T(2,128)} %get-tuple-element.122), calls=%async_computation.5 | async-start | bytes 524288 | tf_op jit(solution)/shard_map/all_to_all | solution.py:212
  198.0 106.1 %all-gather.7.cloned.1.call-start = ((), (), s32[]{:S(2)}) async-start(), calls=%async_computation.10 | async-start | bytes 2228224 | tf_op jit(solution)/shard_map/all_gather | solution.py:1301
  198.1 67.3 %collective-permute-start.25 = (bf16[288,4608]{1,0:T(8,128)(2,1)}, bf16[288,4608]{1,0:T(8,128)(2,1)}, u32[]{:S(2)}, u32[]{:S(2)}) collective-permute-start(bf16[288,4608]{1,0:T(8,128)(2,1)} %get-tuple-element.141.refs_1_), channel_id=1, source_target_pairs={{0,1},{1,0},{2,3},{3,2},{4,5},{5,4},{6,7},{7,6},{8,9},{9,8},{10,11... | collective-permute-start | bytes 7962632 | tf_op jit(solution)/shard_map/ppermute | solution.py:194
  254.2 12.1 %collective-permute-start.27 = (bf16[8,32,1280]{2,1,0:T(8,128)(2,1)}, bf16[8,32,1280]{2,1,0:T(8,128)(2,1)S(1)}, u32[]{:S(2)}, u32[]{:S(2)}) collective-permute-start(bf16[8,32,1280]{2,1,0:T(8,128)(2,1)} %get-tuple-element.145), channel_id=1, source_target_pairs={{0,4},{1,3},{2,6},{3,1},{4,0},{5,7},{6,2},{7,5},{8,12},{9,11},{10,... | collective-permute-start | bytes 1966088 | tf_op jit(solution)/shard_map/ppermute | solution.py:203
  274.3 20.1 %collective-permute-start.30 = (bf16[8,288,256]{2,1,0:T(8,128)(2,1)}, bf16[8,288,256]{2,1,0:T(8,128)(2,1)}, u32[]{:S(2)}, u32[]{:S(2)}) collective-permute-start(bf16[8,288,256]{2,1,0:T(8,128)(2,1)} %get-tuple-element.156), channel_id=1, source_target_pairs={{0,4},{1,3},{2,6},{3,1},{4,0},{5,7},{6,2},{7,5},{8,12},{9,11},{10,... | collective-permute-start | bytes 3538952 | tf_op jit(solution)/shard_map/ppermute | solution.py:203
  274.3 28.8 %collective-permute-start.28 = (bf16[288,2048]{1,0:T(8,128)(2,1)S(1)}, bf16[288,2048]{1,0:T(8,128)(2,1)}, u32[]{:S(2)}, u32[]{:S(2)}) collective-permute-start(bf16[288,2048]{1,0:T(8,128)(2,1)S(1)} %bitcast.50), channel_id=1, source_target_pairs={{0,1},{1,0},{2,3},{3,2},{4,5},{5,4},{6,7},{7,6},{8,9},{9,8},{10,11... | collective-permute-start | bytes 3538952 | tf_op jit(solution)/shard_map/ppermute | solution.py:194
  297.8 25.1 %collective-permute-start.32 = (bf16[4,288,256]{2,1,0:T(8,128)(2,1)}, bf16[4,288,256]{2,1,0:T(8,128)(2,1)}, u32[]{:S(2)}, u32[]{:S(2)}) collective-permute-start(bf16[4,288,256]{2,1,0:T(8,128)(2,1)} %get-tuple-element.163), channel_id=1, source_target_pairs={{0,2},{1,5},{2,0},{3,7},{4,6},{5,1},{6,4},{7,3},{8,10},{9,13},{10,... | collective-permute-start | bytes 1769480 | tf_op jit(solution)/shard_map/ppermute | solution.py:203
  298.4 12.8 %collective-permute-start.33 = (bf16[4,32,1280]{2,1,0:T(8,128)(2,1)}, bf16[4,32,1280]{2,1,0:T(8,128)(2,1)}, u32[]{:S(2)}, u32[]{:S(2)}) collective-permute-start(bf16[4,32,1280]{2,1,0:T(8,128)(2,1)} %get-tuple-element.164), channel_id=1, source_target_pairs={{0,2},{1,5},{2,0},{3,7},{4,6},{5,1},{6,4},{7,3},{8,10},{9,13},{10,... | collective-permute-start | bytes 983048 | tf_op jit(solution)/shard_map/ppermute | solution.py:203
  318.4 24.2 %collective-permute-start.35 = (f32[144,2048]{1,0:T(8,128)}, f32[144,2048]{1,0:T(8,128)S(1)}, u32[]{:S(2)}, u32[]{:S(2)}) collective-permute-start(f32[144,2048]{1,0:T(8,128)} %copy-done.29), channel_id=1, source_target_pairs={{0,1},{1,0},{2,3},{3,2},{4,5},{5,4},{6,7},{7,6},{8,9},{9,8},{10,11... | collective-permute-start | bytes 3538952 | tf_op jit(solution)/shard_map/ppermute | solution.py:194
  326.1 12.7 %collective-permute-start.40 = (bf16[1,288,256]{2,1,0:T(8,128)(2,1)}, bf16[1,288,256]{2,1,0:T(8,128)(2,1)S(1)}, u32[]{:S(2)}, u32[]{:S(2)}) collective-permute-start(bf16[1,288,256]{2,1,0:T(8,128)(2,1)} %get-tuple-element.179), channel_id=1, source_target_pairs={{0,24},{2,26},{4,28},{6,30},{8,16},{10,18},{12,20},{14,22},{16,8},... | collective-permute-start | bytes 442376 | tf_op jit(solution)/shard_map/ppermute | solution.py:198
  326.1 13.3 %collective-permute-start.39 = (bf16[1,288,256]{2,1,0:T(8,128)(2,1)}, bf16[1,288,256]{2,1,0:T(8,128)(2,1)S(1)}, u32[]{:S(2)}, u32[]{:S(2)}) collective-permute-start(bf16[1,288,256]{2,1,0:T(8,128)(2,1)} %get-tuple-element.178), channel_id=1, source_target_pairs={{0,8},{2,10},{4,12},{6,14},{8,0},{10,2},{12,4},{14,6},{16,24},{18,... | collective-permute-start | bytes 442376 | tf_op jit(solution)/shard_map/ppermute | solution.py:198
  334.7 23.5 %collective-permute-start.50 = (f32[128,3072]{1,0:T(8,128)S(1)}, f32[128,3072]{1,0:T(8,128)S(1)}, u32[]{:S(2)}, u32[]{:S(2)}) collective-permute-start(f32[128,3072]{1,0:T(8,128)S(1)} %copy-done.28), channel_id=1, source_target_pairs={{0,1},{1,0},{2,3},{3,2},{4,5},{5,4},{6,7},{7,6},{8,9},{9,8},{10,11... | collective-permute-start | bytes 4718600 | tf_op jit(solution)/shard_map/ppermute | solution.py:194
  (112 other events, 908.3 us)
Sparse Core Ops, SparseCore 0:
  24.5 89.4 all-gather.8
  142.5 61.8 all-gather.4
  219.6 61.3 all-gather.6

commit v5 on v4

--- a/solution.py
+++ b/solution.py
@@ -87,7 +87,8 @@
 
 def kernel_call(body, outs, args, scratch=(), flops=0, transcendentals=0, limit=17, after=()):
     spaces = {Scalars: pltpu.SMEM, Left: pltpu.HBM, Streamed: pltpu.HBM}
-    in_spaces = [spaces.get(type(a), pltpu.VMEM) for a in args] + [pl.ANY] * len(after)
+    in_spaces = [spaces.get(type(a), pltpu.VMEM) for a in args] + [pltpu.HBM] * len(after)
+    after = [pltpu.with_memory_space_constraint(a, pltpu.HBM) for a in after]
     arrays = []
     for a in args:
         if isinstance(a, (Left, Loaded, Streamed)):
@@ -214,7 +215,7 @@
 
 
 Z_BITS = (8, 4, 12)
-XY_BITS = ((1, 2), (2, 1))
+XY_BITS = ((2, 1), (1, 2))
 STEPS_DP = 16
 
 
@@ -260,11 +261,13 @@
 
 
 class Scattering:
-    def __init__(self, kept, sent, size, before):
+    def __init__(self, kept, sent, size):
         self.size = size
-        self.kept = kept
-        sent, _ = lax.optimization_barrier((sent, before))
-        self.received = flip_both(sent, XY_BITS[1], size)
+        self.kept, self.sent = kept, sent
+
+    def first(self, before):
+        sent, _ = lax.optimization_barrier((self.sent, before))
+        self.received = flip_both(sent, XY_BITS[1], self.size)
 
     def second(self, after=()):
         self.kept, sent = add_parts(self.kept, self.received, 2, after)
@@ -398,7 +401,7 @@
     lax.fori_loop(0, 2 * half, move, 0)
 
 
-def weight_grad(left, right, slots, size, before, second=None, after=()):
+def weight_grad(left, right, slots, size, second=None, after=()):
     depth, width = left[0].shape[1], right[0].shape[1]
     rows = depth // size
     args = [Scalars(slots), *left, *right]
@@ -419,7 +422,7 @@
         flops=4 * left[0].shape[0] * depth * width,
         after=after,
     )
-    return Scattering(kept, sent, size, before)
+    return Scattering(kept, sent, size)
 
 
 def swap_columns(*totals):
@@ -605,7 +608,7 @@
     sums.store()
 
 
-def embed_kernel(count, pre_ref, norm_ref, project_ref, bias_ref, *refs):
+def embed_kernel(count, pre_ref, norm_ref, project_ref, bias_ref, pooled_ref, *refs):
     term_refs, *refs = refs
     act_ref, unit_ref, inverse_ref, low_ref = refs
     factors = norm_factors(term_refs, norm_ref, 2, count)
@@ -617,7 +620,14 @@
     unit = embed * inverse
     unit_ref[...] = unit
     inverse_ref[...] = jnp.broadcast_to(inverse, inverse_ref.shape)
-    low_ref[...] = jnp.broadcast_to(unit.astype(jnp.bfloat16)[None], low_ref.shape)
+    low = unit.astype(jnp.bfloat16)
+    copies, rows, _ = low_ref.shape
+    crops = low.shape[0]
+    for copy in range(copies):
+        low_ref[copy, :crops, :] = low
+        if rows > crops:
+            width = D // copies
+            low_ref[copy, crops:, :] = pooled_ref[:, copy * width : (copy + 1) * width]
 
 
 def embed_back_kernel(
@@ -855,12 +865,13 @@
     crops,
     device_crops,
     place,
-    units_ref,
+    sent_ref,
     side_ref,
     prototypes_ref,
     loss_ref,
     proto_grad_ref,
     unit_grad_ref,
+    units_ref,
     proto_ref,
     partner_ref,
     codes_ref,
@@ -878,6 +889,8 @@
     real = lax.broadcasted_iota(jnp.int32, (1, width), 1) < PROTOS
 
     dim = units_ref.shape[1]
+    for i in range(sent_ref.shape[0]):
+        units_ref[i * own : (i + 1) * own, :] = sent_ref[i, :own, :]
     proto_ref[PROTOS // 16 * 16 :, :] = jnp.zeros((width - PROTOS // 16 * 16, dim), jnp.bfloat16)
     proto_ref[:PROTOS, :] = prototypes_ref[...]
 
@@ -1004,7 +1017,7 @@
 
 
 def gathered_loss(units, side, prototypes, place, own, device_crops, loss_factor_weight):
-    crops, dim = units.shape
+    crops, dim = units.shape[0] * own, units.shape[2]
     width = -(-PROTOS // LANES) * LANES
     rows_all = crops + side.shape[0]
     f32, bf16 = jnp.float32, jnp.bfloat16
@@ -1012,9 +1025,10 @@
         lambda *refs: codes_kernel(
             crops, device_crops, *refs, factor=loss_factor_weight / SOFTMAX_HEAT
         ),
-        [((8, 128), f32), ((dim, width), f32), ((own, dim), f32)],
-        [Scalars(place), units, side, prototypes],
+        [((8, 128), f32), ((dim, width), f32, PUT_FAR), ((own, dim), f32)],
+        [Scalars(place), units, Loaded(side), Loaded(prototypes)],
         scratch=[
+            pltpu.VMEM((crops, dim), bf16),
             pltpu.VMEM((width, dim), bf16),
             pltpu.VMEM((crops, 1), jnp.int32),
             pltpu.VMEM((rows_all, width), f32),
@@ -1146,7 +1160,7 @@
         reduce_all = gather_whole(w_reduce)
 
     mid_rows, wide_rows = ((local_rows, MID), f32), ((local_rows, D), f32)
-    mid_sums, wide_sums = ((copies, 2, MID), f32), ((copies, 2, D), f32)
+    mid_sums, wide_sums = ((copies, 2, MID), f32), ((copies, 2, D), f32, PUT_FAR)
 
     def weight_out(weight):
         return (weight.shape, bf16, FAR)
@@ -1190,10 +1204,16 @@
         gather_step([expand_part], [terms_two])
         expand_all = expand_part.finish(slots)
 
-    side = ((expand_all.shape[0], max(expand_all.shape[1] - D, 128)), bf16)
+    side = ((expand_all.shape[0], max(expand_all.shape[1] - D, 128)), bf16, PUT_FAR)
     act_two, pre_three, sums, full_expand, side = kernel_call(
         lambda *refs: expand_kernel(expand_all.count, pixel_total, *refs),
-        [((local_rows, MID), bf16), wide_rows, wide_sums, weight_out(expand_all), side],
+        [
+            ((local_rows, MID), bf16, PUT_FAR),
+            wide_rows,
+            wide_sums,
+            weight_out(expand_all),
+            side,
+        ],
         [pre_two, norm_mid, terms_two] + expand_all.inputs(),
         scratch=expand_all.scratch() + [pltpu.SemaphoreType.DMA],
         flops=2 * local_rows * D * MID,
@@ -1205,11 +1225,24 @@
     else:
         head = gather_whole(head_shard)
 
-    crop_rows = ((local_crops, D), f32)
+    crop_rows = ((local_crops, D), f32, PUT_FAR)
     pooled_low, pre_head, sums, full_project = kernel_call(
         lambda *refs: pool_kernel(head.count, pixel_total, *refs),
-        [((local_crops, D), bf16), crop_rows, wide_sums, ((D, proj), bf16)],
-        [pre_three, input_rows, norm_wide, pool, crop_sizes, terms_three] + head.inputs(),
+        [
+            ((local_crops, D), bf16, PUT_FAR),
+            crop_rows,
+            wide_sums,
+            ((D, proj), bf16, PUT_FAR),
+        ],
+        [
+            pre_three,
+            input_rows,
+            Loaded(norm_wide),
+            Loaded(pool),
+            Loaded(crop_sizes),
+            terms_three,
+        ]
+        + head.inputs(),
         scratch=[pltpu.VMEM((local_rows, 256), bf16), pltpu.VMEM((local_rows, 256), bf16)]
         + head.scratch(CHUNKS),
         flops=2 * local_crops * D * D,
@@ -1218,20 +1251,28 @@
     terms_head = terms_over_dp(sums)
 
     embed_rows = ((local_crops, proj), f32)
+    send_pooled = gathered_codes and copies * proj == D
     act_head, unit_embed, inv_length, unit_low = kernel_call(
         lambda *refs: embed_kernel(crop_total, *refs),
         [
             ((local_crops, D), bf16),
             embed_rows,
             embed_rows,
-            ((copies, local_crops, proj), bf16),
+            ((copies, local_crops * (2 if send_pooled else 1), proj), bf16, PUT_FAR),
         ],
-        [pre_head, norm_wide, Streamed(full_project), bias_out.reshape(1, proj), terms_head],
+        [
+            Loaded(pre_head),
+            Loaded(norm_wide),
+            Streamed(full_project),
+            Loaded(bias_out.reshape(1, proj)),
+            Streamed(pooled_low),
+            terms_head,
+        ],
         flops=2 * local_crops * D * proj,
     )
 
     if gathered_codes:
-        all_units = lax.all_to_all(unit_low, "dp", 0, 0).reshape(crop_count, proj)
+        all_units = lax.all_to_all(unit_low, "dp", 0, 0)
         loss_part, proto_part, unit_grad = gathered_loss(
             all_units,
             side,
@@ -1263,27 +1304,32 @@
             inv_length,
             Streamed(full_project),
             Streamed(pre_head),
-            norm_wide,
+            Loaded(norm_wide),
             terms_head,
         ],
         flops=2 * local_crops * D * proj,
     )
     back_head = terms_over_dp(sums)
 
-    left = lax.all_gather(pooled_low, "dp", axis=0, tiled=True)
+    chip_rows = 2 * w_hidden.shape[0]
+    if send_pooled:
+        left = all_units[:, local_crops:].reshape(crop_count, chip_rows)
+    else:
+        left = lax.all_gather(pooled_low, "dp", axis=0, tiled=True)
+        left = lax.dynamic_slice_in_dim(left, me_dp * chip_rows, chip_rows, 1)
 
     own_part = ((own_rows, D), f32)
     head_low, own_grad, other_grad, sums, total_head = kernel_call(
         lambda *refs: pool_back_kernel(head.count, crop_total, pixel_total, *refs),
         [((local_crops, D), bf16), own_part, own_part, wide_sums, ((2, D), f32)],
         [
-            head_act_grad,
-            pre_head,
+            Loaded(head_act_grad),
+            Loaded(pre_head),
             Streamed(pre_three),
             Streamed(input_rows),
-            norm_wide,
-            spread,
-            crop_sizes,
+            Loaded(norm_wide),
+            Loaded(spread),
+            Loaded(crop_sizes),
             terms_head,
             back_head,
             terms_three,
@@ -1292,7 +1338,6 @@
         scratch=head.scratch(CHUNKS),
         flops=2 * local_crops * D * D,
         transcendentals=local_rows * D,
-        after=[left],
     )
     back_three = terms_over_dp(sums)
     other_grad, _ = lax.optimization_barrier((other_grad, back_three))
@@ -1331,7 +1376,6 @@
             (three_kept, swap_cores(three_sent)),
             chip_slots,
             size,
-            back_two,
             (
                 (act_head, swap_cores(act_head)),
                 (embed_low, swap_cores(embed_low)),
@@ -1370,12 +1414,9 @@
             (two_kept, swap_cores(two_sent)),
             chip_slots,
             size,
-            two_kept,
-            after=[expand_sum.received],
         )
-        expand_sum.second(after=[spatial_sum.kept])
+        spatial_sum.first(two_kept)
         sums, _ = lax.optimization_barrier((sums, spatial_sum.kept))
-        before_one = [expand_sum.kept]
 
     back_one = terms_over_dp(sums)
     one_low, other_low, one_kept, one_sent, total_one = kernel_call(
@@ -1390,20 +1431,22 @@
         after=before_one,
     )
     if by_steps:
+        expand_sum.first(back_one)
         spatial_sum.second([one_low])
+        expand_sum.second([spatial_sum.kept])
         reduce_sum = weight_grad(
             (input_rows, swap_cores(input_rows)),
             (one_kept, swap_cores(one_sent)),
             chip_slots,
             size,
-            one_low,
-            after=[spatial_sum.kept, right],
+            after=[expand_sum.kept, right],
         )
 
     proto_other = swap_cores(proto_part)
     other_low = swap_cores(other_low)
     late = []
     if by_steps:
+        reduce_sum.first(one_low)
         expand_sum.third([reduce_sum.kept])
         spatial_sum.third([expand_sum.kept])
         reduce_sum.second([spatial_sum.kept])
@@ -1429,10 +1472,7 @@
         )[0]
     else:
         proto_grad = (proto_part + proto_other).T
-    chip_rows = 2 * w_hidden.shape[0]
-    hidden_part = product_t(
-        lax.dynamic_slice_in_dim(left, me_dp * chip_rows, chip_rows, 1), right
-    )
+    hidden_part = product_t(left, right)
 
     def own_half(part):
         half = chip_rows // 2

time: 379 us -> 360 us (0.950)
  local copies, waits for them, and re-layouts: 45.2 us -> 22.3 us
  blocking collectives: 59.5 us -> 68.8 us
  starting transfers between devices: 93.8 us -> 87.6 us
  Pallas kernels: 101 us -> 106 us
    unnamed x156 -> x114, local copies, waits for them, and re-layouts: 39.7 us -> 17.7 us
    all_to_all x4 -> x5, blocking collectives: 59.5 us -> 68.8 us  [terms_over_dp(): return lax.all_to_all(copies, 'dp', 0, 0)]
    pallas_call x34, Pallas kernels: 101 us -> 106 us  [kernel_call(): pl.pallas_call(kernel, out_shape=[jax.ShapeDtypeStruct(*out) if len(out)...]
    all_to_all x4 -> x3, starting transfers between devices: 16.4 us -> 13.7 us  [terms_over_dp(): return lax.all_to_all(copies, 'dp', 0, 0)]
    all_to_all x4 -> x3, waiting for transfers between devices: 18.5 us -> 16.1 us  [terms_over_dp(): return lax.all_to_all(copies, 'dp', 0, 0)]
  transfers between devices with their start and end apart: 59 -> 57, of which waited for: 16 -> 18; matrix products, arithmetic and copies ran while one was open for 4% -> 3% of each run, Pallas kernels for 25% -> 21%
where the time goes in v5:
time: 360 us; the launch traced here: 359 us
  Pallas kernels  106 us (29%)
  starting transfers between devices  87.6 us (24%)
  blocking collectives  68.8 us (19%)
  waiting for transfers between devices  49.5 us (14%)
  local copies, waits for them, and re-layouts  22.3 us (6%)
  between operations  16.6 us (5%)
  other arithmetic  7.3 us (2%)
    pallas_call x34, Pallas kernels, kernel_call(): pl.pallas_call(kernel, out_shape=[jax.ShapeDtypeStruct(*out) if len(out)...  106 us
    all_to_all x5, blocking collectives, terms_over_dp(): return lax.all_to_all(copies, 'dp', 0, 0)  68.8 us
    ppermute x21, starting transfers between devices, swap_cores(): return lax.ppermute(values, 'shard', [(0, 1), (1, 0)])  32.3 us
    ppermute x18, starting transfers between devices, flip_dp(): return lax.ppermute(values, 'dp', [(i, i ^ bits) for i in range(size)])  28.2 us
    unnamed x114, local copies, waits for them, and re-layouts  17.7 us
    all_to_all x3, waiting for transfers between devices, terms_over_dp(): return lax.all_to_all(copies, 'dp', 0, 0)  16.1 us
    ppermute x18, waiting for transfers between devices, flip_dp(): return lax.ppermute(values, 'dp', [(i, i ^ bits) for i in range(size)])  13.9 us
    all_to_all x3, starting transfers between devices, terms_over_dp(): return lax.all_to_all(copies, 'dp', 0, 0)  13.7 us
  transfers between devices with their start and end apart: 57, of which 18 were waited for; matrix products, arithmetic and copies ran while one was open for 3% of the time, Pallas kernels for 21%

profile of v5, /device:TPU:1, one launch (start us, length us, event | category | flops | bytes accessed | tf_op | source)
XLA Modules:
  0.0 358.7 jit_solution(10479989199488188539)
XLA Ops:
  30.1 4.2 %collective-permute-done.7.refs_3_ = bf16[1,144,512]{2,1,0:T(8,128)(2,1)S(1)} collective-permute-done((bf16[1,144,512]{2,1,0:T(8,128)(2,1)S(1)}, bf16[1,144,512]{2,1,0:T(8,128)(2,1)S(1)}, u32[]{:S(2)}, u32[]{:S(2)}) %collective-permute-start.7) | collective-permute-done | bytes 147488 | tf_op jit(solution)/shard_map/ppermute | solution.py:199
  34.3 4.3 %collective-permute-done.9.refs_5_ = bf16[1,144,512]{2,1,0:T(8,128)(2,1)S(1)} collective-permute-done((bf16[1,144,512]{2,1,0:T(8,128)(2,1)S(1)}, bf16[1,144,512]{2,1,0:T(8,128)(2,1)S(1)}, u32[]{:S(2)}, u32[]{:S(2)}) %collective-permute-start.9) | collective-permute-done | bytes 147488 | tf_op jit(solution)/shard_map/ppermute | solution.py:199
  43.9 7.6 %collective-permute-start.12 = (bf16[1,16,2304]{2,1,0:T(8,128)(2,1)S(1)}, bf16[1,16,2304]{2,1,0:T(8,128)(2,1)S(1)}, u32[]{:S(2)}, u32[]{:S(2)}) collective-permute-start(bf16[1,16,2304]{2,1,0:T(8,128)(2,1)S(1)} %bitcast.61), channel_id=1, source_target_pairs={{0,16},{2,18},{4,20},{6,22},{8,24},{10,26},{12,28},{14,30},{16,0},... | collective-permute-start | bytes 221192 | tf_op jit(solution)/shard_map/ppermute | solution.py:199
  58.7 16.1 %all_to_all.45.refs_2_.refs_3_.refs_9_.refs_4_ = f32[16,2,512]{2,1,0:T(2,128)} all-to-all(f32[16,2,512]{2,1,0:T(2,128)S(1)} %copy-done.33), channel_id=1, replica_groups=mesh['dp'=16,'shard'=2] {'dp'}, dimensions={0} | all-to-all | bytes 131072 | tf_op jit(solution)/shard_map/all_to_all | solution.py:213
  75.0 5.4 %collective-permute-start.16 = (bf16[16,144,512]{2,1,0:T(8,128)(2,1)S(1)}, bf16[16,144,512]{2,1,0:T(8,128)(2,1)S(1)}, u32[]{:S(2)}, u32[]{:S(2)}) collective-permute-start(bf16[16,144,512]{2,1,0:T(8,128)(2,1)S(1)} %shard_map.230.refs_5_), channel_id=1, source_target_pairs={{0,1},{1,0},{2,3},{3,2},{4,5},{5,4},{6,7},{7,6},{8,9},{9,8},{10,11... | collective-permute-start | bytes 7077896 | tf_op jit(solution)/shard_map/ppermute | solution.py:195
  86.2 6.5 %shard_map.231 = (f32[288,512]{1,0:T(8,128)S(1)}, f32[16,2,512]{2,1,0:T(2,128)S(1)}, bf16[288,4608]{1,0:T(8,128)(2,1)}, bf16[4608,512]{1,0:T(8,128)(2,1)}) custom-call(f32[288,512]{1,0:T(8,128)S(1)} %get-tuple-element.103.refs_0_.refs_5_.refs_2_, f32[4,512]{1,0:T(4,128)S(1)} %copy-done.35, f32[288,16]{1,0:T(8,128)S(1)} %copy-done.30, ...), custom_call_target="tpu_custom_call" | custom-call | flops 1358954496 | bytes 5400704 | tf_op jit(solution)/shard_map/pallas_call | solution.py:117
  93.7 13.9 %all_to_all.46.refs_2_.refs_11_.refs_7_ = f32[16,2,512]{2,1,0:T(2,128)} all-to-all(f32[16,2,512]{2,1,0:T(2,128)} %copy-done.34), channel_id=1, replica_groups=mesh['dp'=16,'shard'=2] {'dp'}, dimensions={0} | all-to-all | bytes 131072 | tf_op jit(solution)/shard_map/all_to_all | solution.py:213
  112.8 4.8 %shard_map.234 = (bf16[288,512]{1,0:T(8,128)(2,1)}, f32[288,2048]{1,0:T(8,128)S(1)}, f32[16,2,2048]{2,1,0:T(2,128)}, bf16[512,2304]{1,0:T(8,128)(2,1)}, bf16[512,256]{1,0:T(8,128)(2,1)}) custom-call(f32[288,512]{1,0:T(8,128)S(1)} %get-tuple-element.107.refs_0_.refs_6_.refs_2_, f32[4,512]{1,0:T(4,128)S(1)} %copy-done.35, f32[16,2,512]{2,1,0:T(2,128)S(1)} %copy-done.16, ...), custom_call_target="tpu_custom_call" | custom-call | flops 603979776 | bytes 3022976 | tf_op jit(solution)/shard_map/pallas_call | solution.py:117
  118.1 4.5 %all-to-all-start.2 = ((f32[16,2,2048]{2,1,0:T(2,128)}), f32[16,2,2048]{2,1,0:T(2,128)}, u32[]{:S(2)}, u32[]{:S(2)}) async-start(f32[16,2,2048]{2,1,0:T(2,128)} %get-tuple-element.111), calls=%async_computation.2 | async-start | bytes 524288 | tf_op jit(solution)/shard_map/all_to_all | solution.py:213
  122.7 8.9 %all-to-all-done.2.refs_5_.refs_9_ = f32[16,2,2048]{2,1,0:T(2,128)} async-done(((f32[16,2,2048]{2,1,0:T(2,128)}), f32[16,2,2048]{2,1,0:T(2,128)}, u32[]{:S(2)}, u32[]{:S(2)}) %all-to-all-start.2) | async-done | bytes 262176 | tf_op jit(solution)/shard_map/all_to_all | solution.py:213
  131.6 6.3 %shard_map.236 = (bf16[32,2048]{1,0:T(8,128)(2,1)}, f32[32,2048]{1,0:T(8,128)}, f32[16,2,2048]{2,1,0:T(2,128)}, bf16[2048,128]{1,0:T(8,128)(2,1)}) custom-call(f32[288,2048]{1,0:T(8,128)S(1)} %get-tuple-element.110.refs_0_.refs_2_.refs_3_, bf16[288,2048]{1,0:T(8,128)(2,1)S(1)} %bitcast.50, f32[4,2048]{1,0:T(4,128)} %refs_4_.3, ...), custom_call_target="tpu_custom_call" | custom-call | flops 268435456 | bytes 12765440 | tf_op jit(solution)/shard_map/pallas_call | solution.py:117
  137.9 11.8 %all_to_all.47.refs_5_.refs_6_.refs_7_ = f32[16,2,2048]{2,1,0:T(2,128)S(1)} all-to-all(f32[16,2,2048]{2,1,0:T(2,128)} %get-tuple-element.116), channel_id=1, replica_groups=mesh['dp'=16,'shard'=2] {'dp'}, dimensions={0} | all-to-all | bytes 524288 | tf_op jit(solution)/shard_map/all_to_all | solution.py:213
  152.8 5.2 %all-to-all-start.4 = ((bf16[16,64,128]{2,1,0:T(8,128)(2,1)}), bf16[16,64,128]{2,1,0:T(8,128)(2,1)S(1)}, u32[]{:S(2)}, u32[]{:S(2)}) async-start(bf16[16,64,128]{2,1,0:T(8,128)(2,1)} %get-tuple-element.117), calls=%async_computation.4 | async-start | bytes 524288 | tf_op jit(solution)/shard_map/all_to_all | solution.py:1275
  158.0 7.4 %all-to-all-done.4.refs_1_ = bf16[16,64,128]{2,1,0:T(8,128)(2,1)S(1)} async-done(((bf16[16,64,128]{2,1,0:T(8,128)(2,1)}), bf16[16,64,128]{2,1,0:T(8,128)(2,1)S(1)}, u32[]{:S(2)}, u32[]{:S(2)}) %all-to-all-start.4) | async-done | bytes 262176 | tf_op jit(solution)/shard_map/all_to_all | solution.py:1275
  165.4 18.2 %shard_map.238 = (f32[8,128]{1,0:T(8,128)S(1)}, f32[128,3072]{1,0:T(8,128)}, f32[32,128]{1,0:T(8,128)S(1)}) custom-call(s32[2]{0:T(128)S(1)} %pad_add_fusion.1.refs_0_, bf16[16,64,128]{2,1,0:T(8,128)(2,1)S(1)} %all-to-all-done.4.refs_1_, bf16[512,256]{1,0:T(8,128)(2,1)} %get-tuple-element.118.refs_2_, bf16[3000,128]{1,0:T(8,128)(2,1)} %refs_3_.3), custom_call_target="tpu_custom_call" | custom-call | flops 3221225472 | bytes 1292296 | tf_op jit(solution)/shard_map/pallas_call | solution.py:117
  186.7 5.2 %all-to-all-start.5 = ((f32[16,2,2048]{2,1,0:T(2,128)}), f32[16,2,2048]{2,1,0:T(2,128)S(1)}, u32[]{:S(2)}, u32[]{:S(2)}) async-start(f32[16,2,2048]{2,1,0:T(2,128)} %get-tuple-element.123), calls=%async_computation.5 | async-start | bytes 524288 | tf_op jit(solution)/shard_map/all_to_all | solution.py:213
  193.7 5.7 %all-to-all-done.5.refs_8_ = f32[16,2,2048]{2,1,0:T(2,128)S(1)} async-done(((f32[16,2,2048]{2,1,0:T(2,128)}), f32[16,2,2048]{2,1,0:T(2,128)S(1)}, u32[]{:S(2)}, u32[]{:S(2)}) %all-to-all-start.5) | async-done | bytes 262176 | tf_op jit(solution)/shard_map/all_to_all | solution.py:213
  199.4 9.7 %shard_map.240 = (bf16[32,2048]{1,0:T(8,128)(2,1)}, f32[144,2048]{1,0:T(8,128)S(1)}, f32[144,2048]{1,0:T(8,128)S(1)}, f32[16,2,2048]{2,1,0:T(2,128)}, f32[2,2048]{1,0:T(2,128)S(1)}) custom-call(f32[32,2048]{1,0:T(8,128)} %get-tuple-element.122.refs_0_, f32[32,2048]{1,0:T(8,128)} %get-tuple-element.113.refs_0_.refs_4_.refs_1_, f32[288,2048]{1,0:T(8,128)} %copy-done.3, ...), custom_call_target="tpu_custom_call" | custom-call | flops 268435456 | bytes 13814016 | tf_op jit(solution)/shard_map/pallas_call | solution.py:117
  209.1 12.6 %all_to_all.48.refs_10_ = f32[16,2,2048]{2,1,0:T(2,128)S(1)} all-to-all(f32[16,2,2048]{2,1,0:T(2,128)} %get-tuple-element.126), channel_id=1, replica_groups=mesh['dp'=16,'shard'=2] {'dp'}, dimensions={0} | all-to-all | bytes 524288 | tf_op jit(solution)/shard_map/all_to_all | solution.py:213
  221.7 5.8 %shard_map.241 = (bf16[288,1024]{1,0:T(8,128)(2,1)S(1)}, bf16[288,1024]{1,0:T(8,128)(2,1)}, f32[288,512]{1,0:T(8,128)S(1)}, f32[16,2,640]{2,1,0:T(2,128)}, f32[2,2048]{1,0:T(2,128)S(1)}) custom-call(s32[1]{0:T(128)} %bitcast.refs_0_.refs_9_, f32[144,2048]{1,0:T(8,128)S(1)} %get-tuple-element.124.refs_1_, f32[144,2048]{1,0:T(8,128)S(1)} %get-tuple-element.127.refs_2_, ...), custom_call_target="tpu_custom_call" | custom-call | flops 603979776 | bytes 8299012 | tf_op jit(solution)/shard_map/pallas_call | solution.py:117
  239.5 4.3 %shard_map.242 = (f32[8,32,1280]{2,1,0:T(8,128)}, bf16[8,32,1280]{2,1,0:T(8,128)(2,1)}) custom-call(s32[16]{0:T(128)S(1)} %fusion.20.refs_0_, bf16[288,512]{1,0:T(8,128)(2,1)} %get-tuple-element.133.refs_1_, bf16[288,512]{1,0:T(8,128)(2,1)} %collective-permute-done.21.refs_2_, bf16[288,1024]{1,0:T(8,128)(2,1)S(1)} %copy-done.39, ...), custom_call_target="tpu_custom_call" | custom-call | flops 603979776 | bytes 2048068 | tf_op jit(solution)/shard_map/pallas_call | solution.py:117
  245.3 4.9 %shard_map.243 = (bf16[288,256]{1,0:T(8,128)(2,1)S(1)}, bf16[288,256]{1,0:T(8,128)(2,1)S(1)}, f32[288,512]{1,0:T(8,128)S(1)}, f32[16,2,512]{2,1,0:T(2,128)S(1)}, f32[2,640]{1,0:T(2,128)S(1)}) custom-call(s32[1]{0:T(128)} %bitcast.refs_0_.refs_9_, f32[288,512]{1,0:T(8,128)S(1)} %copy-done.28, f32[288,512]{1,0:T(8,128)} %copy-done.5, f32[4,512]{1,0:T(4,128)S(1)} %copy-done.35, ...), custom_call_target="tpu_custom_call" | custom-call | flops 1358954496 | bytes 6727684 | tf_op jit(solution)/shard_map/pallas_call | solution.py:117
  253.5 7.8 %shard_map.244 = (f32[8,288,256]{2,1,0:T(8,128)}, bf16[8,288,256]{2,1,0:T(8,128)(2,1)}) custom-call(s32[16]{0:T(128)S(1)} %fusion.20.refs_0_, bf16[288,4608]{1,0:T(8,128)(2,1)} %get-tuple-element.141.refs_1_, bf16[288,4608]{1,0:T(8,128)(2,1)} %collective-permute-done.25.refs_2_, bf16[288,256]{1,0:T(8,128)(2,1)S(1)} %get-tuple-element.142.refs_3_, ...), custom_call_target="tpu_custom_call" | custom-call | flops 1358954496 | bytes 5603392 | tf_op jit(solution)/shard_map/pallas_call | solution.py:117
  263.1 14.4 %all_to_all.49.refs_5_ = f32[16,2,512]{2,1,0:T(2,128)S(1)} all-to-all(f32[16,2,512]{2,1,0:T(2,128)S(1)} %get-tuple-element.145), channel_id=1, replica_groups=mesh['dp'=16,'shard'=2] {'dp'}, dimensions={0} | all-to-all | bytes 131072 | tf_op jit(solution)/shard_map/all_to_all | solution.py:213
  (301 shorter events, 146.5 us)
Async XLA Ops:
  7.2 110.5 %all-gather.6.cloned.1.call-start = ((), (), s32[]{:S(2)}) async-start(), calls=%async_computation.10 | async-start | bytes 4734976 | tf_op jit(solution)/shard_map/all_gather | solution.py:1155
  24.9 13.7 %collective-permute-start.6 = (bf16[8,64,512]{2,1,0:T(8,128)(2,1)}, bf16[8,64,512]{2,1,0:T(8,128)(2,1)S(1)}, u32[]{:S(2)}, u32[]{:S(2)}) collective-permute-start(bf16[8,64,512]{2,1,0:T(8,128)(2,1)} %copy-done.8), channel_id=1, source_target_pairs={{0,2},{1,5},{2,0},{3,7},{4,6},{5,1},{6,4},{7,3},{8,10},{9,13},{10,... | collective-permute-start | bytes 1572872 | tf_op jit(solution)/shard_map/ppermute | solution.py:204
  39.8 13.1 %collective-permute-start.10 = (bf16[16,64,512]{2,1,0:T(8,128)(2,1)S(1)}, bf16[16,64,512]{2,1,0:T(8,128)(2,1)}, u32[]{:S(2)}, u32[]{:S(2)}) collective-permute-start(bf16[16,64,512]{2,1,0:T(8,128)(2,1)S(1)} %get-tuple-element.102.refs_2_), channel_id=1, source_target_pairs={{0,1},{1,0},{2,3},{3,2},{4,5},{5,4},{6,7},{7,6},{8,9},{9,8},{10,11... | collective-permute-start | bytes 3145736 | tf_op jit(solution)/shard_map/ppermute | solution.py:195
  43.4 15.0 %collective-permute-start.11 = (bf16[4,144,512]{2,1,0:T(8,128)(2,1)S(1)}, bf16[4,144,512]{2,1,0:T(8,128)(2,1)S(1)}, u32[]{:S(2)}, u32[]{:S(2)}) collective-permute-start(bf16[4,144,512]{2,1,0:T(8,128)(2,1)S(1)} %get-tuple-element.105.refs_1_.refs_0_), channel_id=1, source_target_pairs={{0,4},{1,3},{2,6},{3,1},{4,0},{5,7},{6,2},{7,5},{8,12},{9,11},{10,... | collective-permute-start | bytes 1769480 | tf_op jit(solution)/shard_map/ppermute | solution.py:204
  43.9 13.5 %collective-permute-start.12 = (bf16[1,16,2304]{2,1,0:T(8,128)(2,1)S(1)}, bf16[1,16,2304]{2,1,0:T(8,128)(2,1)S(1)}, u32[]{:S(2)}, u32[]{:S(2)}) collective-permute-start(bf16[1,16,2304]{2,1,0:T(8,128)(2,1)S(1)} %bitcast.61), channel_id=1, source_target_pairs={{0,16},{2,18},{4,20},{6,22},{8,24},{10,26},{12,28},{14,30},{16,0},... | collective-permute-start | bytes 221192 | tf_op jit(solution)/shard_map/ppermute | solution.py:199
  58.6 16.2 %collective-permute-start.15 = (bf16[8,144,512]{2,1,0:T(8,128)(2,1)S(1)}, bf16[8,144,512]{2,1,0:T(8,128)(2,1)S(1)}, u32[]{:S(2)}, u32[]{:S(2)}) collective-permute-start(bf16[8,144,512]{2,1,0:T(8,128)(2,1)S(1)} %get-tuple-element.106.refs_0_), channel_id=1, source_target_pairs={{0,2},{1,5},{2,0},{3,7},{4,6},{5,1},{6,4},{7,3},{8,10},{9,13},{10,... | collective-permute-start | bytes 3538952 | tf_op jit(solution)/shard_map/ppermute | solution.py:204
  80.5 12.8 %collective-permute-start.17 = (bf16[4,16,2304]{2,1,0:T(8,128)(2,1)S(1)}, bf16[4,16,2304]{2,1,0:T(8,128)(2,1)S(1)}, u32[]{:S(2)}, u32[]{:S(2)}) collective-permute-start(bf16[4,16,2304]{2,1,0:T(8,128)(2,1)S(1)} %get-tuple-element.109.refs_0_), channel_id=1, source_target_pairs={{0,4},{1,3},{2,6},{3,1},{4,0},{5,7},{6,2},{7,5},{8,12},{9,11},{10,... | collective-permute-start | bytes 884744 | tf_op jit(solution)/shard_map/ppermute | solution.py:204
  93.4 14.3 %collective-permute-start.18 = (bf16[8,16,2304]{2,1,0:T(8,128)(2,1)S(1)}, bf16[8,16,2304]{2,1,0:T(8,128)(2,1)S(1)}, u32[]{:S(2)}, u32[]{:S(2)}) collective-permute-start(bf16[8,16,2304]{2,1,0:T(8,128)(2,1)S(1)} %shard_map.232.refs_0_), channel_id=1, source_target_pairs={{0,2},{1,5},{2,0},{3,7},{4,6},{5,1},{6,4},{7,3},{8,10},{9,13},{10,... | collective-permute-start | bytes 1769480 | tf_op jit(solution)/shard_map/ppermute | solution.py:204
  117.7 13.9 %collective-permute-start.20 = (bf16[16,64,2176]{2,1,0:T(8,128)(2,1)}, bf16[16,64,2176]{2,1,0:T(8,128)(2,1)}, u32[]{:S(2)}, u32[]{:S(2)}) collective-permute-start(bf16[16,64,2176]{2,1,0:T(8,128)(2,1)} %bitcast.69), channel_id=1, source_target_pairs={{0,1},{1,0},{2,3},{3,2},{4,5},{5,4},{6,7},{7,6},{8,9},{9,8},{10,11... | collective-permute-start | bytes 13369352 | tf_op jit(solution)/shard_map/ppermute | solution.py:195
  118.1 13.4 %all-to-all-start.2 = ((f32[16,2,2048]{2,1,0:T(2,128)}), f32[16,2,2048]{2,1,0:T(2,128)}, u32[]{:S(2)}, u32[]{:S(2)}) async-start(f32[16,2,2048]{2,1,0:T(2,128)} %get-tuple-element.111), calls=%async_computation.2 | async-start | bytes 524288 | tf_op jit(solution)/shard_map/all_to_all | solution.py:213
  152.8 12.7 %all-to-all-start.4 = ((bf16[16,64,128]{2,1,0:T(8,128)(2,1)}), bf16[16,64,128]{2,1,0:T(8,128)(2,1)S(1)}, u32[]{:S(2)}, u32[]{:S(2)}) async-start(bf16[16,64,128]{2,1,0:T(8,128)(2,1)} %get-tuple-element.117), calls=%async_computation.4 | async-start | bytes 524288 | tf_op jit(solution)/shard_map/all_to_all | solution.py:1275
  186.7 12.7 %all-to-all-start.5 = ((f32[16,2,2048]{2,1,0:T(2,128)}), f32[16,2,2048]{2,1,0:T(2,128)S(1)}, u32[]{:S(2)}, u32[]{:S(2)}) async-start(f32[16,2,2048]{2,1,0:T(2,128)} %get-tuple-element.123), calls=%async_computation.5 | async-start | bytes 524288 | tf_op jit(solution)/shard_map/all_to_all | solution.py:213
  191.9 105.0 %all-gather.4.cloned.1.call-start = ((), (), s32[]{:S(2)}) async-start(), calls=%async_computation.9 | async-start | bytes 2228224 | tf_op jit(solution)/shard_map/all_gather | solution.py:1346
  191.9 60.5 %collective-permute-start.25 = (bf16[288,4608]{1,0:T(8,128)(2,1)}, bf16[288,4608]{1,0:T(8,128)(2,1)}, u32[]{:S(2)}, u32[]{:S(2)}) collective-permute-start(bf16[288,4608]{1,0:T(8,128)(2,1)} %get-tuple-element.141.refs_1_), channel_id=1, source_target_pairs={{0,1},{1,0},{2,3},{3,2},{4,5},{5,4},{6,7},{7,6},{8,9},{9,8},{10,11... | collective-permute-start | bytes 7962632 | tf_op jit(solution)/shard_map/ppermute | solution.py:195
  234.3 11.0 %all-to-all-start.7 = ((f32[16,2,640]{2,1,0:T(2,128)}), f32[16,2,640]{2,1,0:T(2,128)S(1)}, u32[]{:S(2)}, u32[]{:S(2)}) async-start(f32[16,2,640]{2,1,0:T(2,128)} %get-tuple-element.132.refs_10_), calls=%async_computation.7 | async-start | bytes 163840 | tf_op jit(solution)/shard_map/all_to_all | solution.py:213
  261.2 18.9 %collective-permute-start.30 = (bf16[8,288,256]{2,1,0:T(8,128)(2,1)}, bf16[8,288,256]{2,1,0:T(8,128)(2,1)S(1)}, u32[]{:S(2)}, u32[]{:S(2)}) collective-permute-start(bf16[8,288,256]{2,1,0:T(8,128)(2,1)} %get-tuple-element.155), channel_id=1, source_target_pairs={{0,2},{1,5},{2,0},{3,7},{4,6},{5,1},{6,4},{7,3},{8,10},{9,13},{10,... | collective-permute-start | bytes 3538952 | tf_op jit(solution)/shard_map/ppermute | solution.py:204
  262.0 33.8 %collective-permute-start.27 = (bf16[288,2048]{1,0:T(8,128)(2,1)S(1)}, bf16[288,2048]{1,0:T(8,128)(2,1)S(1)}, u32[]{:S(2)}, u32[]{:S(2)}) collective-permute-start(bf16[288,2048]{1,0:T(8,128)(2,1)S(1)} %bitcast.51), channel_id=1, source_target_pairs={{0,1},{1,0},{2,3},{3,2},{4,5},{5,4},{6,7},{7,6},{8,9},{9,8},{10,11... | collective-permute-start | bytes 3538952 | tf_op jit(solution)/shard_map/ppermute | solution.py:195
  284.6 24.4 %collective-permute-start.32 = (bf16[4,288,256]{2,1,0:T(8,128)(2,1)}, bf16[4,288,256]{2,1,0:T(8,128)(2,1)}, u32[]{:S(2)}, u32[]{:S(2)}) collective-permute-start(bf16[4,288,256]{2,1,0:T(8,128)(2,1)} %get-tuple-element.163), channel_id=1, source_target_pairs={{0,4},{1,3},{2,6},{3,1},{4,0},{5,7},{6,2},{7,5},{8,12},{9,11},{10,... | collective-permute-start | bytes 1769480 | tf_op jit(solution)/shard_map/ppermute | solution.py:204
  290.6 10.9 %collective-permute-start.33 = (bf16[4,32,1280]{2,1,0:T(8,128)(2,1)}, bf16[4,32,1280]{2,1,0:T(8,128)(2,1)}, u32[]{:S(2)}, u32[]{:S(2)}) collective-permute-start(bf16[4,32,1280]{2,1,0:T(8,128)(2,1)} %get-tuple-element.164), channel_id=1, source_target_pairs={{0,4},{1,3},{2,6},{3,1},{4,0},{5,7},{6,2},{7,5},{8,12},{9,11},{10,... | collective-permute-start | bytes 983048 | tf_op jit(solution)/shard_map/ppermute | solution.py:204
  307.6 19.4 %collective-permute-start.35 = (f32[144,2048]{1,0:T(8,128)S(1)}, f32[144,2048]{1,0:T(8,128)S(1)}, u32[]{:S(2)}, u32[]{:S(2)}) collective-permute-start(f32[144,2048]{1,0:T(8,128)S(1)} %copy-done.19), channel_id=1, source_target_pairs={{0,1},{1,0},{2,3},{3,2},{4,5},{5,4},{6,7},{7,6},{8,9},{9,8},{10,11... | collective-permute-start | bytes 3538952 | tf_op jit(solution)/shard_map/ppermute | solution.py:195
  314.0 11.1 %collective-permute-start.39 = (bf16[1,288,256]{2,1,0:T(8,128)(2,1)}, bf16[1,288,256]{2,1,0:T(8,128)(2,1)S(1)}, u32[]{:S(2)}, u32[]{:S(2)}) collective-permute-start(bf16[1,288,256]{2,1,0:T(8,128)(2,1)} %get-tuple-element.178), channel_id=1, source_target_pairs={{0,8},{2,10},{4,12},{6,14},{8,0},{10,2},{12,4},{14,6},{16,24},{18,... | collective-permute-start | bytes 442376 | tf_op jit(solution)/shard_map/ppermute | solution.py:199
  315.9 11.0 %collective-permute-start.38 = (bf16[1,288,256]{2,1,0:T(8,128)(2,1)}, bf16[1,288,256]{2,1,0:T(8,128)(2,1)S(1)}, u32[]{:S(2)}, u32[]{:S(2)}) collective-permute-start(bf16[1,288,256]{2,1,0:T(8,128)(2,1)} %get-tuple-element.177), channel_id=1, source_target_pairs={{0,16},{2,18},{4,20},{6,22},{8,24},{10,26},{12,28},{14,30},{16,0},... | collective-permute-start | bytes 442376 | tf_op jit(solution)/shard_map/ppermute | solution.py:199
  318.8 21.0 %collective-permute-start.50 = (f32[128,3072]{1,0:T(8,128)S(1)}, f32[128,3072]{1,0:T(8,128)S(1)}, u32[]{:S(2)}, u32[]{:S(2)}) collective-permute-start(f32[128,3072]{1,0:T(8,128)S(1)} %copy-done.42), channel_id=1, source_target_pairs={{0,1},{1,0},{2,3},{3,2},{4,5},{5,4},{6,7},{7,6},{8,9},{9,8},{10,11... | collective-permute-start | bytes 4718600 | tf_op jit(solution)/shard_map/ppermute | solution.py:195
  334.2 11.3 %collective-permute-start.37 = (f32[10496]{0:T(1024)S(1)}, f32[10496]{0:T(1024)S(1)}, u32[]{:S(2)}, u32[]{:S(2)}) collective-permute-start(f32[10496]{0:T(1024)S(1)} %pad_maximum_fusion.6), channel_id=1, source_target_pairs={{0,1},{1,0},{2,3},{3,2},{4,5},{5,4},{6,7},{7,6},{8,9},{9,8},{10,11... | collective-permute-start | bytes 125960 | tf_op jit(solution)/shard_map/ppermute | solution.py:195
  (90 other events, 825.7 us)
Sparse Core Ops, SparseCore 0:
  25.0 87.5 all-gather.5
  209.2 60.9 all-gather.3

commit v6 on v5

--- a/solution.py
+++ b/solution.py
@@ -185,7 +185,7 @@
     kept, *sent = kernel_call(
         add_parts_kernel,
         [(shape, jnp.float32, PUT_FAR)] + [(shape, jnp.bfloat16, PUT_FAR)] * (count - 1),
-        [Loaded(kept), Loaded(received)],
+        [Loaded(kept), received],
         after=after,
     )
     return kept, sent
@@ -404,7 +404,7 @@
 def weight_grad(left, right, slots, size, second=None, after=()):
     depth, width = left[0].shape[1], right[0].shape[1]
     rows = depth // size
-    args = [Scalars(slots), *left, *right]
+    args = [Scalars(slots), *left, Loaded(right[0]), right[1]]
     scratch, beside, extra = [pltpu.VMEM((depth, width), jnp.float32)], 0, 0
     if second is not None:
         (second_left, second_right, core) = second
@@ -493,9 +493,9 @@
         for (start, stop), (first, second) in self.parts.items():
             first = jnp.sum(first, 0, keepdims=True)
             second = jnp.sum(second, 0, keepdims=True)
+            both = jnp.concatenate([first, second], 0).astype(self.out_ref.dtype)
             for copy in range(self.out_ref.shape[0]):
-                self.out_ref[copy, 0:1, start:stop] = first
-                self.out_ref[copy, 1:2, start:stop] = second
+                self.out_ref[copy, :, start:stop] = both
 
 
 def reduce_kernel(weights, x_ref, *refs):
@@ -669,7 +669,7 @@
     wait = fetch_weight(inputs, weight, sems, CHUNKS)
     step = D // CHUNKS
     head_factors = norm_factors(head_terms, norm_ref, 2, crop_count)
-    totals = jnp.sum(head_back[...], 0)
+    totals = jnp.sum(head_back[...].astype(jnp.float32), 0)
     total_ref[...] = totals
     for columns in (slice(k, k + 512) for k in range(0, D, 512)):
         unit, _ = normalize(head_pre_ref[:, columns], head_factors, columns)
@@ -714,7 +714,7 @@
     pre_terms, back_terms, before_terms, *refs = refs
     kept_ref, sent_ref, out_ref, sums_ref, total_ref, low_ref = refs
     factors = norm_factors(pre_terms, wide_ref, 0, count)
-    totals = jnp.sum(back_terms[...], 0)
+    totals = jnp.sum(back_terms[...].astype(jnp.float32), 0)
     total_ref[...] = totals
     own_rows = own_ref.shape[0]
     for rows, columns in tiles(2 * own_rows, D, 48, 512):
@@ -747,7 +747,7 @@
     kept_ref, sent_ref, out_ref, sums_ref, total_ref, slots, low_ref = refs
     rows = grad_ref.shape[0]
     factors = norm_factors(pre_terms, norm_ref, 2, count)
-    totals = jnp.sum(back_terms[...], 0)
+    totals = jnp.sum(back_terms[...].astype(jnp.float32), 0)
     total_ref[...] = totals
     for high, columns in tiles(rows, MID, 48, 512):
         unit, _ = normalize(pre_ref[high, columns], factors, columns)
@@ -794,7 +794,7 @@
 ):
     rows = grad_ref.shape[0]
     factors = norm_factors(pre_terms, norm_ref, 0, count)
-    totals = jnp.sum(back_terms[...], 0)
+    totals = jnp.sum(back_terms[...].astype(jnp.float32), 0)
     total_ref[...] = totals
     for high, columns in tiles(rows, MID, 48, 512):
         unit, _ = normalize(pre_ref[high, columns], factors, columns)
@@ -1162,6 +1162,8 @@
     mid_rows, wide_rows = ((local_rows, MID), f32), ((local_rows, D), f32)
     mid_sums, wide_sums = ((copies, 2, MID), f32), ((copies, 2, D), f32, PUT_FAR)
 
+    back_sums = ((copies, 2, D), bf16 if copies > 1 else f32, PUT_FAR)
+
     def weight_out(weight):
         return (weight.shape, bf16, FAR)
 
@@ -1297,7 +1299,7 @@
 
     embed_low, head_act_grad, sums, bias_part = kernel_call(
         lambda *refs: embed_back_kernel(crop_total, *refs),
-        [((local_crops, proj), bf16), crop_rows, wide_sums, ((1, proj), f32)],
+        [((local_crops, proj), bf16), crop_rows, back_sums, ((1, proj), f32)],
         [
             unit_grad,
             unit_embed,
@@ -1321,7 +1323,13 @@
     own_part = ((own_rows, D), f32)
     head_low, own_grad, other_grad, sums, total_head = kernel_call(
         lambda *refs: pool_back_kernel(head.count, crop_total, pixel_total, *refs),
-        [((local_crops, D), bf16), own_part, own_part, wide_sums, ((2, D), f32)],
+        [
+            ((local_crops, D), bf16),
+            own_part,
+            own_part + (PUT_FAR,),
+            back_sums,
+            ((2, D), f32, PUT_FAR),
+        ],
         [
             Loaded(head_act_grad),
             Loaded(pre_head),
@@ -1346,17 +1354,22 @@
     right = lax.all_gather(head_low, "dp", axis=0, tiled=True)
 
     def low_halves(width):
-        return [((local_rows, width // 2), bf16)] * 2
+        return [((local_rows, width // 2), bf16, PUT_FAR)] * 2
 
     three_kept, three_sent, two_act_grad, sums, total_three = kernel_call(
         lambda *refs: expand_back_kernel(pixel_total, *refs),
-        [*low_halves(D), mid_rows, ((copies, 2, MID + proj), f32), ((2, D), f32)],
+        [
+            *low_halves(D),
+            mid_rows,
+            ((copies, 2, MID + proj), f32, PUT_FAR),
+            ((2, D), f32, PUT_FAR),
+        ],
         [
             core,
             own_grad,
-            other_grad,
+            Loaded(other_grad),
             Streamed(pre_three),
-            norm_wide,
+            Loaded(norm_wide),
             Streamed(full_expand),
             Streamed(pre_two),
             norm_mid,
@@ -1422,10 +1435,10 @@
     one_low, other_low, one_kept, one_sent, total_one = kernel_call(
         lambda *refs: reduce_back_kernel(pixel_total, *refs),
         [
-            ((local_rows, MID), bf16),
-            ((own_rows, MID), bf16),
+            ((local_rows, MID), bf16, PUT_FAR),
+            ((own_rows, MID), bf16, PUT_FAR),
             *low_halves(MID),
-            ((2, MID), f32),
+            ((2, MID), f32, PUT_FAR),
         ],
         [core, one_act_grad, Streamed(pre_one), norm_mid, terms_one, back_one],
         after=before_one,
@@ -1467,7 +1480,7 @@
         proto_grad = kernel_call(
             proto_grad_kernel,
             [(prototypes.shape, f32)],
-            [Loaded(proto_part), Loaded(proto_other)],
+            [Loaded(proto_part), proto_other],
             after=late,
         )[0]
     else:

time: 360 us -> 357 us (level)
  blocking collectives: 68.8 us -> 82.3 us
  local copies, waits for them, and re-layouts: 22.3 us -> 15 us
  starting transfers between devices: 87.6 us -> 80.5 us
    all_to_all x5 -> x6, blocking collectives: 68.8 us -> 82.3 us  [terms_over_dp(): return lax.all_to_all(copies, 'dp', 0, 0)]
    unnamed x114 -> x100, local copies, waits for them, and re-layouts: 17.7 us -> 10.4 us
    all_to_all x3 -> x2, starting transfers between devices: 13.7 us -> 8.25 us  [terms_over_dp(): return lax.all_to_all(copies, 'dp', 0, 0)]
    all_to_all x3 -> x2, waiting for transfers between devices: 16.1 us -> 12 us  [terms_over_dp(): return lax.all_to_all(copies, 'dp', 0, 0)]
  transfers between devices with their start and end apart: 57 -> 56, of which waited for: 18 -> 16; matrix products, arithmetic and copies ran while one was open for 3% -> 3% of each run, Pallas kernels for 21% -> 27%
where the time goes in v6:
time: 357 us; the launch traced here: 355 us
  Pallas kernels  106 us (30%)
  blocking collectives  82.3 us (23%)
  starting transfers between devices  80.5 us (23%)
  waiting for transfers between devices  47 us (13%)
  between operations  16.7 us (5%)
  local copies, waits for them, and re-layouts  15 us (4%)
  other arithmetic  7.3 us (2%)
    pallas_call x34, Pallas kernels, kernel_call(): pl.pallas_call(kernel, out_shape=[jax.ShapeDtypeStruct(*out) if len(out)...  106 us
    all_to_all x6, blocking collectives, terms_over_dp(): return lax.all_to_all(copies, 'dp', 0, 0)  82.3 us
    ppermute x21, starting transfers between devices, swap_cores(): return lax.ppermute(values, 'shard', [(0, 1), (1, 0)])  30.9 us
    ppermute x18, starting transfers between devices, flip_dp(): return lax.ppermute(values, 'dp', [(i, i ^ bits) for i in range(size)])  27.7 us
    ppermute x18, waiting for transfers between devices, flip_dp(): return lax.ppermute(values, 'dp', [(i, i ^ bits) for i in range(size)])  16.5 us
    all_to_all x2, waiting for transfers between devices, terms_over_dp(): return lax.all_to_all(copies, 'dp', 0, 0)  12 us
    unnamed x100, local copies, waits for them, and re-layouts  10.4 us
    ppermute x21, waiting for transfers between devices, swap_cores(): return lax.ppermute(values, 'shard', [(0, 1), (1, 0)])  8.31 us
  transfers between devices with their start and end apart: 56, of which 16 were waited for; matrix products, arithmetic and copies ran while one was open for 3% of the time, Pallas kernels for 27%

profile of v6, /device:TPU:1, one launch (start us, length us, event | category | flops | bytes accessed | tf_op | source)
XLA Modules:
  0.0 355.3 jit_solution(1495964553556792915)
XLA Ops:
  30.1 4.2 %collective-permute-done.7.refs_3_ = bf16[1,144,512]{2,1,0:T(8,128)(2,1)S(1)} collective-permute-done((bf16[1,144,512]{2,1,0:T(8,128)(2,1)S(1)}, bf16[1,144,512]{2,1,0:T(8,128)(2,1)S(1)}, u32[]{:S(2)}, u32[]{:S(2)}) %collective-permute-start.7) | collective-permute-done | bytes 147488 | tf_op jit(solution)/shard_map/ppermute | solution.py:199
  34.3 4.3 %collective-permute-done.9.refs_5_ = bf16[1,144,512]{2,1,0:T(8,128)(2,1)S(1)} collective-permute-done((bf16[1,144,512]{2,1,0:T(8,128)(2,1)S(1)}, bf16[1,144,512]{2,1,0:T(8,128)(2,1)S(1)}, u32[]{:S(2)}, u32[]{:S(2)}) %collective-permute-start.9) | collective-permute-done | bytes 147488 | tf_op jit(solution)/shard_map/ppermute | solution.py:199
  43.9 7.6 %collective-permute-start.12 = (bf16[1,16,2304]{2,1,0:T(8,128)(2,1)S(1)}, bf16[1,16,2304]{2,1,0:T(8,128)(2,1)S(1)}, u32[]{:S(2)}, u32[]{:S(2)}) collective-permute-start(bf16[1,16,2304]{2,1,0:T(8,128)(2,1)S(1)} %bitcast.61), channel_id=1, source_target_pairs={{0,16},{2,18},{4,20},{6,22},{8,24},{10,26},{12,28},{14,30},{16,0},... | collective-permute-start | bytes 221192 | tf_op jit(solution)/shard_map/ppermute | solution.py:199
  58.7 16.1 %all_to_all.45.refs_2_.refs_3_.refs_9_.refs_4_ = f32[16,2,512]{2,1,0:T(2,128)} all-to-all(f32[16,2,512]{2,1,0:T(2,128)S(1)} %copy-done.28), channel_id=1, replica_groups=mesh['dp'=16,'shard'=2] {'dp'}, dimensions={0} | all-to-all | bytes 131072 | tf_op jit(solution)/shard_map/all_to_all | solution.py:213
  75.0 5.4 %collective-permute-start.16 = (bf16[16,144,512]{2,1,0:T(8,128)(2,1)S(1)}, bf16[16,144,512]{2,1,0:T(8,128)(2,1)S(1)}, u32[]{:S(2)}, u32[]{:S(2)}) collective-permute-start(bf16[16,144,512]{2,1,0:T(8,128)(2,1)S(1)} %shard_map.230.refs_5_), channel_id=1, source_target_pairs={{0,1},{1,0},{2,3},{3,2},{4,5},{5,4},{6,7},{7,6},{8,9},{9,8},{10,11... | collective-permute-start | bytes 7077896 | tf_op jit(solution)/shard_map/ppermute | solution.py:195
  86.2 6.5 %shard_map.231 = (f32[288,512]{1,0:T(8,128)S(1)}, f32[16,2,512]{2,1,0:T(2,128)S(1)}, bf16[288,4608]{1,0:T(8,128)(2,1)}, bf16[4608,512]{1,0:T(8,128)(2,1)}) custom-call(f32[288,512]{1,0:T(8,128)S(1)} %get-tuple-element.103.refs_0_.refs_5_.refs_2_, f32[4,512]{1,0:T(4,128)S(1)} %copy-done.30, f32[288,16]{1,0:T(8,128)S(1)} %copy-done.25, ...), custom_call_target="tpu_custom_call" | custom-call | flops 1358954496 | bytes 5400704 | tf_op jit(solution)/shard_map/pallas_call | solution.py:117
  93.7 13.9 %all_to_all.46.refs_2_.refs_11_.refs_7_ = f32[16,2,512]{2,1,0:T(2,128)} all-to-all(f32[16,2,512]{2,1,0:T(2,128)} %copy-done.29), channel_id=1, replica_groups=mesh['dp'=16,'shard'=2] {'dp'}, dimensions={0} | all-to-all | bytes 131072 | tf_op jit(solution)/shard_map/all_to_all | solution.py:213
  112.8 4.9 %shard_map.234 = (bf16[288,512]{1,0:T(8,128)(2,1)}, f32[288,2048]{1,0:T(8,128)S(1)}, f32[16,2,2048]{2,1,0:T(2,128)}, bf16[512,2304]{1,0:T(8,128)(2,1)}, bf16[512,256]{1,0:T(8,128)(2,1)}) custom-call(f32[288,512]{1,0:T(8,128)S(1)} %get-tuple-element.107.refs_0_.refs_6_.refs_2_, f32[4,512]{1,0:T(4,128)S(1)} %copy-done.30, f32[16,2,512]{2,1,0:T(2,128)S(1)} %copy-done.17, ...), custom_call_target="tpu_custom_call" | custom-call | flops 603979776 | bytes 3022976 | tf_op jit(solution)/shard_map/pallas_call | solution.py:117
  118.1 4.5 %all-to-all-start.2 = ((f32[16,2,2048]{2,1,0:T(2,128)}), f32[16,2,2048]{2,1,0:T(2,128)}, u32[]{:S(2)}, u32[]{:S(2)}) async-start(f32[16,2,2048]{2,1,0:T(2,128)} %get-tuple-element.111), calls=%async_computation.2 | async-start | bytes 524288 | tf_op jit(solution)/shard_map/all_to_all | solution.py:213
  122.7 8.9 %all-to-all-done.2.refs_5_.refs_9_ = f32[16,2,2048]{2,1,0:T(2,128)} async-done(((f32[16,2,2048]{2,1,0:T(2,128)}), f32[16,2,2048]{2,1,0:T(2,128)}, u32[]{:S(2)}, u32[]{:S(2)}) %all-to-all-start.2) | async-done | bytes 262176 | tf_op jit(solution)/shard_map/all_to_all | solution.py:213
  131.6 6.3 %shard_map.236 = (bf16[32,2048]{1,0:T(8,128)(2,1)}, f32[32,2048]{1,0:T(8,128)}, f32[16,2,2048]{2,1,0:T(2,128)}, bf16[2048,128]{1,0:T(8,128)(2,1)}) custom-call(f32[288,2048]{1,0:T(8,128)S(1)} %get-tuple-element.110.refs_0_.refs_2_.refs_3_, bf16[288,2048]{1,0:T(8,128)(2,1)S(1)} %bitcast.50, f32[4,2048]{1,0:T(4,128)} %refs_4_.3, ...), custom_call_target="tpu_custom_call" | custom-call | flops 268435456 | bytes 12765440 | tf_op jit(solution)/shard_map/pallas_call | solution.py:117
  137.9 11.8 %all_to_all.47.refs_5_.refs_6_.refs_7_ = f32[16,2,2048]{2,1,0:T(2,128)S(1)} all-to-all(f32[16,2,2048]{2,1,0:T(2,128)} %get-tuple-element.116), channel_id=1, replica_groups=mesh['dp'=16,'shard'=2] {'dp'}, dimensions={0} | all-to-all | bytes 524288 | tf_op jit(solution)/shard_map/all_to_all | solution.py:213
  152.8 5.2 %all-to-all-start.4 = ((bf16[16,64,128]{2,1,0:T(8,128)(2,1)}), bf16[16,64,128]{2,1,0:T(8,128)(2,1)S(1)}, u32[]{:S(2)}, u32[]{:S(2)}) async-start(bf16[16,64,128]{2,1,0:T(8,128)(2,1)} %get-tuple-element.117), calls=%async_computation.4 | async-start | bytes 524288 | tf_op jit(solution)/shard_map/all_to_all | solution.py:1277
  159.9 5.5 %all-to-all-done.4.refs_1_ = bf16[16,64,128]{2,1,0:T(8,128)(2,1)S(1)} async-done(((bf16[16,64,128]{2,1,0:T(8,128)(2,1)}), bf16[16,64,128]{2,1,0:T(8,128)(2,1)S(1)}, u32[]{:S(2)}, u32[]{:S(2)}) %all-to-all-start.4) | async-done | bytes 262176 | tf_op jit(solution)/shard_map/all_to_all | solution.py:1277
  165.4 18.2 %shard_map.238 = (f32[8,128]{1,0:T(8,128)S(1)}, f32[128,3072]{1,0:T(8,128)}, f32[32,128]{1,0:T(8,128)S(1)}) custom-call(s32[2]{0:T(128)S(1)} %pad_add_fusion.1.refs_0_, bf16[16,64,128]{2,1,0:T(8,128)(2,1)S(1)} %all-to-all-done.4.refs_1_, bf16[512,256]{1,0:T(8,128)(2,1)} %get-tuple-element.118.refs_2_, bf16[3000,128]{1,0:T(8,128)(2,1)} %refs_3_.3), custom_call_target="tpu_custom_call" | custom-call | flops 3221225472 | bytes 1292296 | tf_op jit(solution)/shard_map/pallas_call | solution.py:117
  186.6 11.9 %all_to_all.48.refs_8_ = bf16[16,2,2048]{2,1,0:T(2,128)(2,1)S(1)} all-to-all(bf16[16,2,2048]{2,1,0:T(2,128)(2,1)} %get-tuple-element.123), channel_id=1, replica_groups=mesh['dp'=16,'shard'=2] {'dp'}, dimensions={0} | all-to-all | bytes 262144 | tf_op jit(solution)/shard_map/all_to_all | solution.py:213
  198.5 9.9 %shard_map.240 = (bf16[32,2048]{1,0:T(8,128)(2,1)}, f32[144,2048]{1,0:T(8,128)S(1)}, f32[144,2048]{1,0:T(8,128)}, bf16[16,2,2048]{2,1,0:T(2,128)(2,1)}, f32[2,2048]{1,0:T(2,128)}) custom-call(f32[32,2048]{1,0:T(8,128)} %get-tuple-element.122.refs_0_, f32[32,2048]{1,0:T(8,128)} %get-tuple-element.113.refs_0_.refs_4_.refs_1_, f32[288,2048]{1,0:T(8,128)} %copy-done.3, ...), custom_call_target="tpu_custom_call" | custom-call | flops 268435456 | bytes 13682944 | tf_op jit(solution)/shard_map/pallas_call | solution.py:117
  208.5 10.3 %all_to_all.49.refs_10_ = bf16[16,2,2048]{2,1,0:T(2,128)(2,1)S(1)} all-to-all(bf16[16,2,2048]{2,1,0:T(2,128)(2,1)} %get-tuple-element.126), channel_id=1, replica_groups=mesh['dp'=16,'shard'=2] {'dp'}, dimensions={0} | all-to-all | bytes 262144 | tf_op jit(solution)/shard_map/all_to_all | solution.py:213
  218.8 6.2 %shard_map.241 = (bf16[288,1024]{1,0:T(8,128)(2,1)}, bf16[288,1024]{1,0:T(8,128)(2,1)}, f32[288,512]{1,0:T(8,128)S(1)}, f32[16,2,640]{2,1,0:T(2,128)}, f32[2,2048]{1,0:T(2,128)}) custom-call(s32[1]{0:T(128)} %bitcast.refs_0_.refs_9_, f32[144,2048]{1,0:T(8,128)S(1)} %get-tuple-element.124.refs_1_, f32[144,2048]{1,0:T(8,128)} %get-tuple-element.127.refs_2_, ...), custom_call_target="tpu_custom_call" | custom-call | flops 603979776 | bytes 8167940 | tf_op jit(solution)/shard_map/pallas_call | solution.py:117
  233.3 4.5 %shard_map.242 = (f32[8,32,1280]{2,1,0:T(8,128)}, bf16[8,32,1280]{2,1,0:T(8,128)(2,1)}) custom-call(s32[16]{0:T(128)S(1)} %fusion.20.refs_0_, bf16[288,512]{1,0:T(8,128)(2,1)} %get-tuple-element.133.refs_1_, bf16[288,512]{1,0:T(8,128)(2,1)} %collective-permute-done.21.refs_2_, bf16[288,1024]{1,0:T(8,128)(2,1)} %get-tuple-element.134.refs_3_, ...), custom_call_target="tpu_custom_call" | custom-call | flops 603979776 | bytes 2048068 | tf_op jit(solution)/shard_map/pallas_call | solution.py:117
  240.9 5.1 %shard_map.243 = (bf16[288,256]{1,0:T(8,128)(2,1)}, bf16[288,256]{1,0:T(8,128)(2,1)}, f32[288,512]{1,0:T(8,128)S(1)}, f32[16,2,512]{2,1,0:T(2,128)S(1)}, f32[2,640]{1,0:T(2,128)S(1)}) custom-call(s32[1]{0:T(128)} %bitcast.refs_0_.refs_9_, f32[288,512]{1,0:T(8,128)S(1)} %get-tuple-element.130.refs_1_, f32[288,512]{1,0:T(8,128)} %copy-done.5, ...), custom_call_target="tpu_custom_call" | custom-call | flops 1358954496 | bytes 6727684 | tf_op jit(solution)/shard_map/pallas_call | solution.py:117
  248.1 6.9 %shard_map.244 = (f32[8,288,256]{2,1,0:T(8,128)}, bf16[8,288,256]{2,1,0:T(8,128)(2,1)}) custom-call(s32[16]{0:T(128)S(1)} %fusion.20.refs_0_, bf16[288,4608]{1,0:T(8,128)(2,1)S(1)} %copy-done.10, bf16[288,4608]{1,0:T(8,128)(2,1)} %collective-permute-done.25.refs_2_, bf16[288,256]{1,0:T(8,128)(2,1)} %get-tuple-element.142.refs_3_, ...), custom_call_target="tpu_custom_call" | custom-call | flops 1358954496 | bytes 5603392 | tf_op jit(solution)/shard_map/pallas_call | solution.py:117
  256.9 18.2 %all_to_all.50.refs_5_ = f32[16,2,512]{2,1,0:T(2,128)S(1)} all-to-all(f32[16,2,512]{2,1,0:T(2,128)S(1)} %get-tuple-element.145), channel_id=1, replica_groups=mesh['dp'=16,'shard'=2] {'dp'}, dimensions={0} | all-to-all | bytes 131072 | tf_op jit(solution)/shard_map/all_to_all | solution.py:213
  288.4 4.6 %collective-permute-start.28 = (bf16[288,256]{1,0:T(8,128)(2,1)S(1)}, bf16[288,256]{1,0:T(8,128)(2,1)S(1)}, u32[]{:S(2)}, u32[]{:S(2)}) collective-permute-start(bf16[288,256]{1,0:T(8,128)(2,1)S(1)} %copy-done.48), channel_id=1, source_target_pairs={{0,1},{1,0},{2,3},{3,2},{4,5},{5,4},{6,7},{7,6},{8,9},{9,8},{10,11... | collective-permute-start | bytes 442376 | tf_op jit(solution)/shard_map/ppermute | solution.py:195
  (286 shorter events, 137.5 us)
Async XLA Ops:
  7.2 110.5 %all-gather.6.cloned.1.call-start = ((), (), s32[]{:S(2)}) async-start(), calls=%async_computation.10 | async-start | bytes 4734976 | tf_op jit(solution)/shard_map/all_gather | solution.py:1155
  7.2 10.4 %collective-permute-start.1 = (bf16[1,64,512]{2,1,0:T(8,128)(2,1)}, bf16[1,64,512]{2,1,0:T(8,128)(2,1)S(1)}, u32[]{:S(2)}, u32[]{:S(2)}) collective-permute-start(bf16[1,64,512]{2,1,0:T(8,128)(2,1)} %bitcast.65), channel_id=1, source_target_pairs={{0,16},{2,18},{4,20},{6,22},{8,24},{10,26},{12,28},{14,30},{16,0},... | collective-permute-start | bytes 196616 | tf_op jit(solution)/shard_map/ppermute | solution.py:199
  24.9 13.7 %collective-permute-start.6 = (bf16[8,64,512]{2,1,0:T(8,128)(2,1)}, bf16[8,64,512]{2,1,0:T(8,128)(2,1)S(1)}, u32[]{:S(2)}, u32[]{:S(2)}) collective-permute-start(bf16[8,64,512]{2,1,0:T(8,128)(2,1)} %copy-done.8), channel_id=1, source_target_pairs={{0,2},{1,5},{2,0},{3,7},{4,6},{5,1},{6,4},{7,3},{8,10},{9,13},{10,... | collective-permute-start | bytes 1572872 | tf_op jit(solution)/shard_map/ppermute | solution.py:204
  39.8 13.1 %collective-permute-start.10 = (bf16[16,64,512]{2,1,0:T(8,128)(2,1)S(1)}, bf16[16,64,512]{2,1,0:T(8,128)(2,1)}, u32[]{:S(2)}, u32[]{:S(2)}) collective-permute-start(bf16[16,64,512]{2,1,0:T(8,128)(2,1)S(1)} %get-tuple-element.102.refs_2_), channel_id=1, source_target_pairs={{0,1},{1,0},{2,3},{3,2},{4,5},{5,4},{6,7},{7,6},{8,9},{9,8},{10,11... | collective-permute-start | bytes 3145736 | tf_op jit(solution)/shard_map/ppermute | solution.py:195
  43.4 15.0 %collective-permute-start.11 = (bf16[4,144,512]{2,1,0:T(8,128)(2,1)S(1)}, bf16[4,144,512]{2,1,0:T(8,128)(2,1)S(1)}, u32[]{:S(2)}, u32[]{:S(2)}) collective-permute-start(bf16[4,144,512]{2,1,0:T(8,128)(2,1)S(1)} %get-tuple-element.105.refs_1_.refs_0_), channel_id=1, source_target_pairs={{0,4},{1,3},{2,6},{3,1},{4,0},{5,7},{6,2},{7,5},{8,12},{9,11},{10,... | collective-permute-start | bytes 1769480 | tf_op jit(solution)/shard_map/ppermute | solution.py:204
  43.9 13.4 %collective-permute-start.12 = (bf16[1,16,2304]{2,1,0:T(8,128)(2,1)S(1)}, bf16[1,16,2304]{2,1,0:T(8,128)(2,1)S(1)}, u32[]{:S(2)}, u32[]{:S(2)}) collective-permute-start(bf16[1,16,2304]{2,1,0:T(8,128)(2,1)S(1)} %bitcast.61), channel_id=1, source_target_pairs={{0,16},{2,18},{4,20},{6,22},{8,24},{10,26},{12,28},{14,30},{16,0},... | collective-permute-start | bytes 221192 | tf_op jit(solution)/shard_map/ppermute | solution.py:199
  58.6 16.2 %collective-permute-start.15 = (bf16[8,144,512]{2,1,0:T(8,128)(2,1)S(1)}, bf16[8,144,512]{2,1,0:T(8,128)(2,1)S(1)}, u32[]{:S(2)}, u32[]{:S(2)}) collective-permute-start(bf16[8,144,512]{2,1,0:T(8,128)(2,1)S(1)} %get-tuple-element.106.refs_0_), channel_id=1, source_target_pairs={{0,2},{1,5},{2,0},{3,7},{4,6},{5,1},{6,4},{7,3},{8,10},{9,13},{10,... | collective-permute-start | bytes 3538952 | tf_op jit(solution)/shard_map/ppermute | solution.py:204
  80.5 12.9 %collective-permute-start.17 = (bf16[4,16,2304]{2,1,0:T(8,128)(2,1)S(1)}, bf16[4,16,2304]{2,1,0:T(8,128)(2,1)S(1)}, u32[]{:S(2)}, u32[]{:S(2)}) collective-permute-start(bf16[4,16,2304]{2,1,0:T(8,128)(2,1)S(1)} %get-tuple-element.109.refs_0_), channel_id=1, source_target_pairs={{0,4},{1,3},{2,6},{3,1},{4,0},{5,7},{6,2},{7,5},{8,12},{9,11},{10,... | collective-permute-start | bytes 884744 | tf_op jit(solution)/shard_map/ppermute | solution.py:204
  93.4 14.3 %collective-permute-start.18 = (bf16[8,16,2304]{2,1,0:T(8,128)(2,1)S(1)}, bf16[8,16,2304]{2,1,0:T(8,128)(2,1)S(1)}, u32[]{:S(2)}, u32[]{:S(2)}) collective-permute-start(bf16[8,16,2304]{2,1,0:T(8,128)(2,1)S(1)} %shard_map.232.refs_0_), channel_id=1, source_target_pairs={{0,2},{1,5},{2,0},{3,7},{4,6},{5,1},{6,4},{7,3},{8,10},{9,13},{10,... | collective-permute-start | bytes 1769480 | tf_op jit(solution)/shard_map/ppermute | solution.py:204
  117.7 13.9 %collective-permute-start.20 = (bf16[16,64,2176]{2,1,0:T(8,128)(2,1)}, bf16[16,64,2176]{2,1,0:T(8,128)(2,1)}, u32[]{:S(2)}, u32[]{:S(2)}) collective-permute-start(bf16[16,64,2176]{2,1,0:T(8,128)(2,1)} %bitcast.69), channel_id=1, source_target_pairs={{0,1},{1,0},{2,3},{3,2},{4,5},{5,4},{6,7},{7,6},{8,9},{9,8},{10,11... | collective-permute-start | bytes 13369352 | tf_op jit(solution)/shard_map/ppermute | solution.py:195
  118.1 13.4 %all-to-all-start.2 = ((f32[16,2,2048]{2,1,0:T(2,128)}), f32[16,2,2048]{2,1,0:T(2,128)}, u32[]{:S(2)}, u32[]{:S(2)}) async-start(f32[16,2,2048]{2,1,0:T(2,128)} %get-tuple-element.111), calls=%async_computation.2 | async-start | bytes 524288 | tf_op jit(solution)/shard_map/all_to_all | solution.py:213
  152.8 12.7 %all-to-all-start.4 = ((bf16[16,64,128]{2,1,0:T(8,128)(2,1)}), bf16[16,64,128]{2,1,0:T(8,128)(2,1)S(1)}, u32[]{:S(2)}, u32[]{:S(2)}) async-start(bf16[16,64,128]{2,1,0:T(8,128)(2,1)} %get-tuple-element.117), calls=%async_computation.4 | async-start | bytes 524288 | tf_op jit(solution)/shard_map/all_to_all | solution.py:1277
  158.0 136.1 %all-gather.4.cloned.1.call-start = ((), (), s32[]{:S(2)}) async-start(), calls=%async_computation.9 | async-start | bytes 2228224 | tf_op jit(solution)/shard_map/all_gather | solution.py:1354
  158.3 88.6 %collective-permute-start.25 = (bf16[288,4608]{1,0:T(8,128)(2,1)}, bf16[288,4608]{1,0:T(8,128)(2,1)}, u32[]{:S(2)}, u32[]{:S(2)}) collective-permute-start(bf16[288,4608]{1,0:T(8,128)(2,1)} %get-tuple-element.141.refs_1_), channel_id=1, source_target_pairs={{0,1},{1,0},{2,3},{3,2},{4,5},{5,4},{6,7},{7,6},{8,9},{9,8},{10,11... | collective-permute-start | bytes 7962632 | tf_op jit(solution)/shard_map/ppermute | solution.py:195
  229.5 11.4 %all-to-all-start.7 = ((f32[16,2,640]{2,1,0:T(2,128)}), f32[16,2,640]{2,1,0:T(2,128)S(1)}, u32[]{:S(2)}, u32[]{:S(2)}) async-start(f32[16,2,640]{2,1,0:T(2,128)} %get-tuple-element.132.refs_10_), calls=%async_computation.7 | async-start | bytes 163840 | tf_op jit(solution)/shard_map/all_to_all | solution.py:213
  255.0 22.1 %collective-permute-start.30 = (bf16[8,288,256]{2,1,0:T(8,128)(2,1)}, bf16[8,288,256]{2,1,0:T(8,128)(2,1)S(1)}, u32[]{:S(2)}, u32[]{:S(2)}) collective-permute-start(bf16[8,288,256]{2,1,0:T(8,128)(2,1)} %get-tuple-element.155), channel_id=1, source_target_pairs={{0,2},{1,5},{2,0},{3,7},{4,6},{5,1},{6,4},{7,3},{8,10},{9,13},{10,... | collective-permute-start | bytes 3538952 | tf_op jit(solution)/shard_map/ppermute | solution.py:204
  255.6 37.5 %collective-permute-start.27 = (bf16[288,2048]{1,0:T(8,128)(2,1)S(1)}, bf16[288,2048]{1,0:T(8,128)(2,1)S(1)}, u32[]{:S(2)}, u32[]{:S(2)}) collective-permute-start(bf16[288,2048]{1,0:T(8,128)(2,1)S(1)} %bitcast.51), channel_id=1, source_target_pairs={{0,1},{1,0},{2,3},{3,2},{4,5},{5,4},{6,7},{7,6},{8,9},{9,8},{10,11... | collective-permute-start | bytes 3538952 | tf_op jit(solution)/shard_map/ppermute | solution.py:195
  280.3 26.9 %collective-permute-start.32 = (bf16[4,288,256]{2,1,0:T(8,128)(2,1)}, bf16[4,288,256]{2,1,0:T(8,128)(2,1)S(1)}, u32[]{:S(2)}, u32[]{:S(2)}) collective-permute-start(bf16[4,288,256]{2,1,0:T(8,128)(2,1)} %get-tuple-element.163), channel_id=1, source_target_pairs={{0,4},{1,3},{2,6},{3,1},{4,0},{5,7},{6,2},{7,5},{8,12},{9,11},{10,... | collective-permute-start | bytes 1769480 | tf_op jit(solution)/shard_map/ppermute | solution.py:204
  287.2 11.9 %collective-permute-start.33 = (bf16[4,32,1280]{2,1,0:T(8,128)(2,1)}, bf16[4,32,1280]{2,1,0:T(8,128)(2,1)}, u32[]{:S(2)}, u32[]{:S(2)}) collective-permute-start(bf16[4,32,1280]{2,1,0:T(8,128)(2,1)} %get-tuple-element.164), channel_id=1, source_target_pairs={{0,4},{1,3},{2,6},{3,1},{4,0},{5,7},{6,2},{7,5},{8,12},{9,11},{10,... | collective-permute-start | bytes 983048 | tf_op jit(solution)/shard_map/ppermute | solution.py:204
  305.1 20.7 %collective-permute-start.35 = (f32[144,2048]{1,0:T(8,128)}, f32[144,2048]{1,0:T(8,128)S(1)}, u32[]{:S(2)}, u32[]{:S(2)}) collective-permute-start(f32[144,2048]{1,0:T(8,128)} %get-tuple-element.127.refs_2_), channel_id=1, source_target_pairs={{0,1},{1,0},{2,3},{3,2},{4,5},{5,4},{6,7},{7,6},{8,9},{9,8},{10,11... | collective-permute-start | bytes 3538952 | tf_op jit(solution)/shard_map/ppermute | solution.py:195
  314.6 11.1 %collective-permute-start.38 = (bf16[1,288,256]{2,1,0:T(8,128)(2,1)}, bf16[1,288,256]{2,1,0:T(8,128)(2,1)S(1)}, u32[]{:S(2)}, u32[]{:S(2)}) collective-permute-start(bf16[1,288,256]{2,1,0:T(8,128)(2,1)} %get-tuple-element.177), channel_id=1, source_target_pairs={{0,16},{2,18},{4,20},{6,22},{8,24},{10,26},{12,28},{14,30},{16,0},... | collective-permute-start | bytes 442376 | tf_op jit(solution)/shard_map/ppermute | solution.py:199
  316.0 20.7 %collective-permute-start.50 = (f32[128,3072]{1,0:T(8,128)S(1)}, f32[128,3072]{1,0:T(8,128)S(1)}, u32[]{:S(2)}, u32[]{:S(2)}) collective-permute-start(f32[128,3072]{1,0:T(8,128)S(1)} %copy-done.35), channel_id=1, source_target_pairs={{0,1},{1,0},{2,3},{3,2},{4,5},{5,4},{6,7},{7,6},{8,9},{9,8},{10,11... | collective-permute-start | bytes 4718600 | tf_op jit(solution)/shard_map/ppermute | solution.py:195
  331.6 10.4 %collective-permute-start.37 = (f32[10496]{0:T(1024)S(1)}, f32[10496]{0:T(1024)S(1)}, u32[]{:S(2)}, u32[]{:S(2)}) collective-permute-start(f32[10496]{0:T(1024)S(1)} %pad_maximum_fusion.6), channel_id=1, source_target_pairs={{0,1},{1,0},{2,3},{3,2},{4,5},{5,4},{6,7},{7,6},{8,9},{9,8},{10,11... | collective-permute-start | bytes 125960 | tf_op jit(solution)/shard_map/ppermute | solution.py:195
  336.7 9.8 %collective-permute-start.49 = (f32[64,2048]{1,0:T(8,128)S(1)}, f32[64,2048]{1,0:T(8,128)S(1)}, u32[]{:S(2)}, u32[]{:S(2)}) collective-permute-start(f32[64,2048]{1,0:T(8,128)S(1)} %constant_dynamic-slice_fusion), channel_id=1, source_target_pairs={{0,1},{1,0},{2,3},{3,2},{4,5},{5,4},{6,7},{7,6},{8,9},{9,8},{10,11... | collective-permute-start | bytes 1572872 | tf_op jit(solution)/shard_map/ppermute | solution.py:195
  (82 other events, 780.0 us)
Sparse Core Ops, SparseCore 0:
  25.0 87.4 all-gather.5
  208.7 61.6 all-gather.3

commit v7 on v6

--- a/solution.py
+++ b/solution.py
@@ -25,7 +25,7 @@
 BOTH = ("dp", "shard")
 GATHERED_CODES_BYTES = 32 * 2**20
 MIB = 2**20
-LANES = 512
+LANES = 768
 CHUNKS = 4
 
 
@@ -737,7 +737,7 @@
     sums.store()
     bias = jnp.concatenate([bias_ref[...], jnp.zeros_like(bias_ref)], 0)
     for copy in range(sums_ref.shape[0]):
-        sums_ref[copy, :, MID:] = bias
+        sums_ref[copy, :, MID:] = bias.astype(sums_ref.dtype)
 
 
 def spatial_back_kernel(
@@ -1162,7 +1162,8 @@
     mid_rows, wide_rows = ((local_rows, MID), f32), ((local_rows, D), f32)
     mid_sums, wide_sums = ((copies, 2, MID), f32), ((copies, 2, D), f32, PUT_FAR)
 
-    back_sums = ((copies, 2, D), bf16 if copies > 1 else f32, PUT_FAR)
+    back_type = bf16 if copies > 1 else f32
+    back_sums = ((copies, 2, D), back_type, PUT_FAR)
 
     def weight_out(weight):
         return (weight.shape, bf16, FAR)
@@ -1361,7 +1362,7 @@
         [
             *low_halves(D),
             mid_rows,
-            ((copies, 2, MID + proj), f32, PUT_FAR),
+            ((copies, 2, MID + proj), back_type, PUT_FAR),
             ((2, D), f32, PUT_FAR),
         ],
         [
@@ -1400,7 +1401,12 @@
 
     two_kept, two_sent, one_act_grad, sums, total_two = kernel_call(
         lambda *refs: spatial_back_kernel(pixel_total, *refs),
-        [*low_halves(MID), mid_rows, mid_sums, ((2, MID + proj), f32)],
+        [
+            *low_halves(MID),
+            mid_rows,
+            ((copies, 2, MID), back_type),
+            ((2, MID + proj), f32),
+        ],
         [
             core,
             two_act_grad,

time: 357 us -> 356 us (level)
  no operation moved by 1% of the time
where the time goes in v7:
time: 356 us; the launch traced here: 354 us
  Pallas kernels  106 us (30%)
  blocking collectives  82.9 us (23%)
  starting transfers between devices  80.5 us (23%)
  waiting for transfers between devices  45.6 us (13%)
  between operations  16.7 us (5%)
  local copies, waits for them, and re-layouts  15 us (4%)
  other arithmetic  7.3 us (2%)
    pallas_call x34, Pallas kernels, kernel_call(): pl.pallas_call(kernel, out_shape=[jax.ShapeDtypeStruct(*out) if len(out)...  106 us
    all_to_all x6, blocking collectives, terms_over_dp(): return lax.all_to_all(copies, 'dp', 0, 0)  82.9 us
    ppermute x21, starting transfers between devices, swap_cores(): return lax.ppermute(values, 'shard', [(0, 1), (1, 0)])  31.1 us
    ppermute x18, starting transfers between devices, flip_dp(): return lax.ppermute(values, 'dp', [(i, i ^ bits) for i in range(size)])  27.7 us
    ppermute x18, waiting for transfers between devices, flip_dp(): return lax.ppermute(values, 'dp', [(i, i ^ bits) for i in range(size)])  16.5 us
    all_to_all x2, waiting for transfers between devices, terms_over_dp(): return lax.all_to_all(copies, 'dp', 0, 0)  10.6 us
    unnamed x100, local copies, waits for them, and re-layouts  10.4 us
    ppermute x21, waiting for transfers between devices, swap_cores(): return lax.ppermute(values, 'shard', [(0, 1), (1, 0)])  8.31 us
  transfers between devices with their start and end apart: 56, of which 16 were waited for; matrix products, arithmetic and copies ran while one was open for 3% of the time, Pallas kernels for 27%

profile of v7, /device:TPU:1, one launch (start us, length us, event | category | flops | bytes accessed | tf_op | source)
XLA Modules:
  0.0 354.2 jit_solution(14968286335192923108)
XLA Ops:
  30.1 4.2 %collective-permute-done.7.refs_3_ = bf16[1,144,512]{2,1,0:T(8,128)(2,1)S(1)} collective-permute-done((bf16[1,144,512]{2,1,0:T(8,128)(2,1)S(1)}, bf16[1,144,512]{2,1,0:T(8,128)(2,1)S(1)}, u32[]{:S(2)}, u32[]{:S(2)}) %collective-permute-start.7) | collective-permute-done | bytes 147488 | tf_op jit(solution)/shard_map/ppermute | solution.py:199
  34.3 4.3 %collective-permute-done.9.refs_5_ = bf16[1,144,512]{2,1,0:T(8,128)(2,1)S(1)} collective-permute-done((bf16[1,144,512]{2,1,0:T(8,128)(2,1)S(1)}, bf16[1,144,512]{2,1,0:T(8,128)(2,1)S(1)}, u32[]{:S(2)}, u32[]{:S(2)}) %collective-permute-start.9) | collective-permute-done | bytes 147488 | tf_op jit(solution)/shard_map/ppermute | solution.py:199
  43.9 7.6 %collective-permute-start.12 = (bf16[1,16,2304]{2,1,0:T(8,128)(2,1)S(1)}, bf16[1,16,2304]{2,1,0:T(8,128)(2,1)S(1)}, u32[]{:S(2)}, u32[]{:S(2)}) collective-permute-start(bf16[1,16,2304]{2,1,0:T(8,128)(2,1)S(1)} %bitcast.61), channel_id=1, source_target_pairs={{0,16},{2,18},{4,20},{6,22},{8,24},{10,26},{12,28},{14,30},{16,0},... | collective-permute-start | bytes 221192 | tf_op jit(solution)/shard_map/ppermute | solution.py:199
  58.7 16.1 %all_to_all.45.refs_2_.refs_3_.refs_9_.refs_4_ = f32[16,2,512]{2,1,0:T(2,128)} all-to-all(f32[16,2,512]{2,1,0:T(2,128)S(1)} %copy-done.28), channel_id=1, replica_groups=mesh['dp'=16,'shard'=2] {'dp'}, dimensions={0} | all-to-all | bytes 131072 | tf_op jit(solution)/shard_map/all_to_all | solution.py:213
  75.0 5.4 %collective-permute-start.16 = (bf16[16,144,512]{2,1,0:T(8,128)(2,1)S(1)}, bf16[16,144,512]{2,1,0:T(8,128)(2,1)S(1)}, u32[]{:S(2)}, u32[]{:S(2)}) collective-permute-start(bf16[16,144,512]{2,1,0:T(8,128)(2,1)S(1)} %shard_map.230.refs_5_), channel_id=1, source_target_pairs={{0,1},{1,0},{2,3},{3,2},{4,5},{5,4},{6,7},{7,6},{8,9},{9,8},{10,11... | collective-permute-start | bytes 7077896 | tf_op jit(solution)/shard_map/ppermute | solution.py:195
  86.2 6.5 %shard_map.231 = (f32[288,512]{1,0:T(8,128)S(1)}, f32[16,2,512]{2,1,0:T(2,128)S(1)}, bf16[288,4608]{1,0:T(8,128)(2,1)}, bf16[4608,512]{1,0:T(8,128)(2,1)}) custom-call(f32[288,512]{1,0:T(8,128)S(1)} %get-tuple-element.103.refs_0_.refs_5_.refs_2_, f32[4,512]{1,0:T(4,128)S(1)} %copy-done.30, f32[288,16]{1,0:T(8,128)S(1)} %copy-done.25, ...), custom_call_target="tpu_custom_call" | custom-call | flops 1358954496 | bytes 5400704 | tf_op jit(solution)/shard_map/pallas_call | solution.py:117
  93.7 13.9 %all_to_all.46.refs_2_.refs_11_.refs_7_ = f32[16,2,512]{2,1,0:T(2,128)} all-to-all(f32[16,2,512]{2,1,0:T(2,128)} %copy-done.29), channel_id=1, replica_groups=mesh['dp'=16,'shard'=2] {'dp'}, dimensions={0} | all-to-all | bytes 131072 | tf_op jit(solution)/shard_map/all_to_all | solution.py:213
  112.8 4.9 %shard_map.234 = (bf16[288,512]{1,0:T(8,128)(2,1)}, f32[288,2048]{1,0:T(8,128)S(1)}, f32[16,2,2048]{2,1,0:T(2,128)}, bf16[512,2304]{1,0:T(8,128)(2,1)}, bf16[512,256]{1,0:T(8,128)(2,1)}) custom-call(f32[288,512]{1,0:T(8,128)S(1)} %get-tuple-element.107.refs_0_.refs_6_.refs_2_, f32[4,512]{1,0:T(4,128)S(1)} %copy-done.30, f32[16,2,512]{2,1,0:T(2,128)S(1)} %copy-done.17, ...), custom_call_target="tpu_custom_call" | custom-call | flops 603979776 | bytes 3022976 | tf_op jit(solution)/shard_map/pallas_call | solution.py:117
  118.1 4.5 %all-to-all-start.2 = ((f32[16,2,2048]{2,1,0:T(2,128)}), f32[16,2,2048]{2,1,0:T(2,128)}, u32[]{:S(2)}, u32[]{:S(2)}) async-start(f32[16,2,2048]{2,1,0:T(2,128)} %get-tuple-element.111), calls=%async_computation.2 | async-start | bytes 524288 | tf_op jit(solution)/shard_map/all_to_all | solution.py:213
  122.7 8.9 %all-to-all-done.2.refs_5_.refs_9_ = f32[16,2,2048]{2,1,0:T(2,128)} async-done(((f32[16,2,2048]{2,1,0:T(2,128)}), f32[16,2,2048]{2,1,0:T(2,128)}, u32[]{:S(2)}, u32[]{:S(2)}) %all-to-all-start.2) | async-done | bytes 262176 | tf_op jit(solution)/shard_map/all_to_all | solution.py:213
  131.6 6.3 %shard_map.236 = (bf16[32,2048]{1,0:T(8,128)(2,1)}, f32[32,2048]{1,0:T(8,128)}, f32[16,2,2048]{2,1,0:T(2,128)}, bf16[2048,128]{1,0:T(8,128)(2,1)}) custom-call(f32[288,2048]{1,0:T(8,128)S(1)} %get-tuple-element.110.refs_0_.refs_2_.refs_3_, bf16[288,2048]{1,0:T(8,128)(2,1)S(1)} %bitcast.50, f32[4,2048]{1,0:T(4,128)} %refs_4_.3, ...), custom_call_target="tpu_custom_call" | custom-call | flops 268435456 | bytes 12765440 | tf_op jit(solution)/shard_map/pallas_call | solution.py:117
  137.9 11.8 %all_to_all.47.refs_5_.refs_6_.refs_7_ = f32[16,2,2048]{2,1,0:T(2,128)S(1)} all-to-all(f32[16,2,2048]{2,1,0:T(2,128)} %get-tuple-element.116), channel_id=1, replica_groups=mesh['dp'=16,'shard'=2] {'dp'}, dimensions={0} | all-to-all | bytes 524288 | tf_op jit(solution)/shard_map/all_to_all | solution.py:213
  152.8 5.2 %all-to-all-start.4 = ((bf16[16,64,128]{2,1,0:T(8,128)(2,1)}), bf16[16,64,128]{2,1,0:T(8,128)(2,1)S(1)}, u32[]{:S(2)}, u32[]{:S(2)}) async-start(bf16[16,64,128]{2,1,0:T(8,128)(2,1)} %get-tuple-element.117), calls=%async_computation.4 | async-start | bytes 524288 | tf_op jit(solution)/shard_map/all_to_all | solution.py:1278
  159.9 5.5 %all-to-all-done.4.refs_1_ = bf16[16,64,128]{2,1,0:T(8,128)(2,1)S(1)} async-done(((bf16[16,64,128]{2,1,0:T(8,128)(2,1)}), bf16[16,64,128]{2,1,0:T(8,128)(2,1)S(1)}, u32[]{:S(2)}, u32[]{:S(2)}) %all-to-all-start.4) | async-done | bytes 262176 | tf_op jit(solution)/shard_map/all_to_all | solution.py:1278
  165.4 17.9 %shard_map.238 = (f32[8,128]{1,0:T(8,128)S(1)}, f32[128,3072]{1,0:T(8,128)}, f32[32,128]{1,0:T(8,128)S(1)}) custom-call(s32[2]{0:T(128)S(1)} %pad_add_fusion.1.refs_0_, bf16[16,64,128]{2,1,0:T(8,128)(2,1)S(1)} %all-to-all-done.4.refs_1_, bf16[512,256]{1,0:T(8,128)(2,1)} %get-tuple-element.118.refs_2_, bf16[3000,128]{1,0:T(8,128)(2,1)} %refs_3_.3), custom_call_target="tpu_custom_call" | custom-call | flops 3221225472 | bytes 1292296 | tf_op jit(solution)/shard_map/pallas_call | solution.py:117
  186.3 11.9 %all_to_all.48.refs_8_ = bf16[16,2,2048]{2,1,0:T(2,128)(2,1)S(1)} all-to-all(bf16[16,2,2048]{2,1,0:T(2,128)(2,1)} %get-tuple-element.123), channel_id=1, replica_groups=mesh['dp'=16,'shard'=2] {'dp'}, dimensions={0} | all-to-all | bytes 262144 | tf_op jit(solution)/shard_map/all_to_all | solution.py:213
  198.3 9.9 %shard_map.240 = (bf16[32,2048]{1,0:T(8,128)(2,1)}, f32[144,2048]{1,0:T(8,128)S(1)}, f32[144,2048]{1,0:T(8,128)}, bf16[16,2,2048]{2,1,0:T(2,128)(2,1)}, f32[2,2048]{1,0:T(2,128)}) custom-call(f32[32,2048]{1,0:T(8,128)} %get-tuple-element.122.refs_0_, f32[32,2048]{1,0:T(8,128)} %get-tuple-element.113.refs_0_.refs_4_.refs_1_, f32[288,2048]{1,0:T(8,128)} %copy-done.3, ...), custom_call_target="tpu_custom_call" | custom-call | flops 268435456 | bytes 13682944 | tf_op jit(solution)/shard_map/pallas_call | solution.py:117
  208.2 10.3 %all_to_all.49.refs_10_ = bf16[16,2,2048]{2,1,0:T(2,128)(2,1)S(1)} all-to-all(bf16[16,2,2048]{2,1,0:T(2,128)(2,1)} %get-tuple-element.126), channel_id=1, replica_groups=mesh['dp'=16,'shard'=2] {'dp'}, dimensions={0} | all-to-all | bytes 262144 | tf_op jit(solution)/shard_map/all_to_all | solution.py:213
  218.5 6.1 %shard_map.241 = (bf16[288,1024]{1,0:T(8,128)(2,1)}, bf16[288,1024]{1,0:T(8,128)(2,1)}, f32[288,512]{1,0:T(8,128)S(1)}, bf16[16,2,640]{2,1,0:T(2,128)(2,1)}, f32[2,2048]{1,0:T(2,128)}) custom-call(s32[1]{0:T(128)} %bitcast.refs_0_.refs_9_, f32[144,2048]{1,0:T(8,128)S(1)} %get-tuple-element.124.refs_1_, f32[144,2048]{1,0:T(8,128)} %get-tuple-element.127.refs_2_, ...), custom_call_target="tpu_custom_call" | custom-call | flops 603979776 | bytes 8167940 | tf_op jit(solution)/shard_map/pallas_call | solution.py:117
  232.9 4.5 %shard_map.242 = (f32[8,32,1280]{2,1,0:T(8,128)}, bf16[8,32,1280]{2,1,0:T(8,128)(2,1)}) custom-call(s32[16]{0:T(128)S(1)} %fusion.20.refs_0_, bf16[288,512]{1,0:T(8,128)(2,1)} %get-tuple-element.133.refs_1_, bf16[288,512]{1,0:T(8,128)(2,1)} %collective-permute-done.21.refs_2_, bf16[288,1024]{1,0:T(8,128)(2,1)} %get-tuple-element.134.refs_3_, ...), custom_call_target="tpu_custom_call" | custom-call | flops 603979776 | bytes 2048068 | tf_op jit(solution)/shard_map/pallas_call | solution.py:117
  239.2 5.1 %shard_map.243 = (bf16[288,256]{1,0:T(8,128)(2,1)}, bf16[288,256]{1,0:T(8,128)(2,1)}, f32[288,512]{1,0:T(8,128)S(1)}, bf16[16,2,512]{2,1,0:T(2,128)(2,1)S(1)}, f32[2,640]{1,0:T(2,128)S(1)}) custom-call(s32[1]{0:T(128)} %bitcast.refs_0_.refs_9_, f32[288,512]{1,0:T(8,128)S(1)} %get-tuple-element.130.refs_1_, f32[288,512]{1,0:T(8,128)} %copy-done.5, ...), custom_call_target="tpu_custom_call" | custom-call | flops 1358954496 | bytes 6686724 | tf_op jit(solution)/shard_map/pallas_call | solution.py:117
  247.0 6.9 %shard_map.244 = (f32[8,288,256]{2,1,0:T(8,128)}, bf16[8,288,256]{2,1,0:T(8,128)(2,1)}) custom-call(s32[16]{0:T(128)S(1)} %fusion.20.refs_0_, bf16[288,4608]{1,0:T(8,128)(2,1)S(1)} %copy-done.10, bf16[288,4608]{1,0:T(8,128)(2,1)} %collective-permute-done.25.refs_2_, bf16[288,256]{1,0:T(8,128)(2,1)} %get-tuple-element.142.refs_3_, ...), custom_call_target="tpu_custom_call" | custom-call | flops 1358954496 | bytes 5603392 | tf_op jit(solution)/shard_map/pallas_call | solution.py:117
  255.2 18.8 %all_to_all.50.refs_5_ = bf16[16,2,512]{2,1,0:T(2,128)(2,1)S(1)} all-to-all(bf16[16,2,512]{2,1,0:T(2,128)(2,1)S(1)} %get-tuple-element.145), channel_id=1, replica_groups=mesh['dp'=16,'shard'=2] {'dp'}, dimensions={0} | all-to-all | bytes 65536 | tf_op jit(solution)/shard_map/all_to_all | solution.py:213
  287.4 4.6 %collective-permute-start.28 = (bf16[288,256]{1,0:T(8,128)(2,1)S(1)}, bf16[288,256]{1,0:T(8,128)(2,1)S(1)}, u32[]{:S(2)}, u32[]{:S(2)}) collective-permute-start(bf16[288,256]{1,0:T(8,128)(2,1)S(1)} %copy-done.48), channel_id=1, source_target_pairs={{0,1},{1,0},{2,3},{3,2},{4,5},{5,4},{6,7},{7,6},{8,9},{9,8},{10,11... | collective-permute-start | bytes 442376 | tf_op jit(solution)/shard_map/ppermute | solution.py:195
  (286 shorter events, 136.2 us)
Async XLA Ops:
  7.2 110.5 %all-gather.6.cloned.1.call-start = ((), (), s32[]{:S(2)}) async-start(), calls=%async_computation.10 | async-start | bytes 4734976 | tf_op jit(solution)/shard_map/all_gather | solution.py:1155
  7.2 10.4 %collective-permute-start.1 = (bf16[1,64,512]{2,1,0:T(8,128)(2,1)}, bf16[1,64,512]{2,1,0:T(8,128)(2,1)S(1)}, u32[]{:S(2)}, u32[]{:S(2)}) collective-permute-start(bf16[1,64,512]{2,1,0:T(8,128)(2,1)} %bitcast.65), channel_id=1, source_target_pairs={{0,16},{2,18},{4,20},{6,22},{8,24},{10,26},{12,28},{14,30},{16,0},... | collective-permute-start | bytes 196616 | tf_op jit(solution)/shard_map/ppermute | solution.py:199
  24.9 13.7 %collective-permute-start.6 = (bf16[8,64,512]{2,1,0:T(8,128)(2,1)}, bf16[8,64,512]{2,1,0:T(8,128)(2,1)S(1)}, u32[]{:S(2)}, u32[]{:S(2)}) collective-permute-start(bf16[8,64,512]{2,1,0:T(8,128)(2,1)} %copy-done.8), channel_id=1, source_target_pairs={{0,2},{1,5},{2,0},{3,7},{4,6},{5,1},{6,4},{7,3},{8,10},{9,13},{10,... | collective-permute-start | bytes 1572872 | tf_op jit(solution)/shard_map/ppermute | solution.py:204
  39.8 13.1 %collective-permute-start.10 = (bf16[16,64,512]{2,1,0:T(8,128)(2,1)S(1)}, bf16[16,64,512]{2,1,0:T(8,128)(2,1)}, u32[]{:S(2)}, u32[]{:S(2)}) collective-permute-start(bf16[16,64,512]{2,1,0:T(8,128)(2,1)S(1)} %get-tuple-element.102.refs_2_), channel_id=1, source_target_pairs={{0,1},{1,0},{2,3},{3,2},{4,5},{5,4},{6,7},{7,6},{8,9},{9,8},{10,11... | collective-permute-start | bytes 3145736 | tf_op jit(solution)/shard_map/ppermute | solution.py:195
  43.4 15.0 %collective-permute-start.11 = (bf16[4,144,512]{2,1,0:T(8,128)(2,1)S(1)}, bf16[4,144,512]{2,1,0:T(8,128)(2,1)S(1)}, u32[]{:S(2)}, u32[]{:S(2)}) collective-permute-start(bf16[4,144,512]{2,1,0:T(8,128)(2,1)S(1)} %get-tuple-element.105.refs_1_.refs_0_), channel_id=1, source_target_pairs={{0,4},{1,3},{2,6},{3,1},{4,0},{5,7},{6,2},{7,5},{8,12},{9,11},{10,... | collective-permute-start | bytes 1769480 | tf_op jit(solution)/shard_map/ppermute | solution.py:204
  43.9 13.4 %collective-permute-start.12 = (bf16[1,16,2304]{2,1,0:T(8,128)(2,1)S(1)}, bf16[1,16,2304]{2,1,0:T(8,128)(2,1)S(1)}, u32[]{:S(2)}, u32[]{:S(2)}) collective-permute-start(bf16[1,16,2304]{2,1,0:T(8,128)(2,1)S(1)} %bitcast.61), channel_id=1, source_target_pairs={{0,16},{2,18},{4,20},{6,22},{8,24},{10,26},{12,28},{14,30},{16,0},... | collective-permute-start | bytes 221192 | tf_op jit(solution)/shard_map/ppermute | solution.py:199
  58.6 16.2 %collective-permute-start.15 = (bf16[8,144,512]{2,1,0:T(8,128)(2,1)S(1)}, bf16[8,144,512]{2,1,0:T(8,128)(2,1)S(1)}, u32[]{:S(2)}, u32[]{:S(2)}) collective-permute-start(bf16[8,144,512]{2,1,0:T(8,128)(2,1)S(1)} %get-tuple-element.106.refs_0_), channel_id=1, source_target_pairs={{0,2},{1,5},{2,0},{3,7},{4,6},{5,1},{6,4},{7,3},{8,10},{9,13},{10,... | collective-permute-start | bytes 3538952 | tf_op jit(solution)/shard_map/ppermute | solution.py:204
  80.5 12.9 %collective-permute-start.17 = (bf16[4,16,2304]{2,1,0:T(8,128)(2,1)S(1)}, bf16[4,16,2304]{2,1,0:T(8,128)(2,1)S(1)}, u32[]{:S(2)}, u32[]{:S(2)}) collective-permute-start(bf16[4,16,2304]{2,1,0:T(8,128)(2,1)S(1)} %get-tuple-element.109.refs_0_), channel_id=1, source_target_pairs={{0,4},{1,3},{2,6},{3,1},{4,0},{5,7},{6,2},{7,5},{8,12},{9,11},{10,... | collective-permute-start | bytes 884744 | tf_op jit(solution)/shard_map/ppermute | solution.py:204
  93.4 14.3 %collective-permute-start.18 = (bf16[8,16,2304]{2,1,0:T(8,128)(2,1)S(1)}, bf16[8,16,2304]{2,1,0:T(8,128)(2,1)S(1)}, u32[]{:S(2)}, u32[]{:S(2)}) collective-permute-start(bf16[8,16,2304]{2,1,0:T(8,128)(2,1)S(1)} %shard_map.232.refs_0_), channel_id=1, source_target_pairs={{0,2},{1,5},{2,0},{3,7},{4,6},{5,1},{6,4},{7,3},{8,10},{9,13},{10,... | collective-permute-start | bytes 1769480 | tf_op jit(solution)/shard_map/ppermute | solution.py:204
  117.7 13.9 %collective-permute-start.20 = (bf16[16,64,2176]{2,1,0:T(8,128)(2,1)}, bf16[16,64,2176]{2,1,0:T(8,128)(2,1)}, u32[]{:S(2)}, u32[]{:S(2)}) collective-permute-start(bf16[16,64,2176]{2,1,0:T(8,128)(2,1)} %bitcast.69), channel_id=1, source_target_pairs={{0,1},{1,0},{2,3},{3,2},{4,5},{5,4},{6,7},{7,6},{8,9},{9,8},{10,11... | collective-permute-start | bytes 13369352 | tf_op jit(solution)/shard_map/ppermute | solution.py:195
  118.1 13.4 %all-to-all-start.2 = ((f32[16,2,2048]{2,1,0:T(2,128)}), f32[16,2,2048]{2,1,0:T(2,128)}, u32[]{:S(2)}, u32[]{:S(2)}) async-start(f32[16,2,2048]{2,1,0:T(2,128)} %get-tuple-element.111), calls=%async_computation.2 | async-start | bytes 524288 | tf_op jit(solution)/shard_map/all_to_all | solution.py:213
  152.8 12.7 %all-to-all-start.4 = ((bf16[16,64,128]{2,1,0:T(8,128)(2,1)}), bf16[16,64,128]{2,1,0:T(8,128)(2,1)S(1)}, u32[]{:S(2)}, u32[]{:S(2)}) async-start(bf16[16,64,128]{2,1,0:T(8,128)(2,1)} %get-tuple-element.117), calls=%async_computation.4 | async-start | bytes 524288 | tf_op jit(solution)/shard_map/all_to_all | solution.py:1278
  158.0 135.0 %all-gather.4.cloned.1.call-start = ((), (), s32[]{:S(2)}) async-start(), calls=%async_computation.9 | async-start | bytes 2228224 | tf_op jit(solution)/shard_map/all_gather | solution.py:1355
  158.3 87.5 %collective-permute-start.25 = (bf16[288,4608]{1,0:T(8,128)(2,1)}, bf16[288,4608]{1,0:T(8,128)(2,1)}, u32[]{:S(2)}, u32[]{:S(2)}) collective-permute-start(bf16[288,4608]{1,0:T(8,128)(2,1)} %get-tuple-element.141.refs_1_), channel_id=1, source_target_pairs={{0,1},{1,0},{2,3},{3,2},{4,5},{5,4},{6,7},{7,6},{8,9},{9,8},{10,11... | collective-permute-start | bytes 7962632 | tf_op jit(solution)/shard_map/ppermute | solution.py:195
  229.2 10.1 %all-to-all-start.7 = ((bf16[16,2,640]{2,1,0:T(2,128)(2,1)}), bf16[16,2,640]{2,1,0:T(2,128)(2,1)S(1)}, u32[]{:S(2)}, u32[]{:S(2)}) async-start(bf16[16,2,640]{2,1,0:T(2,128)(2,1)} %get-tuple-element.132.refs_10_), calls=%async_computation.7 | async-start | bytes 81920 | tf_op jit(solution)/shard_map/all_to_all | solution.py:213
  253.9 22.2 %collective-permute-start.30 = (bf16[8,288,256]{2,1,0:T(8,128)(2,1)}, bf16[8,288,256]{2,1,0:T(8,128)(2,1)S(1)}, u32[]{:S(2)}, u32[]{:S(2)}) collective-permute-start(bf16[8,288,256]{2,1,0:T(8,128)(2,1)} %get-tuple-element.155), channel_id=1, source_target_pairs={{0,2},{1,5},{2,0},{3,7},{4,6},{5,1},{6,4},{7,3},{8,10},{9,13},{10,... | collective-permute-start | bytes 3538952 | tf_op jit(solution)/shard_map/ppermute | solution.py:204
  254.3 37.7 %collective-permute-start.27 = (bf16[288,2048]{1,0:T(8,128)(2,1)S(1)}, bf16[288,2048]{1,0:T(8,128)(2,1)S(1)}, u32[]{:S(2)}, u32[]{:S(2)}) collective-permute-start(bf16[288,2048]{1,0:T(8,128)(2,1)S(1)} %bitcast.51), channel_id=1, source_target_pairs={{0,1},{1,0},{2,3},{3,2},{4,5},{5,4},{6,7},{7,6},{8,9},{9,8},{10,11... | collective-permute-start | bytes 3538952 | tf_op jit(solution)/shard_map/ppermute | solution.py:195
  279.2 27.0 %collective-permute-start.32 = (bf16[4,288,256]{2,1,0:T(8,128)(2,1)}, bf16[4,288,256]{2,1,0:T(8,128)(2,1)S(1)}, u32[]{:S(2)}, u32[]{:S(2)}) collective-permute-start(bf16[4,288,256]{2,1,0:T(8,128)(2,1)} %get-tuple-element.163), channel_id=1, source_target_pairs={{0,4},{1,3},{2,6},{3,1},{4,0},{5,7},{6,2},{7,5},{8,12},{9,11},{10,... | collective-permute-start | bytes 1769480 | tf_op jit(solution)/shard_map/ppermute | solution.py:204
  286.2 11.9 %collective-permute-start.33 = (bf16[4,32,1280]{2,1,0:T(8,128)(2,1)}, bf16[4,32,1280]{2,1,0:T(8,128)(2,1)}, u32[]{:S(2)}, u32[]{:S(2)}) collective-permute-start(bf16[4,32,1280]{2,1,0:T(8,128)(2,1)} %get-tuple-element.164), channel_id=1, source_target_pairs={{0,4},{1,3},{2,6},{3,1},{4,0},{5,7},{6,2},{7,5},{8,12},{9,11},{10,... | collective-permute-start | bytes 983048 | tf_op jit(solution)/shard_map/ppermute | solution.py:204
  304.0 20.7 %collective-permute-start.35 = (f32[144,2048]{1,0:T(8,128)}, f32[144,2048]{1,0:T(8,128)S(1)}, u32[]{:S(2)}, u32[]{:S(2)}) collective-permute-start(f32[144,2048]{1,0:T(8,128)} %get-tuple-element.127.refs_2_), channel_id=1, source_target_pairs={{0,1},{1,0},{2,3},{3,2},{4,5},{5,4},{6,7},{7,6},{8,9},{9,8},{10,11... | collective-permute-start | bytes 3538952 | tf_op jit(solution)/shard_map/ppermute | solution.py:195
  313.5 11.1 %collective-permute-start.38 = (bf16[1,288,256]{2,1,0:T(8,128)(2,1)}, bf16[1,288,256]{2,1,0:T(8,128)(2,1)S(1)}, u32[]{:S(2)}, u32[]{:S(2)}) collective-permute-start(bf16[1,288,256]{2,1,0:T(8,128)(2,1)} %get-tuple-element.177), channel_id=1, source_target_pairs={{0,16},{2,18},{4,20},{6,22},{8,24},{10,26},{12,28},{14,30},{16,0},... | collective-permute-start | bytes 442376 | tf_op jit(solution)/shard_map/ppermute | solution.py:199
  314.9 20.7 %collective-permute-start.50 = (f32[128,3072]{1,0:T(8,128)S(1)}, f32[128,3072]{1,0:T(8,128)S(1)}, u32[]{:S(2)}, u32[]{:S(2)}) collective-permute-start(f32[128,3072]{1,0:T(8,128)S(1)} %copy-done.35), channel_id=1, source_target_pairs={{0,1},{1,0},{2,3},{3,2},{4,5},{5,4},{6,7},{7,6},{8,9},{9,8},{10,11... | collective-permute-start | bytes 4718600 | tf_op jit(solution)/shard_map/ppermute | solution.py:195
  330.6 10.4 %collective-permute-start.37 = (f32[10496]{0:T(1024)S(1)}, f32[10496]{0:T(1024)S(1)}, u32[]{:S(2)}, u32[]{:S(2)}) collective-permute-start(f32[10496]{0:T(1024)S(1)} %pad_maximum_fusion.6), channel_id=1, source_target_pairs={{0,1},{1,0},{2,3},{3,2},{4,5},{5,4},{6,7},{7,6},{8,9},{9,8},{10,11... | collective-permute-start | bytes 125960 | tf_op jit(solution)/shard_map/ppermute | solution.py:195
  335.6 9.8 %collective-permute-start.49 = (f32[64,2048]{1,0:T(8,128)S(1)}, f32[64,2048]{1,0:T(8,128)S(1)}, u32[]{:S(2)}, u32[]{:S(2)}) collective-permute-start(f32[64,2048]{1,0:T(8,128)S(1)} %constant_dynamic-slice_fusion), channel_id=1, source_target_pairs={{0,1},{1,0},{2,3},{3,2},{4,5},{5,4},{6,7},{7,6},{8,9},{9,8},{10,11... | collective-permute-start | bytes 1572872 | tf_op jit(solution)/shard_map/ppermute | solution.py:195
  (82 other events, 777.1 us)
Sparse Core Ops, SparseCore 0:
  25.0 87.4 all-gather.5
  208.3 62.0 all-gather.3
